TPU v7x, 32 devices: a whole 2x2x4 slice. The times are simulated.
32 devices in a mesh: grp: 4 (over y, core), dev: 8 (over z, x).
Axes of the slice: x: 2, y: 2, z: 4, core: 2. Of those that a mesh axis runs over, the one named last changes fastest.
Arguments:
- item_factors: bfloat16 [8192, 256], P(('grp', 'dev'))
- send_list: int32 [32, 4, 1], P(('grp', 'dev')), may hold values from 0 to 1
- route_list: int32 [32, 8, 1], P(('grp', 'dev')), may hold values from 0 to 3
- tile_slot: int32 [32, 64], P(('grp', 'dev')), may hold values from 0 to 7
- confidence: bfloat16 [2048, 128, 128], P(('grp', 'dev')), may hold values from 0 to 160, as said below
Outputs:
- user_factors: float32 [16384, 256], P(('grp', 'dev'))
Inputs may be any that keep to these rules, and one draw needn't show every extreme that they name: `confidence`: every user row of every tile has at least one observed item.
All inputs are finite; a program needn't handle non-finite values.
Results may differ from a plain program's by a relative error of at most 0.0055.
Values may be sent and summed in bfloat16 or wider, within the bound.
No kernel may reach another device: no remote copies, remote signals or barrier semaphores. Data moves between devices by JAX's collectives and lax.ppermute only.
A program may use at most 128 MiB of HBM per device.

v0:
```python
import jax
import jax.numpy as jnp
from jax import lax
from jax.sharding import PartitionSpec as P

RANK = 256
BLOCK = 128
PANELS_DEV = 2
USER_BLOCKS = 4
TILES_PER = 16
ITERS = 8


ridge = 0.1


def apply_operator(direction, gram, tile_panels, weights):
    dir_bf = direction.astype(jnp.bfloat16).reshape(USER_BLOCKS, BLOCK, RANK)
    scores = jnp.einsum("ubr,utir->utbi", dir_bf, tile_panels, preferred_element_type=jnp.float32)
    weighted = (weights.astype(jnp.float32) * scores).astype(jnp.bfloat16)
    back = jnp.einsum("utbi,utir->ubr", weighted, tile_panels, preferred_element_type=jnp.float32)
    back = back.reshape(USER_BLOCKS * BLOCK, RANK)
    return jnp.dot(direction, gram, precision=lax.Precision.HIGHEST) + ridge * direction + back


def solve_users(gram, tile_panels, weights):
    observed = (weights > 0).astype(jnp.float32)
    target = ((1.0 + weights.astype(jnp.float32)) * observed).astype(jnp.bfloat16)
    right_side = jnp.einsum(
        "utbi,utir->ubr", target, tile_panels, preferred_element_type=jnp.float32
    )
    right_side = right_side.reshape(USER_BLOCKS * BLOCK, RANK)
    solution = jnp.zeros_like(right_side)
    residual = right_side
    direction = right_side
    norm_now = jnp.sum(residual * residual, axis=1, keepdims=True)
    for step in range(ITERS):
        image = apply_operator(direction, gram, tile_panels, weights)
        alpha = norm_now / jnp.sum(direction * image, axis=1, keepdims=True)
        solution = solution + alpha * direction
        residual = residual - alpha * image
        norm_next = jnp.sum(residual * residual, axis=1, keepdims=True)
        direction = residual + norm_next / norm_now * direction
        norm_now = norm_next
    return solution


def shards(item_factors, send_list, route_list, tile_slot, confidence):
    partial_gram = lax.dot_general(
        item_factors, item_factors, (((0,), (0,)), ((), ())), preferred_element_type=jnp.float32
    )
    gram = lax.psum(partial_gram, ("grp", "dev"))
    own_panels = item_factors.reshape(PANELS_DEV, BLOCK, RANK)
    outgoing = own_panels[send_list[0]]
    arrived = lax.all_to_all(outgoing, "grp", split_axis=0, concat_axis=0, tiled=True)
    group_pool = arrived.reshape(-1, BLOCK, RANK)
    pool_size = group_pool.shape[0]
    everyone = lax.all_gather(group_pool, "dev", axis=0, tiled=True)
    all_routes = lax.all_gather(route_list, "dev", axis=0, tiled=True)
    member = lax.axis_index("dev")
    mine = lax.dynamic_index_in_dim(all_routes, member, 1, keepdims=False)
    sources = jnp.arange(lax.axis_size("dev"), dtype=jnp.int32)[:, None] * pool_size
    panels = everyone[(sources + mine).reshape(-1)]
    tile_panels = panels[tile_slot[0]].reshape(USER_BLOCKS, TILES_PER, BLOCK, RANK)
    weights = confidence.reshape(USER_BLOCKS, TILES_PER, BLOCK, BLOCK)
    return solve_users(gram, tile_panels, weights)


def solution(mesh):
    placed = (
        P(("grp", "dev"), None),
        P(("grp", "dev"), None, None),
        P(("grp", "dev"), None, None),
        P(("grp", "dev"), None),
        P(("grp", "dev"), None, None),
    )
    return jax.shard_map(
        shards, mesh=mesh, in_specs=placed, out_specs=P(("grp", "dev"), None), check_vma=False
    )
```

profile of v0, /device:TPU:1, one launch (start us, length us, event | category | flops | bytes accessed | tf_op | source)
XLA Modules:
  0.0 239.5 jit_solution(17851956002359873050)
XLA Ops:
  7.4 0.0 copy-start
  7.4 0.0 all-gather.3.cloned.1.call-start
  7.4 0.8 fusion.33
  8.2 0.1 copy-done
  8.3 0.6 gather_fusion
  8.8 9.2 %all_to_all.5 = bf16[4,1,128,256]{3,2,1,0:T(8,128)(2,1)} all-to-all(bf16[4,1,128,256]{3,2,1,0:T(8,128)(2,1)S(1)} %bitcast.241), channel_id=1, replica_groups=mesh['grp'=4,'dev'=8] {'grp'}, dimensions={0} | all-to-all | bytes 524288 | tf_op jit(solution)/shard_map/all_to_all | solution.py:55
  18.0 0.0 all-gather.3.cloned.1.call-update
  18.1 0.0 all-reduce.2.cloned.1.call-start
  18.1 0.9 fusion.45
  19.0 0.0 all-reduce.2.cloned.1.call-update
  19.1 0.0 copy-start.13
  19.1 0.0 copy-start.12
  19.1 2.1 broadcast_compare_fusion
  21.2 0.0 copy-done.2
  21.3 3.4 %copy.9 = f32[64,128,128]{1,2,0:T(8,128)} copy(bf16[64,128,128]{2,1,0:T(8,128)(2,1)S(1)} %copy-done.2) | data formatting | bytes 6291456 | tf_op jit(solution)/shard_map/convert_element_type | solution.py:28
  24.6 0.0 copy-done.13
  24.6 0.0 copy-done.12
  24.7 17.4 %all_gather.7 = s32[8,8,1]{1,2,0:T(1,128)S(1)} all-gather(s32[1,8,1]{1,2,0:T(1,128)S(1)} %copy-done.12), channel_id=1, replica_groups=mesh['grp'=4,'dev'=8] {'dev'}, dimensions={0}, use_global_device_ids=true | all-gather | bytes 288 | tf_op jit(solution)/shard_map/all_gather | solution.py:59
  42.1 0.3 dynamic-slice_reduce_fusion
  42.4 1.2 copy.8
  43.6 24.1 %all-gather.3.cloned.1.call-done = bf16[32,1,128,256]{3,2,1,0:T(8,128)(2,1)} async-done(((bf16[4,1,128,256]{3,2,1,0:T(8,128)(2,1)}), bf16[32,1,128,256]{3,2,1,0:T(8,128)(2,1)}) %all-gather.3.cloned.1.call-update) | async-done | bytes 2097168 | tf_op jit(solution)/shard_map/all_gather | solution.py:58
  67.6 2.2 gather_fusion.1
  69.8 2.8 %gather_fusion.2 = bf16[64,128,256]{2,1,0:T(8,128)(2,1)} fusion(bf16[8,128,256]{2,1,0:T(8,128)(2,1)S(1)} %gather_fusion.1, s32[1024]{0:T(1024)S(1)} %pad_clamp_fusion), kind=kCustom, calls=%fused_computation.2 | custom fusion | bytes 8388864 | tf_op jit(solution)/shard_map/gather | solution.py:64
  72.6 4.6 %fusion.29 = (f32[4,128]{1,0:T(4,128)S(1)}, f32[4,128,256,1]{2,1,3,0:T(8,128)S(1)}) fusion(bf16[4,16,128,256]{3,2,1,0:T(8,128)(2,1)} %bitcast.211, pred[4,16,128,128]{2,3,1,0:T(32,128)(4,1)S(1)} %bitcast.230, f32[4,16,128,128]{2,3,1,0:T(8,128)} %bitcast.220), kind=kOutput, calls=%fused_computation.52 | convolution fusion | flops 540278272 | bytes 9963520 | tf_op jit(solution)/shard_map/utbi,utir->ubr/dot_general | solution.py:29
  77.2 6.5 %fusion.11 = f32[4,128,256,1]{2,1,3,0:T(8,128)S(1)} fusion(bf16[4,16,128,256]{3,2,1,0:T(8,128)(2,1)} %bitcast.212, f32[4,16,128,128]{2,3,1,0:T(8,128)} %bitcast.221, f32[4,128,256,1]{2,1,3,0:T(8,128)S(1)} %get-tuple-element.32), kind=kOutput, calls=%fused_computation.23 | convolution fusion | flops 1075970048 | bytes 9437184 | tf_op jit(solution)/shard_map/utbi,utir->ubr/dot_general | solution.py:21
  83.7 72.5 %all-reduce.2.cloned.1.call-done = f32[256,256]{1,0:T(8,128)} async-done(((f32[256,256]{1,0:T(8,128)}), f32[256,256]{1,0:T(8,128)}) %all-reduce.2.cloned.1.call-update) | async-done | bytes 262160 | tf_op jit(solution)/shard_map/psum | solution.py:52
  156.2 1.6 multiply_reduce_fusion.13
  157.9 0.2 multiply_reduce_fusion.12
  158.1 0.2 fusion.44
  158.3 0.0 copy-start.1
  158.3 6.5 %fusion.12 = f32[4,128,256,1]{2,1,3,0:T(8,128)S(1)} fusion(bf16[4,16,128,256]{3,2,1,0:T(8,128)(2,1)} %bitcast.213, f32[4,16,128,128]{2,3,1,0:T(8,128)} %bitcast.222, bf16[4,128,256,1]{2,1,3,0:T(8,128)(2,1)S(1)} %bitcast.240), kind=kOutput, calls=%fused_computation.24 | convolution fusion | flops 1075838976 | bytes 9175040 | tf_op jit(solution)/shard_map/utbi,utir->ubr/dot_general | solution.py:21
  164.9 0.0 copy-done.1
  164.9 0.7 multiply_reduce_fusion.11
  165.5 0.3 multiply_reduce_fusion.10
  165.9 0.1 fusion.43
  166.0 6.5 %fusion.13 = f32[4,128,256,1]{2,1,3,0:T(8,128)S(1)} fusion(bf16[4,16,128,256]{3,2,1,0:T(8,128)(2,1)} %bitcast.214, f32[4,16,128,128]{2,3,1,0:T(8,128)} %bitcast.223, bf16[4,128,256,1]{2,1,3,0:T(8,128)(2,1)S(1)} %bitcast.242), kind=kOutput, calls=%fused_computation.25 | convolution fusion | flops 1075838976 | bytes 9175040 | tf_op jit(solution)/shard_map/utbi,utir->ubr/dot_general | solution.py:21
  172.5 0.7 multiply_reduce_fusion.9
  173.2 0.2 multiply_reduce_fusion.8
  173.4 0.8 fusion.42
  174.3 6.7 %fusion.14 = f32[4,128,256,1]{2,1,3,0:T(8,128)S(1)} fusion(bf16[4,16,128,256]{3,2,1,0:T(8,128)(2,1)} %bitcast.215, f32[4,16,128,128]{2,3,1,0:T(8,128)} %bitcast.224, bf16[4,128,256,1]{2,1,3,0:T(8,128)(2,1)} %bitcast.243), kind=kOutput, calls=%fused_computation.26 | convolution fusion | flops 1075838976 | bytes 9175040 | tf_op jit(solution)/shard_map/utbi,utir->ubr/dot_general | solution.py:21
  181.1 0.7 multiply_reduce_fusion.7
  181.8 0.2 multiply_reduce_fusion.6
  182.0 0.3 copy-done.8
  182.3 0.8 fusion.41
  183.2 7.3 %fusion.15 = f32[4,128,256,1]{2,1,3,0:T(8,128)} fusion(bf16[4,16,128,256]{3,2,1,0:T(8,128)(2,1)} %bitcast.216, f32[4,16,128,128]{2,3,1,0:T(8,128)} %bitcast.225, bf16[4,128,256,1]{2,1,3,0:T(8,128)(2,1)} %bitcast.244), kind=kOutput, calls=%fused_computation.27 | convolution fusion | flops 1075838976 | bytes 9175040 | tf_op jit(solution)/shard_map/utbi,utir->ubr/dot_general | solution.py:21
  190.5 1.7 multiply_reduce_fusion.5
  192.3 0.2 multiply_reduce_fusion.4
  192.5 0.8 copy-done.5
  193.3 0.8 fusion.40
  194.1 7.6 %fusion.16 = f32[4,128,256,1]{2,1,3,0:T(8,128)} fusion(bf16[4,16,128,256]{3,2,1,0:T(8,128)(2,1)} %bitcast.217, f32[4,16,128,128]{2,3,1,0:T(8,128)} %bitcast.226, bf16[4,128,256,1]{2,1,3,0:T(8,128)(2,1)} %bitcast.245), kind=kOutput, calls=%fused_computation.28 | convolution fusion | flops 1075838976 | bytes 9175040 | tf_op jit(solution)/shard_map/utbi,utir->ubr/dot_general | solution.py:21
  201.7 1.7 multiply_reduce_fusion.3
  203.5 1.3 multiply_reduce_fusion.2
  204.8 0.0 copy-done.10
  204.8 2.1 fusion.39
  206.8 7.4 %fusion.17 = f32[4,128,256,1]{2,1,3,0:T(8,128)} fusion(bf16[4,16,128,256]{3,2,1,0:T(8,128)(2,1)} %bitcast.218, f32[4,16,128,128]{2,3,1,0:T(8,128)} %bitcast.227, bf16[4,128,256,1]{2,1,3,0:T(8,128)(2,1)} %bitcast.246), kind=kOutput, calls=%fused_computation.29 | convolution fusion | flops 1075838976 | bytes 9175040 | tf_op jit(solution)/shard_map/utbi,utir->ubr/dot_general | solution.py:21
  214.2 2.0 multiply_reduce_fusion.1
  216.3 0.2 multiply_reduce_fusion
  216.5 0.6 copy-done.11
  217.1 2.2 fusion.38
  219.3 7.4 %fusion.18 = f32[4,128,256,1]{2,1,3,0:T(8,128)} fusion(bf16[4,16,128,256]{3,2,1,0:T(8,128)(2,1)} %bitcast.219, f32[4,16,128,128]{2,3,1,0:T(8,128)} %bitcast.228, bf16[4,128,256,1]{2,1,3,0:T(8,128)(2,1)} %bitcast.239), kind=kOutput, calls=%fused_computation.30 | convolution fusion | flops 1075838976 | bytes 9175040 | tf_op jit(solution)/shard_map/utbi,utir->ubr/dot_general | solution.py:21
  226.7 2.1 fusion.28
  228.8 0.7 div.134
  229.5 0.0 copy-done.4
  229.5 2.6 %multiply_add_fusion = f32[512,256]{1,0:T(8,128)} fusion(f32[512,256]{1,0:T(8,128)} %get-tuple-element.6, f32[512,256]{1,0:T(8,128)} %get-tuple-element.8, f32[512,256]{1,0:T(8,128)S(1)} %copy-done.4, f32[512,256]{1,0:T(8,128)S(1)} %get-tuple-element.16, f32[512,256]{1,0:T(8,128)S(1)} %get-tuple-element.20, f32[512,256]{1,0:T(8,128)S(1)} %get-tuple-element.24, ...), kind=kLoop, calls=%fused_computation.53 | loop fusion | flops 1966080 | bytes 4734976 | tf_op jit(solution)/shard_map/add | solution.py:40
  (33 shorter events, 0.2 us)
Async XLA Ops:
  7.4 0.9 copy-start
  7.4 13.9 %copy-start.2 = (bf16[64,128,128]{2,1,0:T(8,128)(2,1)S(1)}, bf16[64,128,128]{2,1,0:T(8,128)(2,1)}, u32[]{:S(2)}) copy-start(bf16[64,128,128]{2,1,0:T(8,128)(2,1)} %param.9) | copy-start | bytes 6291460
  7.4 60.2 %all-gather.3.cloned.1.call-start = ((), (), s32[]{:S(2)}) async-start(), calls=%async_computation.2 | async-start | bytes 2359296 | tf_op jit(solution)/shard_map/all_gather | solution.py:58
  18.1 138.2 %all-reduce.2.cloned.1.call-start = ((), (), s32[]{:S(2)}) async-start(), calls=%async_computation.1 | async-start | bytes 524288 | tf_op jit(solution)/shard_map/psum | solution.py:52
  19.1 5.6 %copy-start.13 = (s32[1,64]{1,0:T(1,128)S(1)}, s32[1,64]{1,0:T(1,128)}, u32[]{:S(2)}) copy-start(s32[1,64]{1,0:T(1,128)} %param.8) | copy-start | bytes 772
  19.1 5.6 %copy-start.12 = (s32[1,8,1]{1,2,0:T(1,128)S(1)}, s32[1,8,1]{1,2,0:T(1,128)}, u32[]{:S(2)}) copy-start(s32[1,8,1]{1,2,0:T(1,128)} %param.7) | copy-start | bytes 100
  158.3 6.5 %copy-start.1 = (f32[256,256]{1,0:T(8,128)S(1)}, f32[256,256]{1,0:T(8,128)}, u32[]{:S(2)}) copy-start(f32[256,256]{1,0:T(8,128)} %all-reduce.2.cloned.1.call-done) | copy-start | bytes 786436
  173.2 7.9 %copy-start.6 = (f32[512]{0:T(512)}, f32[512]{0:T(512)S(1)}, u32[]{:S(2)}) copy-start(f32[512]{0:T(512)S(1)} %div.124) | copy-start | bytes 6148
  181.7 0.6 copy-start.8
  192.2 1.9 copy-start.9
  192.5 0.8 copy-start.5
  194.1 7.6 %copy-start.3 = (f32[512,256]{1,0:T(8,128)}, f32[512,256]{1,0:T(8,128)S(1)}, u32[]{:S(2)}) copy-start(f32[512,256]{1,0:T(8,128)S(1)} %get-tuple-element.12) | copy-start | bytes 1572868
  203.5 1.3 copy-start.10
  216.5 0.6 copy-start.11
  219.3 10.2 %copy-start.4 = (f32[512,256]{1,0:T(8,128)S(1)}, f32[512,256]{1,0:T(8,128)}, u32[]{:S(2)}) copy-start(f32[512,256]{1,0:T(8,128)} %copy-done.3) | copy-start | bytes 1572868
  219.3 10.2 %copy-start.7 = (f32[512]{0:T(512)S(1)}, f32[512]{0:T(512)}, u32[]{:S(2)}) copy-start(f32[512]{0:T(512)} %copy-done.6) | copy-start | bytes 6148
Sparse Core Ops, SparseCore 0:
  18.2 49.3 all-gather.2
Sparse Core Ops, SparseCore 1:
  24.0 132.1 all-reduce.1
where the time goes:
time: 241 us; the launch traced here: 239 us
  waiting for transfers between devices  96.6 us (40%)
  matrix products  72.7 us (30%)
  blocking collectives  26.6 us (11%)
  other arithmetic  16.2 us (7%)
  between operations  15.1 us (6%)
  local copies, waits for them, and re-layouts  12.2 us (5%)
    psum x1, waiting for transfers between devices, shards(): gram = lax.psum(partial_gram, ('grp', 'dev'))  72.5 us
    dot_general x8, matrix products, apply_operator(): jnp.einsum('utbi,utir->ubr', weighted, tile_panels, preferred_element_typ...  55.9 us
    all_gather x1, waiting for transfers between devices, shards(): everyone = lax.all_gather(group_pool, 'dev', axis=0, tiled=True)  24.1 us
    all_gather x1, blocking collectives, shards(): all_routes = lax.all_gather(route_list, 'dev', axis=0, tiled=True)  17.4 us
    dot_general x8, matrix products, apply_operator(): jnp.dot(direction, gram, precision=lax.Precision.HIGHEST)  11.2 us
    all_to_all x1, blocking collectives, shards(): lax.all_to_all(outgoing, 'grp', split_axis=0, concat_axis=0, tiled=True)  9.2 us
    convert_element_type x7, other arithmetic, apply_operator(): dir_bf = direction.astype(jnp.bfloat16).reshape(USER_BLOCKS, BLOCK, RANK)  7.14 us
  transfers between devices with their start and end apart: 2, of which 2 were waited for; matrix products, arithmetic and copies ran while one was open for 10% of the time, Pallas kernels for 0%

commit v1 on v0

v1 whole, which is shorter than its diff:
```python
import functools

import jax
import jax.numpy as jnp
from jax import lax
from jax.experimental import pallas as pl
from jax.experimental.pallas import tpu as pltpu
from jax.sharding import PartitionSpec as P

RANK = 256
BLOCK = 128
PANELS_DEV = 2
USER_BLOCKS = 4
TILES_PER = 16
ITERS = 8
BF16 = jnp.bfloat16
F32 = jnp.float32

ridge = 0.1

VM = pl.BlockSpec(memory_space=pltpu.VMEM)
SM = pl.BlockSpec(memory_space=pltpu.SMEM)
params = pltpu.CompilerParams(vmem_limit_bytes=40 * 2**20)


def shape(rows, dtype=BF16):
    return jax.ShapeDtypeStruct((rows, RANK), dtype)


def call(body, name, in_specs, out_specs, out_shape, scratch=()):
    return pl.pallas_call(
        body,
        in_specs=in_specs,
        out_specs=out_specs,
        out_shape=out_shape,
        scratch_shapes=list(scratch),
        compiler_params=params,
        name=name,
    )


def own_panel(items, index):
    return items[pl.ds(pl.multiple_of(index * BLOCK, BLOCK), BLOCK), :]


def pack_core(send, items, out, gram_own, gram):
    group = lax.axis_index("grp")
    core = lax.rem(group, 2)
    out[0:BLOCK, :] = own_panel(items, send[0, group ^ 1, 0])
    out[BLOCK : 2 * BLOCK, :] = own_panel(items, send[0, group ^ 3, 0])
    rows = items[...]
    gram[...] = lax.dot_general(rows, rows, (((0,), (0,)), ((), ())), preferred_element_type=F32)
    out[2 * BLOCK : 3 * BLOCK, :] = own_panel(gram, 1 - core).astype(BF16)
    gram_own[...] = own_panel(gram, core)


def pack_y(send, items, gram_own, from_core, out, gram_sum):
    group = lax.axis_index("grp")
    out[0:BLOCK, :] = own_panel(items, send[0, group ^ 2, 0])
    out[BLOCK : 2 * BLOCK, :] = from_core[BLOCK : 2 * BLOCK, :]
    total = gram_own[...] + from_core[2 * BLOCK : 3 * BLOCK, :].astype(F32)
    out[2 * BLOCK : 3 * BLOCK, :] = total.astype(BF16)
    gram_sum[...] = total


def pack_dev(send, route, items, gram_own, from_core, from_y, *refs):
    outs, gram_sum, pool = refs[:8], refs[8], refs[9]
    group = lax.axis_index("grp")
    member = lax.axis_index("dev")
    pool[group] = own_panel(items, send[0, group, 0])
    pool[group ^ 1] = from_core[0:BLOCK, :]
    pool[group ^ 2] = from_y[0:BLOCK, :]
    pool[group ^ 3] = from_y[BLOCK : 2 * BLOCK, :]
    for step in range(8):
        outs[step][0:BLOCK, :] = pool[route[0, member ^ step, 0]]
    total = gram_own[...] + from_y[2 * BLOCK : 3 * BLOCK, :].astype(F32)
    outs[4][BLOCK : 2 * BLOCK, :] = total.astype(BF16)
    gram_sum[...] = total


def add_gram(gram_own, arrived, panel, out, gram_sum):
    total = gram_own[...] + arrived[BLOCK : 2 * BLOCK, :].astype(F32)
    out[0:BLOCK, :] = panel[...]
    out[BLOCK : 2 * BLOCK, :] = total.astype(BF16)
    gram_sum[...] = total


def last_gram(tile_slot, gram_own, arrived, out, gram_sum, places):
    total = gram_own[...] + arrived[BLOCK : 2 * BLOCK, :].astype(F32)
    out[...] = total.astype(BF16)
    gram_sum[...] = total
    member = lax.axis_index("dev")

    def place(tile, _):
        places[tile] = tile_slot[0, tile] ^ member
        return _

    lax.fori_loop(0, places.shape[0], place, 0)


def build_kernel(places, tiles, weights, high, low, target_sum):
    block = pl.program_id(0)
    weights[...] = jnp.zeros_like(weights)
    target_sum[...] = jnp.zeros_like(target_sum)
    for tile in range(TILES_PER):
        first = places[block * TILES_PER + tile] * BLOCK
        columns = pl.ds(pl.multiple_of(first, BLOCK), BLOCK)
        confidence = tiles[tile].astype(F32)
        target = jnp.where(confidence > 0, 1.0 + confidence, 0.0).astype(BF16)
        weights[:, columns] += confidence
        target_sum[:, columns] += target.astype(F32)
    total = target_sum[...]
    top = total.astype(BF16)
    high[...] = top
    low[...] = (total - top.astype(F32)).astype(BF16)


def build_weights(places, confidence, width):
    users = USER_BLOCKS * BLOCK
    return pl.pallas_call(
        build_kernel,
        grid_spec=pltpu.PrefetchScalarGridSpec(
            num_scalar_prefetch=1,
            grid=(USER_BLOCKS,),
            in_specs=[pl.BlockSpec((TILES_PER, BLOCK, BLOCK), lambda b, _: (b, 0, 0))],
            out_specs=[pl.BlockSpec((BLOCK, width), lambda b, _: (b, 0))] * 3,
            scratch_shapes=[pltpu.VMEM((BLOCK, width), F32)],
        ),
        out_shape=[
            jax.ShapeDtypeStruct((users, width), F32),
            jax.ShapeDtypeStruct((users, width), BF16),
            jax.ShapeDtypeStruct((users, width), BF16),
        ],
        compiler_params=params,
        name="build_weights",
    )(places, confidence)


def solve_kernel(count, chunk, halves, weights, high, low, *refs):
    gram_parts, panels = refs[:halves], refs[halves : halves + count]
    result, items, items_t, gram, residual_ref, direction_ref = refs[halves + count :]
    dot = functools.partial(jnp.dot, preferred_element_type=F32)
    for i in range(count):
        rows = slice(i * BLOCK, (i + 1) * BLOCK)
        panel = panels[i][0:BLOCK, :]
        items[rows, :] = panel
        items_t[:, rows] = panel.T
    if halves == 1:
        whole = gram_parts[0][...]
        top = whole.astype(BF16)
        gram[0] = top
        gram[1] = (whole - top.astype(F32)).astype(BF16)
    else:
        core = lax.rem(lax.axis_index("grp"), 2)
        mine = pl.ds(pl.multiple_of(core * BLOCK, BLOCK), BLOCK)
        other = pl.ds(pl.multiple_of((1 - core) * BLOCK, BLOCK), BLOCK)
        whole = gram_parts[0][...]
        top = whole.astype(BF16)
        gram[0, mine, :] = top
        gram[1, mine, :] = (whole - top.astype(F32)).astype(BF16)
        gram[0, other, :] = gram_parts[1][...]
        gram[1, other, :] = jnp.zeros((BLOCK, RANK), BF16)
    parts = [slice(i, i + chunk) for i in range(0, weights.shape[0], chunk)]
    norms = []
    for users in parts:
        right_side = dot(high[users, :], items[...]) + dot(low[users, :], items[...])
        residual_ref[users, :] = right_side
        direction_ref[users, :] = right_side
        result[users, :] = jnp.zeros_like(right_side)
        norms.append(jnp.sum(right_side * right_side, axis=1, keepdims=True))

    def step(_, norms):
        after = []
        for users, norm_now in zip(parts, norms):
            direction = direction_ref[users, :]
            top = direction.astype(BF16)
            rest = (direction - top.astype(F32)).astype(BF16)
            scores = dot(top, items_t[...])
            weighted = (weights[users, :] * scores).astype(BF16)
            image = dot(weighted, items[...])
            image = image + (dot(top, gram[0]) + (dot(rest, gram[0]) + dot(top, gram[1])))
            image = image + ridge * direction
            alpha = norm_now / jnp.sum(direction * image, axis=1, keepdims=True)
            result[users, :] += alpha * direction
            residual = residual_ref[users, :] - alpha * image
            residual_ref[users, :] = residual
            norm_next = jnp.sum(residual * residual, axis=1, keepdims=True)
            direction_ref[users, :] = residual + (norm_next / norm_now) * direction
            after.append(norm_next)
        return tuple(after)

    lax.fori_loop(0, ITERS, step, tuple(norms))


def solve_users(weights, high, low, gram_parts, panels, chunk=256):
    users, width = weights.shape
    return call(
        functools.partial(solve_kernel, len(panels), chunk, len(gram_parts)),
        "solve_users",
        [VM] * (3 + len(gram_parts) + len(panels)),
        VM,
        shape(users, F32),
        [
            pltpu.VMEM((width, RANK), BF16),
            pltpu.VMEM((RANK, width), BF16),
            pltpu.VMEM((2, RANK, RANK), BF16),
            pltpu.VMEM((users, RANK), F32),
            pltpu.VMEM((users, RANK), F32),
        ],
    )(weights, high, low, *gram_parts, *panels)


def swap(array, group_bits, member_bits):
    order = [
        (g * 8 + d, (g ^ group_bits) * 8 + (d ^ member_bits)) for g in range(4) for d in range(8)
    ]
    return lax.ppermute(array, ("grp", "dev"), order)


def shards_4x8(item_factors, send_list, route_list, tile_slot, confidence):
    tiles = tile_slot.shape[1]
    out, gram = call(
        pack_core, "pack_core", [SM, VM], [VM, VM],
        [shape(3 * BLOCK), shape(BLOCK, F32)], [pltpu.VMEM((RANK, RANK), F32)],
    )(send_list, item_factors)
    from_core = swap(out, 1, 0)
    out, gram = call(
        pack_y, "pack_y", [SM, VM, VM, VM], [VM, VM], [shape(3 * BLOCK), shape(BLOCK, F32)]
    )(send_list, item_factors, gram, from_core)
    from_y = swap(out, 2, 0)
    *outs, gram = call(
        pack_dev, "pack_dev", [SM, SM, VM, VM, VM, VM], [VM] * 9,
        [shape(2 * BLOCK if k == 4 else BLOCK) for k in range(8)] + [shape(BLOCK, F32)],
        [pltpu.VMEM((4, BLOCK, RANK), BF16)],
    )(send_list, route_list, item_factors, gram, from_core, from_y)
    panels = [outs[0]] + [None] * 7
    for k in (4, 5, 7, 6):
        panels[k] = swap(outs[k], 0, k)
    add = call(add_gram, "add_gram", [VM] * 3, [VM] * 2, [shape(2 * BLOCK), shape(BLOCK, F32)])
    out, gram = add(gram, panels[4], outs[1])
    panels[1] = swap(out, 0, 1)
    panels[3] = swap(outs[3], 0, 3)
    out, gram = add(gram, panels[1], outs[2])
    panels[2] = swap(out, 0, 2)
    out, gram, places = call(
        last_gram, "last_gram", [SM, VM, VM], [VM, VM, SM],
        [shape(BLOCK), shape(BLOCK, F32), jax.ShapeDtypeStruct((tiles,), jnp.int32)],
    )(tile_slot, gram, panels[2])
    other = swap(out, 1, 0)
    weights, high, low = build_weights(places, confidence, 8 * BLOCK)
    return solve_users(weights, high, low, [gram, other], panels)


def shards(item_factors, send_list, route_list, tile_slot, confidence):
    partial_gram = lax.dot_general(
        item_factors, item_factors, (((0,), (0,)), ((), ())), preferred_element_type=F32
    )
    gram = lax.psum(partial_gram, ("grp", "dev"))
    own_panels = item_factors.reshape(PANELS_DEV, BLOCK, RANK)
    outgoing = own_panels[send_list[0].reshape(-1)]
    group_pool = lax.all_to_all(outgoing, "grp", split_axis=0, concat_axis=0, tiled=True)
    picked = group_pool[route_list[0].reshape(-1)]
    arrived = lax.all_to_all(picked, "dev", split_axis=0, concat_axis=0, tiled=True)
    count = arrived.shape[0]
    weights, high, low = build_weights(tile_slot[0], confidence, count * BLOCK)
    return solve_users(weights, high, low, [gram], [arrived[i] for i in range(count)], BLOCK)


def solution(mesh):
    placed = (
        P(("grp", "dev"), None),
        P(("grp", "dev"), None, None),
        P(("grp", "dev"), None, None),
        P(("grp", "dev"), None),
        P(("grp", "dev"), None, None),
    )
    body = shards_4x8 if (mesh.shape["grp"], mesh.shape["dev"]) == (4, 8) else shards
    return jax.shard_map(
        body, mesh=mesh, in_specs=placed, out_specs=P(("grp", "dev"), None), check_vma=False
    )
```

time: 241 us -> 55.1 us (0.23)
  waiting for transfers between devices: 96.6 us -> 14.4 us
  matrix products: 72.7 us -> 0 us
  blocking collectives: 26.6 us -> 0 us
  starting transfers between devices: 0.05 us -> 18.6 us
  Pallas kernels: 0 us -> 17.7 us
  other arithmetic: 16.2 us -> 0 us
  between operations: 15.1 us -> 0.09 us
  local copies, waits for them, and re-layouts: 12.2 us -> 4.09 us
    dot_general x18 -> x0, matrix products: 72.7 us -> none  [the longest x8 55.9 us: apply_operator(): jnp.einsum('utbi,utir->ubr', weighted, tile_panels, preferred_element_typ...]
    psum x1 -> x0, waiting for transfers between devices: 72.5 us -> none  [shards(): gram = lax.psum(partial_gram, ('grp', 'dev'))]
    all_gather x1 -> x0, waiting for transfers between devices: 24.1 us -> none  [shards(): everyone = lax.all_gather(group_pool, 'dev', axis=0, tiled=True)]
    ppermute x0 -> x10, starting transfers between devices: none -> 18.6 us  [swap(): return lax.ppermute(array, ('grp', 'dev'), order)]
    pallas_call x0 -> x8, Pallas kernels: none -> 17.7 us  [the longest x1 10.8 us: solve_users(): call(functools.partial(solve_kernel, len(panels), chunk, len(gram_parts))...]
    all_gather x1 -> x0, blocking collectives: 17.4 us -> none  [shards(): all_routes = lax.all_gather(route_list, 'dev', axis=0, tiled=True)]
    ppermute x0 -> x10, waiting for transfers between devices: none -> 14.4 us  [swap(): return lax.ppermute(array, ('grp', 'dev'), order)]
    all_to_all x1 -> x0, blocking collectives: 9.2 us -> none  [shards(): lax.all_to_all(outgoing, 'grp', split_axis=0, concat_axis=0, tiled=True)]
  transfers between devices with their start and end apart: 2 -> 10, of which waited for: 2 -> 4; matrix products, arithmetic and copies ran while one was open for 10% -> 1% of each run, Pallas kernels for 0% -> 9%
where the time goes in v1:
time: 55.1 us; the launch traced here: 54.9 us
  starting transfers between devices  18.6 us (34%)
  Pallas kernels  17.7 us (32%)
  waiting for transfers between devices  14.4 us (26%)
  local copies, waits for them, and re-layouts  4.09 us (7%)
    ppermute x10, starting transfers between devices, swap(): return lax.ppermute(array, ('grp', 'dev'), order)  18.6 us
    ppermute x10, waiting for transfers between devices, swap(): return lax.ppermute(array, ('grp', 'dev'), order)  14.4 us
    pallas_call x1, Pallas kernels, solve_users(): call(functools.partial(solve_kernel, len(panels), chunk, len(gram_parts))...  10.8 us
    unnamed x10, local copies, waits for them, and re-layouts  4.09 us
    pallas_call x1, Pallas kernels, build_weights(): pl.pallas_call(build_kernel, grid_spec=pltpu.PrefetchScalarGridSpec(num_s...  3.17 us
    pallas_call x1, Pallas kernels, shards_4x8(): call(last_gram, 'last_gram', [SM, VM, VM], [VM, VM, SM], [shape(BLOCK), s...  1.55 us
  transfers between devices with their start and end apart: 10, of which 4 were waited for; matrix products, arithmetic and copies ran while one was open for 1% of the time, Pallas kernels for 9%

profile of v1, /device:TPU:1, one launch (start us, length us, event | category | flops | bytes accessed | tf_op | source)
XLA Modules:
  0.0 54.9 jit_solution(14044151208098002319)
XLA Ops:
  0.0 0.0 copy-start
  0.0 0.9 %copy.8.send = s32[1,4,1]{2,1,0:T(4,128)S(1)} copy(s32[1,4,1]{1,2,0:T(1,128)} %param.6) | data formatting | bytes 32 | tf_op args[1]
  0.9 0.0 copy-start.1
  0.9 0.9 %copy-done.1 = bf16[256,256]{1,0:T(8,128)(2,1)S(1)} copy-done((bf16[256,256]{1,0:T(8,128)(2,1)S(1)}, bf16[256,256]{1,0:T(8,128)(2,1)}, u32[]{:S(2)}) %copy-start.1) | copy-done | bytes 131096
  1.8 0.8 %pack_core.1 = (bf16[384,256]{1,0:T(8,128)(2,1)S(1)}, f32[128,256]{1,0:T(8,128)S(1)}) custom-call(s32[1,4,1]{2,1,0:T(4,128)S(1)} %copy.8.send, bf16[256,256]{1,0:T(8,128)(2,1)S(1)} %copy-done.1), custom_call_target="tpu_custom_call" | custom-call | tf_op jit(solution)/shard_map/pack_core/pallas_call | solution.py:222
  2.6 0.1 collective-permute-start
  2.8 1.4 %collective-permute-done.from_core = bf16[384,256]{1,0:T(8,128)(2,1)S(1)} collective-permute-done((bf16[384,256]{1,0:T(8,128)(2,1)S(1)}, bf16[384,256]{1,0:T(8,128)(2,1)S(1)}, u32[]{:S(2)}, u32[]{:S(2)}) %collective-permute-start) | collective-permute-done | bytes 196640 | tf_op jit(solution)/shard_map/ppermute | solution.py:217
  4.1 0.6 %pack_y.1 = (bf16[384,256]{1,0:T(8,128)(2,1)S(1)}, f32[128,256]{1,0:T(8,128)S(1)}) custom-call(s32[1,4,1]{2,1,0:T(4,128)S(1)} %copy.8.send, bf16[256,256]{1,0:T(8,128)(2,1)S(1)} %copy-done.1, f32[128,256]{1,0:T(8,128)S(1)} %get-tuple-element.28.gram_own, bf16[384,256]{1,0:T(8,128)(2,1)S(1)} %collective-permute-done.from_core), custom_call_target="tpu_custom_call" | custom-call | tf_op jit(solution)/shard_map/pack_y/pallas_call | solution.py:227
  4.7 2.4 %collective-permute-start.1 = (bf16[384,256]{1,0:T(8,128)(2,1)S(1)}, bf16[384,256]{1,0:T(8,128)(2,1)S(1)}, u32[]{:S(2)}, u32[]{:S(2)}) collective-permute-start(bf16[384,256]{1,0:T(8,128)(2,1)S(1)} %get-tuple-element.31), channel_id=1, source_target_pairs={{0,16},{1,17},{2,18},{3,19},{4,20},{5,21},{6,22},{7,23},{8,24},{9,... | collective-permute-start | bytes 589832 | tf_op jit(solution)/shard_map/ppermute | solution.py:217
  7.2 0.7 %copy.9.route = s32[1,8,1]{2,1,0:T(8,128)S(1)} copy(s32[1,8,1]{1,2,0:T(1,128)} %param.7) | data formatting | bytes 64 | tf_op args[2]
  7.9 4.2 %collective-permute-done.1.from_y = bf16[384,256]{1,0:T(8,128)(2,1)S(1)} collective-permute-done((bf16[384,256]{1,0:T(8,128)(2,1)S(1)}, bf16[384,256]{1,0:T(8,128)(2,1)S(1)}, u32[]{:S(2)}, u32[]{:S(2)}) %collective-permute-start.1) | collective-permute-done | bytes 196640 | tf_op jit(solution)/shard_map/ppermute | solution.py:217
  12.2 0.0 copy-start.2
  12.2 0.9 %copy-done.2 = bf16[256,256]{1,0:T(8,128)(2,1)S(1)} copy-done((bf16[256,256]{1,0:T(8,128)(2,1)S(1)}, bf16[256,256]{1,0:T(8,128)(2,1)}, u32[]{:S(2)}) %copy-start.2) | copy-done | bytes 131096
  13.1 0.7 %pack_dev.1 = (bf16[128,256]{1,0:T(8,128)(2,1)S(1)}, bf16[128,256]{1,0:T(8,128)(2,1)S(1)}, bf16[128,256]{1,0:T(8,128)(2,1)S(1)}, bf16[128,256]{1,0:T(8,128)(2,1)...) custom-call(s32[1,4,1]{2,1,0:T(4,128)S(1)} %copy.8.send, ...), custom_call_target="tpu_custom_call" | custom-call | tf_op jit(solution)/shard_map/pack_dev/pallas_call | solution.py:231
  13.8 2.3 %collective-permute-start.2 = (bf16[256,256]{1,0:T(8,128)(2,1)S(1)}, bf16[256,256]{1,0:T(8,128)(2,1)S(1)}, u32[]{:S(2)}, u32[]{:S(2)}) collective-permute-start(bf16[256,256]{1,0:T(8,128)(2,1)S(1)} %get-tuple-element.33), channel_id=1, source_target_pairs={{0,4},{1,5},{2,6},{3,7},{4,0},{5,1},{6,2},{7,3},{8,12},{9,13},{10,... | collective-permute-start | bytes 393224 | tf_op jit(solution)/shard_map/ppermute | solution.py:217
  16.0 6.0 %collective-permute-done.2.arrived.refs_6_ = bf16[256,256]{1,0:T(8,128)(2,1)S(1)} collective-permute-done((bf16[256,256]{1,0:T(8,128)(2,1)S(1)}, bf16[256,256]{1,0:T(8,128)(2,1)S(1)}, u32[]{:S(2)}, u32[]{:S(2)}) %collective-permute-start.2) | collective-permute-done | bytes 131104 | tf_op jit(solution)/shard_map/ppermute | solution.py:217
  22.0 1.1 %collective-permute-start.3 = (bf16[256,256]{1,0:T(8,128)(2,1)S(1)}, bf16[256,256]{1,0:T(8,128)(2,1)S(1)}, u32[]{:S(2)}, u32[]{:S(2)}) collective-permute-start(bf16[256,256]{1,0:T(8,128)(2,1)S(1)} %get-tuple-element.36), channel_id=1, source_target_pairs={{0,1},{1,0},{2,3},{3,2},{4,5},{5,4},{6,7},{7,6},{8,9},{9,8},{10,11... | collective-permute-start | bytes 393224 | tf_op jit(solution)/shard_map/ppermute | solution.py:217
  23.1 2.8 %collective-permute-done.3.arrived.refs_3_ = bf16[256,256]{1,0:T(8,128)(2,1)S(1)} collective-permute-done((bf16[256,256]{1,0:T(8,128)(2,1)S(1)}, bf16[256,256]{1,0:T(8,128)(2,1)S(1)}, u32[]{:S(2)}, u32[]{:S(2)}) %collective-permute-start.3) | collective-permute-done | bytes 131104 | tf_op jit(solution)/shard_map/ppermute | solution.py:217
  25.9 1.7 %collective-permute-start.4 = (bf16[256,256]{1,0:T(8,128)(2,1)S(1)}, bf16[256,256]{1,0:T(8,128)(2,1)S(1)}, u32[]{:S(2)}, u32[]{:S(2)}) collective-permute-start(bf16[256,256]{1,0:T(8,128)(2,1)S(1)} %get-tuple-element.39), channel_id=1, source_target_pairs={{0,2},{1,3},{2,0},{3,1},{4,6},{5,7},{6,4},{7,5},{8,10},{9,11},{10,... | collective-permute-start | bytes 393224 | tf_op jit(solution)/shard_map/ppermute | solution.py:217
  27.7 1.0 %collective-permute-start.6 = (bf16[128,256]{1,0:T(8,128)(2,1)S(1)}, bf16[128,256]{1,0:T(8,128)(2,1)S(1)}, u32[]{:S(2)}, u32[]{:S(2)}) collective-permute-start(bf16[128,256]{1,0:T(8,128)(2,1)S(1)} %get-tuple-element.47), channel_id=1, source_target_pairs={{0,3},{1,2},{2,1},{3,0},{4,7},{5,6},{6,5},{7,4},{8,11},{9,10},{10,... | collective-permute-start | bytes 196616 | tf_op jit(solution)/shard_map/ppermute | solution.py:217
  28.7 3.1 %collective-permute-start.7 = (bf16[128,256]{1,0:T(8,128)(2,1)S(1)}, bf16[128,256]{1,0:T(8,128)(2,1)S(1)}, u32[]{:S(2)}, u32[]{:S(2)}) collective-permute-start(bf16[128,256]{1,0:T(8,128)(2,1)S(1)} %get-tuple-element.48), channel_id=1, source_target_pairs={{0,5},{1,4},{2,7},{3,6},{4,1},{5,0},{6,3},{7,2},{8,13},{9,12},{10,... | collective-permute-start | bytes 196616 | tf_op jit(solution)/shard_map/ppermute | solution.py:217
  31.8 1.1 %collective-permute-start.8 = (bf16[128,256]{1,0:T(8,128)(2,1)S(1)}, bf16[128,256]{1,0:T(8,128)(2,1)S(1)}, u32[]{:S(2)}, u32[]{:S(2)}) collective-permute-start(bf16[128,256]{1,0:T(8,128)(2,1)S(1)} %get-tuple-element.49), channel_id=1, source_target_pairs={{0,6},{1,7},{2,4},{3,5},{4,2},{5,3},{6,0},{7,1},{8,14},{9,15},{10,... | collective-permute-start | bytes 196616 | tf_op jit(solution)/shard_map/ppermute | solution.py:217
  32.9 3.1 %collective-permute-start.9 = (bf16[128,256]{1,0:T(8,128)(2,1)S(1)}, bf16[128,256]{1,0:T(8,128)(2,1)S(1)}, u32[]{:S(2)}, u32[]{:S(2)}) collective-permute-start(bf16[128,256]{1,0:T(8,128)(2,1)S(1)} %get-tuple-element.50), channel_id=1, source_target_pairs={{0,7},{1,6},{2,5},{3,4},{4,3},{5,2},{6,1},{7,0},{8,15},{9,14},{10,... | collective-permute-start | bytes 196616 | tf_op jit(solution)/shard_map/ppermute | solution.py:217
  35.9 0.0 collective-permute-done.4.arrived.refs_4_
  35.9 0.0 copy-start.3
  35.9 0.7 %copy-done.3 = s32[1,64]{1,0:T(1,128)S(1)} copy-done((s32[1,64]{1,0:T(1,128)S(1)}, s32[1,64]{1,0:T(1,128)}, u32[]{:S(2)}) %copy-start.3) | copy-done | bytes 280
  36.6 1.6 %last_gram.1 = (bf16[128,256]{1,0:T(8,128)(2,1)S(1)}, f32[128,256]{1,0:T(8,128)S(1)}, s32[64]{0:T(128)S(1)}) custom-call(s32[1,64]{1,0:T(1,128)S(1)} %copy-done.3, f32[128,256]{1,0:T(8,128)S(1)} %get-tuple-element.38.gram_own, bf16[256,256]{1,0:T(8,128)(2,1)S(1)} %collective-permute-done.4.arrived.refs_4_), custom_call_target="tpu_custom_call" | custom-call | tf_op jit(solution)/shard_map/last_gram/pallas_call | solution.py:245
  38.2 2.7 %collective-permute-start.5 = (bf16[128,256]{1,0:T(8,128)(2,1)S(1)}, bf16[128,256]{1,0:T(8,128)(2,1)S(1)}, u32[]{:S(2)}, u32[]{:S(2)}) collective-permute-start(bf16[128,256]{1,0:T(8,128)(2,1)S(1)} %get-tuple-element.45), channel_id=1, source_target_pairs={{0,8},{1,9},{2,10},{3,11},{4,12},{5,13},{6,14},{7,15},{8,0},{9,1},... | collective-permute-start | bytes 196616 | tf_op jit(solution)/shard_map/ppermute | solution.py:217
  40.9 0.0 copy-done
  40.9 3.2 %build_weights.1 = (f32[512,1024]{1,0:T(8,128)S(1)}, bf16[512,1024]{1,0:T(8,128)(2,1)S(1)}, bf16[512,1024]{1,0:T(8,128)(2,1)S(1)}) custom-call(s32[64]{0:T(128)S(1)} %get-tuple-element.40.places, bf16[64,128,128]{2,1,0:T(8,128)(2,1)S(1)} %copy-done), custom_call_target="tpu_custom_call" | custom-call | tf_op jit(solution)/shard_map/build_weights/pallas_call | solution.py:120
  44.0 0.0 collective-permute-done.6.refs_5_
  44.1 0.0 collective-permute-done.7.refs_7_
  44.1 0.0 collective-permute-done.8.refs_8_
  44.1 0.0 collective-permute-done.9.refs_9_
  44.1 0.0 collective-permute-done.5.refs_1_
  44.1 10.8 %solve_users.1 = f32[512,256]{1,0:T(8,128)} custom-call(f32[512,1024]{1,0:T(8,128)S(1)} %get-tuple-element.41.weights, bf16[512,1024]{1,0:T(8,128)(2,1)S(1)} %get-tuple-element.42.high, bf16[512,1024]{1,0:T(8,128)(2,1)S(1)} %get-tuple-element.43.low, f32[128,256]{1,0:T(8,128)S(1)} %get-tuple-element.44.refs_0_, ...), custom_call_target="tpu_custom_call" | custom-call | tf_op jit(solution)/shard_map/solve_users/pallas_call | solution.py:197
  (2 shorter events, 0.0 us)
Async XLA Ops:
  0.0 40.9 %copy-start = (bf16[64,128,128]{2,1,0:T(8,128)(2,1)S(1)}, bf16[64,128,128]{2,1,0:T(8,128)(2,1)}, u32[]{:S(2)}) copy-start(bf16[64,128,128]{2,1,0:T(8,128)(2,1)} %tiles.1) | copy-start | bytes 6291460
  0.9 0.9 %copy-start.1 = (bf16[256,256]{1,0:T(8,128)(2,1)S(1)}, bf16[256,256]{1,0:T(8,128)(2,1)}, u32[]{:S(2)}) copy-start(bf16[256,256]{1,0:T(8,128)(2,1)} %items.5) | copy-start | bytes 393220
  2.6 1.5 %collective-permute-start = (bf16[384,256]{1,0:T(8,128)(2,1)S(1)}, bf16[384,256]{1,0:T(8,128)(2,1)S(1)}, u32[]{:S(2)}, u32[]{:S(2)}) collective-permute-start(bf16[384,256]{1,0:T(8,128)(2,1)S(1)} %get-tuple-element.29), channel_id=1, source_target_pairs={{0,8},{1,9},{2,10},{3,11},{4,12},{5,13},{6,14},{7,15},{8,0},{9,1},... | collective-permute-start | bytes 589832 | tf_op jit(solution)/shard_map/ppermute | solution.py:217
  4.7 7.4 %collective-permute-start.1 = (bf16[384,256]{1,0:T(8,128)(2,1)S(1)}, bf16[384,256]{1,0:T(8,128)(2,1)S(1)}, u32[]{:S(2)}, u32[]{:S(2)}) collective-permute-start(bf16[384,256]{1,0:T(8,128)(2,1)S(1)} %get-tuple-element.31), channel_id=1, source_target_pairs={{0,16},{1,17},{2,18},{3,19},{4,20},{5,21},{6,22},{7,23},{8,24},{9,... | collective-permute-start | bytes 589832 | tf_op jit(solution)/shard_map/ppermute | solution.py:217
  12.2 0.9 %copy-start.2 = (bf16[256,256]{1,0:T(8,128)(2,1)S(1)}, bf16[256,256]{1,0:T(8,128)(2,1)}, u32[]{:S(2)}) copy-start(bf16[256,256]{1,0:T(8,128)(2,1)} %items.5) | copy-start | bytes 393220
  13.8 8.2 %collective-permute-start.2 = (bf16[256,256]{1,0:T(8,128)(2,1)S(1)}, bf16[256,256]{1,0:T(8,128)(2,1)S(1)}, u32[]{:S(2)}, u32[]{:S(2)}) collective-permute-start(bf16[256,256]{1,0:T(8,128)(2,1)S(1)} %get-tuple-element.33), channel_id=1, source_target_pairs={{0,4},{1,5},{2,6},{3,7},{4,0},{5,1},{6,2},{7,3},{8,12},{9,13},{10,... | collective-permute-start | bytes 393224 | tf_op jit(solution)/shard_map/ppermute | solution.py:217
  22.0 3.9 %collective-permute-start.3 = (bf16[256,256]{1,0:T(8,128)(2,1)S(1)}, bf16[256,256]{1,0:T(8,128)(2,1)S(1)}, u32[]{:S(2)}, u32[]{:S(2)}) collective-permute-start(bf16[256,256]{1,0:T(8,128)(2,1)S(1)} %get-tuple-element.36), channel_id=1, source_target_pairs={{0,1},{1,0},{2,3},{3,2},{4,5},{5,4},{6,7},{7,6},{8,9},{9,8},{10,11... | collective-permute-start | bytes 393224 | tf_op jit(solution)/shard_map/ppermute | solution.py:217
  25.9 10.0 %collective-permute-start.4 = (bf16[256,256]{1,0:T(8,128)(2,1)S(1)}, bf16[256,256]{1,0:T(8,128)(2,1)S(1)}, u32[]{:S(2)}, u32[]{:S(2)}) collective-permute-start(bf16[256,256]{1,0:T(8,128)(2,1)S(1)} %get-tuple-element.39), channel_id=1, source_target_pairs={{0,2},{1,3},{2,0},{3,1},{4,6},{5,7},{6,4},{7,5},{8,10},{9,11},{10,... | collective-permute-start | bytes 393224 | tf_op jit(solution)/shard_map/ppermute | solution.py:217
  27.7 16.4 %collective-permute-start.6 = (bf16[128,256]{1,0:T(8,128)(2,1)S(1)}, bf16[128,256]{1,0:T(8,128)(2,1)S(1)}, u32[]{:S(2)}, u32[]{:S(2)}) collective-permute-start(bf16[128,256]{1,0:T(8,128)(2,1)S(1)} %get-tuple-element.47), channel_id=1, source_target_pairs={{0,3},{1,2},{2,1},{3,0},{4,7},{5,6},{6,5},{7,4},{8,11},{9,10},{10,... | collective-permute-start | bytes 196616 | tf_op jit(solution)/shard_map/ppermute | solution.py:217
  28.7 15.4 %collective-permute-start.7 = (bf16[128,256]{1,0:T(8,128)(2,1)S(1)}, bf16[128,256]{1,0:T(8,128)(2,1)S(1)}, u32[]{:S(2)}, u32[]{:S(2)}) collective-permute-start(bf16[128,256]{1,0:T(8,128)(2,1)S(1)} %get-tuple-element.48), channel_id=1, source_target_pairs={{0,5},{1,4},{2,7},{3,6},{4,1},{5,0},{6,3},{7,2},{8,13},{9,12},{10,... | collective-permute-start | bytes 196616 | tf_op jit(solution)/shard_map/ppermute | solution.py:217
  31.8 12.3 %collective-permute-start.8 = (bf16[128,256]{1,0:T(8,128)(2,1)S(1)}, bf16[128,256]{1,0:T(8,128)(2,1)S(1)}, u32[]{:S(2)}, u32[]{:S(2)}) collective-permute-start(bf16[128,256]{1,0:T(8,128)(2,1)S(1)} %get-tuple-element.49), channel_id=1, source_target_pairs={{0,6},{1,7},{2,4},{3,5},{4,2},{5,3},{6,0},{7,1},{8,14},{9,15},{10,... | collective-permute-start | bytes 196616 | tf_op jit(solution)/shard_map/ppermute | solution.py:217
  32.9 11.2 %collective-permute-start.9 = (bf16[128,256]{1,0:T(8,128)(2,1)S(1)}, bf16[128,256]{1,0:T(8,128)(2,1)S(1)}, u32[]{:S(2)}, u32[]{:S(2)}) collective-permute-start(bf16[128,256]{1,0:T(8,128)(2,1)S(1)} %get-tuple-element.50), channel_id=1, source_target_pairs={{0,7},{1,6},{2,5},{3,4},{4,3},{5,2},{6,1},{7,0},{8,15},{9,14},{10,... | collective-permute-start | bytes 196616 | tf_op jit(solution)/shard_map/ppermute | solution.py:217
  35.9 0.7 %copy-start.3 = (s32[1,64]{1,0:T(1,128)S(1)}, s32[1,64]{1,0:T(1,128)}, u32[]{:S(2)}) copy-start(s32[1,64]{1,0:T(1,128)} %tile_slot.1) | copy-start | bytes 772
  38.2 5.9 %collective-permute-start.5 = (bf16[128,256]{1,0:T(8,128)(2,1)S(1)}, bf16[128,256]{1,0:T(8,128)(2,1)S(1)}, u32[]{:S(2)}, u32[]{:S(2)}) collective-permute-start(bf16[128,256]{1,0:T(8,128)(2,1)S(1)} %get-tuple-element.45), channel_id=1, source_target_pairs={{0,8},{1,9},{2,10},{3,11},{4,12},{5,13},{6,14},{7,15},{8,0},{9,1},... | collective-permute-start | bytes 196616 | tf_op jit(solution)/shard_map/ppermute | solution.py:217

commit v2 on v1

v2 whole, which is shorter than its diff:
```python
import functools

import jax
import jax.numpy as jnp
from jax import lax
from jax.experimental import pallas as pl
from jax.experimental.pallas import tpu as pltpu
from jax.sharding import PartitionSpec as P

RANK = 256
BLOCK = 128
PANELS_DEV = 2
USER_BLOCKS = 4
TILES_PER = 16
ITERS = 8
BF16 = jnp.bfloat16
F32 = jnp.float32

ridge = 0.1
COST = 1000000000
LEAD = 3000000000

VM = pl.BlockSpec(memory_space=pltpu.VMEM)
ANY = pl.BlockSpec(memory_space=pl.ANY)
SM = pl.BlockSpec(memory_space=pltpu.SMEM)


def params():
    return pltpu.CompilerParams(vmem_limit_bytes=40 * 2**20)


def shape(rows, dtype=BF16):
    return jax.ShapeDtypeStruct((rows, RANK), dtype)


def call(body, name, in_specs, out_specs, out_shape, scratch=(), cost=0):
    return pl.pallas_call(
        body,
        in_specs=in_specs,
        out_specs=out_specs,
        out_shape=out_shape,
        scratch_shapes=list(scratch),
        compiler_params=params(),
        cost_estimate=pl.CostEstimate(flops=cost, transcendentals=0, bytes_accessed=0),
        name=name,
    )


def own_panel(items, index):
    return items[pl.ds(pl.multiple_of(index * BLOCK, BLOCK), BLOCK), :]


def first_kernel(send_hbm, route_hbm, items_hbm, _, out, panel_y, panel_own, gram_own, picks, *scratch):
    send, route, items, gram, sems = scratch
    sources = (items_hbm, send_hbm, route_hbm)
    copies = [
        pltpu.make_async_copy(source, target, sems.at[i])
        for i, (source, target) in enumerate(zip(sources, (items, send, route)))
    ]
    for copy in copies:
        copy.start()
    group = lax.axis_index("grp")
    member = lax.axis_index("dev")
    core = lax.rem(group, 2)
    copies[0].wait()
    rows = items[...]
    gram[...] = lax.dot_general(rows, rows, (((0,), (0,)), ((), ())), preferred_element_type=F32)
    copies[1].wait()
    out[0:BLOCK, :] = own_panel(items, send[0, group ^ 1])
    out[BLOCK : 2 * BLOCK, :] = own_panel(items, send[0, group ^ 3])
    panel_y[...] = own_panel(items, send[0, group ^ 2])
    panel_own[...] = own_panel(items, send[0, group])
    out[2 * BLOCK : 3 * BLOCK, :] = own_panel(gram, 1 - core).astype(BF16)
    gram_own[...] = own_panel(gram, core)
    copies[2].wait()
    for step in range(8):
        picks[step : step + 1, :] = jnp.full((1, BLOCK), route[0, member ^ step] ^ group, jnp.int32)


def pack_y(panel_y, gram_own, from_core, out, gram_out, gram_sum):
    out[0:BLOCK, :] = panel_y[...]
    out[BLOCK : 2 * BLOCK, :] = from_core[BLOCK : 2 * BLOCK, :]
    total = gram_own[...] + from_core[2 * BLOCK : 3 * BLOCK, :].astype(F32)
    gram_out[...] = total.astype(BF16)
    gram_sum[...] = total


def pack_dev(picks, panel_own, from_core, from_y, *refs):
    outs, pool = refs[:8], refs[8]
    pool[0] = panel_own[...]
    pool[1] = from_core[0:BLOCK, :]
    pool[2] = from_y[0:BLOCK, :]
    pool[3] = from_y[BLOCK : 2 * BLOCK, :]
    for step in range(8):
        outs[step][...] = pool[jnp.max(picks[step : step + 1, :])]


def add_gram(gram_own, arrived, out, gram_sum):
    total = gram_own[...] + arrived[...].astype(F32)
    out[...] = total.astype(BF16)
    gram_sum[...] = total


def pack_near(gram_own, arrived, *refs):
    panels, outs, gram_sum = refs[:3], refs[4:7], refs[7]
    total = gram_own[...] + arrived[...].astype(F32)
    gram_sum[...] = total
    for panel, out in zip(panels, outs):
        out[0:BLOCK, :] = panel[...]
        out[BLOCK : 2 * BLOCK, :] = total.astype(BF16)


def last_gram(gram_own, *refs):
    out, gram_sum = refs[-2:]
    total = gram_own[...]
    for part in refs[:3]:
        total += part[BLOCK : 2 * BLOCK, :].astype(F32)
    out[...] = total.astype(BF16)
    gram_sum[...] = total


def touch(*refs):
    refs[-1][...] = jnp.zeros_like(refs[-1])


def after(cost, *arrays):
    return call(
        touch, "after", [ANY] * len(arrays), VM, jax.ShapeDtypeStruct((8, BLOCK), F32), cost=cost
    )(*arrays)


def build_kernel(mixed, slots, tiles, _, weights, high, low, target_sum):
    block = pl.program_id(0)
    turn = lax.axis_index("dev") if mixed else 0
    weights[...] = jnp.zeros_like(weights)
    target_sum[...] = jnp.zeros_like(target_sum)
    for tile in range(TILES_PER):
        first = (slots[0, block * TILES_PER + tile] ^ turn) * BLOCK
        columns = pl.ds(pl.multiple_of(first, BLOCK), BLOCK)
        confidence = tiles[tile].astype(F32)
        target = jnp.where(confidence > 0, 1.0 + confidence, 0.0).astype(BF16)
        weights[:, columns] += confidence
        target_sum[:, columns] += target.astype(F32)
    total = target_sum[...]
    top = total.astype(BF16)
    high[...] = top
    low[...] = (total - top.astype(F32)).astype(BF16)


def build_weights(slots, confidence, after, width, mixed):
    users = USER_BLOCKS * BLOCK
    return pl.pallas_call(
        functools.partial(build_kernel, mixed),
        grid_spec=pltpu.PrefetchScalarGridSpec(
            num_scalar_prefetch=1,
            grid=(USER_BLOCKS,),
            in_specs=[pl.BlockSpec((TILES_PER, BLOCK, BLOCK), lambda b, _: (b, 0, 0)), ANY],
            out_specs=[pl.BlockSpec((BLOCK, width), lambda b, _: (b, 0))] * 3,
            scratch_shapes=[pltpu.VMEM((BLOCK, width), F32)],
        ),
        out_shape=[
            jax.ShapeDtypeStruct((users, width), F32),
            jax.ShapeDtypeStruct((users, width), BF16),
            jax.ShapeDtypeStruct((users, width), BF16),
        ],
        compiler_params=params(),
        name="build_weights",
    )(slots, confidence, after)


def right_kernel(count, chunk, weights, high, low, *refs):
    panels, (items, items_t, right_side, image) = refs[:count], refs[count + 1 :]
    dot = functools.partial(jnp.dot, preferred_element_type=F32)
    for i in range(count):
        rows = slice(i * BLOCK, (i + 1) * BLOCK)
        panel = panels[i][0:BLOCK, :]
        items[rows, :] = panel
        items_t[:, rows] = panel.T
    for start in range(0, weights.shape[0], chunk):
        users = slice(start, start + chunk)
        target = dot(high[users, :], items[...]) + dot(low[users, :], items[...])
        right_side[users, :] = target
        scores = dot(target.astype(BF16), items_t[...])
        image[users, :] = dot((weights[users, :] * scores).astype(BF16), items[...])


def solve_kernel(halves, chunk, weights, items, items_t, right_side, first_image, *refs):
    gram_parts = refs[:halves]
    result, gram, residual_ref, direction_ref = refs[halves:]
    dot = functools.partial(jnp.dot, preferred_element_type=F32)
    whole = gram_parts[0][...]
    top = whole.astype(BF16)
    rest = (whole - top.astype(F32)).astype(BF16)
    if halves == 1:
        gram[0] = top
        gram[1] = rest
    else:
        core = lax.rem(lax.axis_index("grp"), 2)
        mine = pl.ds(pl.multiple_of(core * BLOCK, BLOCK), BLOCK)
        other = pl.ds(pl.multiple_of((1 - core) * BLOCK, BLOCK), BLOCK)
        gram[0, mine, :] = top
        gram[1, mine, :] = rest
        gram[0, other, :] = gram_parts[1][...]
        gram[1, other, :] = jnp.zeros((BLOCK, RANK), BF16)
    parts = [slice(i, i + chunk) for i in range(0, weights.shape[0], chunk)]

    def advance(users, norm_now, direction, residual, solved, image):
        top = direction.astype(BF16)
        rest = (direction - top.astype(F32)).astype(BF16)
        if image is None:
            scores = dot(top, items_t[...])
            image = dot((weights[users, :] * scores).astype(BF16), items[...])
        image = image + (dot(top, gram[0]) + (dot(rest, gram[0]) + dot(top, gram[1])))
        image = image + ridge * direction
        alpha = norm_now / jnp.sum(direction * image, axis=1, keepdims=True)
        moved = alpha * direction
        result[users, :] = moved if solved is None else solved + moved
        residual = residual - alpha * image
        residual_ref[users, :] = residual
        norm_next = jnp.sum(residual * residual, axis=1, keepdims=True)
        direction_ref[users, :] = residual + (norm_next / norm_now) * direction
        return norm_next

    norms = []
    for users in parts:
        start = right_side[users, :]
        norm = jnp.sum(start * start, axis=1, keepdims=True)
        norms.append(advance(users, norm, start, start, None, first_image[users, :]))

    def step(_, norms):
        return tuple(
            advance(users, norm, direction_ref[users, :], residual_ref[users, :], result[users, :], None)
            for users, norm in zip(parts, norms)
        )

    lax.fori_loop(1, ITERS, step, tuple(norms))


def start_solve(weights, high, low, panels, after, chunk=256):
    users, width = weights.shape
    return call(
        functools.partial(right_kernel, len(panels), chunk), "right_side",
        [VM] * (3 + len(panels)) + [ANY], [VM] * 4,
        [shape(width), jax.ShapeDtypeStruct((RANK, width), BF16), shape(users, F32), shape(users, F32)],
    )(weights, high, low, *panels, after)


def solve_users(weights, started, gram_parts, chunk=256):
    users = weights.shape[0]
    return call(
        functools.partial(solve_kernel, len(gram_parts), chunk), "solve_users",
        [VM] * (5 + len(gram_parts)), VM, shape(users, F32),
        [pltpu.VMEM((2, RANK, RANK), BF16), pltpu.VMEM((users, RANK), F32), pltpu.VMEM((users, RANK), F32)],
    )(weights, *started, *gram_parts)


def swap(array, group_bits, member_bits):
    order = [
        (g * 8 + d, (g ^ group_bits) * 8 + (d ^ member_bits)) for g in range(4) for d in range(8)
    ]
    return lax.ppermute(array, ("grp", "dev"), order)


def shards_4x8(item_factors, send_list, route_list, tile_slot, confidence):
    send_list, route_list = send_list.reshape(1, -1), route_list.reshape(1, -1)
    half, both = shape(BLOCK), shape(2 * BLOCK)
    total = shape(BLOCK, F32)
    out, panel_y, panel_own, gram, picks = call(
        first_kernel, "first", [ANY] * 4, [VM] * 5,
        [shape(3 * BLOCK), half, half, total, jax.ShapeDtypeStruct((8, BLOCK), jnp.int32)],
        [
            pltpu.SMEM(send_list.shape, jnp.int32), pltpu.SMEM(route_list.shape, jnp.int32),
            pltpu.VMEM(item_factors.shape, BF16), pltpu.VMEM((RANK, RANK), F32),
            pltpu.SemaphoreType.DMA((3,)),
        ],
    )(send_list, route_list, item_factors, after(LEAD))
    from_core = swap(out, 1, 0)
    out, gram_out, gram = call(pack_y, "pack_y", [VM] * 3, [VM] * 3, [both, half, total])(
        panel_y, gram, from_core
    )
    from_y = swap(out, 2, 0)
    gram_in = swap(gram_out, 0, 4)
    outs = call(
        pack_dev, "pack_dev", [VM] * 4, [VM] * 8, [half] * 8, [pltpu.VMEM((4, BLOCK, RANK), BF16)]
    )(picks, panel_own, from_core, from_y)
    panels = [outs[0]] + [None] * 7
    for k in (5, 4, 7, 6):
        panels[k] = swap(outs[k], 0, k)
    gram_out, gram = call(add_gram, "add_gram", [VM] * 2, [VM] * 2, [half, total])(gram, gram_in)
    gram_in = swap(gram_out, 2, 0)
    token = after(COST, panels[5])
    *near, gram = call(pack_near, "pack_near", [VM] * 5 + [ANY], [VM] * 4, [both] * 3 + [total])(
        gram, gram_in, outs[1], outs[2], outs[3], token
    )
    for k in (3, 2, 1):
        panels[k] = swap(near[k - 1], 0, k)
    weights, high, low = build_weights(tile_slot, confidence, after(0, panels[7], gram), 8 * BLOCK, True)
    token = after(COST, panels[7], panels[6])
    out, gram = call(last_gram, "last_gram", [VM] * 4 + [ANY] * 2, [VM] * 2, [half, total])(
        gram, panels[3], panels[2], panels[1], token, high
    )
    other = swap(out, 1, 0)
    started = start_solve(weights, high, low, panels, gram)
    return solve_users(weights, started, [gram, other])


def shards(item_factors, send_list, route_list, tile_slot, confidence):
    partial_gram = lax.dot_general(
        item_factors, item_factors, (((0,), (0,)), ((), ())), preferred_element_type=F32
    )
    gram = lax.psum(partial_gram, ("grp", "dev"))
    own_panels = item_factors.reshape(PANELS_DEV, BLOCK, RANK)
    outgoing = own_panels[send_list[0].reshape(-1)]
    group_pool = lax.all_to_all(outgoing, "grp", split_axis=0, concat_axis=0, tiled=True)
    picked = group_pool[route_list[0].reshape(-1)]
    arrived = lax.all_to_all(picked, "dev", split_axis=0, concat_axis=0, tiled=True)
    count = arrived.shape[0]
    weights, high, low = build_weights(tile_slot, confidence, gram, count * BLOCK, False)
    started = start_solve(weights, high, low, [arrived[i] for i in range(count)], gram, BLOCK)
    return solve_users(weights, started, [gram], BLOCK)


def solution(mesh):
    placed = (
        P(("grp", "dev"), None),
        P(("grp", "dev"), None, None),
        P(("grp", "dev"), None, None),
        P(("grp", "dev"), None),
        P(("grp", "dev"), None, None),
    )
    body = shards_4x8 if (mesh.shape["grp"], mesh.shape["dev"]) == (4, 8) else shards
    return jax.shard_map(
        body, mesh=mesh, in_specs=placed, out_specs=P(("grp", "dev"), None), check_vma=False
    )
```

time: 55.1 us -> 41.7 us (0.76)
  waiting for transfers between devices: 14.4 us -> 5.78 us
  local copies, waits for them, and re-layouts: 4.09 us -> 0.93 us
  Pallas kernels: 17.7 us -> 15.6 us
    ppermute x10 -> x12, waiting for transfers between devices: 14.4 us -> 5.78 us  [swap(): return lax.ppermute(array, ('grp', 'dev'), order)]
    unnamed x10, local copies, waits for them, and re-layouts: 4.09 us -> 0.93 us
    pallas_call x8 -> x13, Pallas kernels: 17.7 us -> 15.6 us  [the longest x1 9.4 us: solve_users(): call(functools.partial(solve_kernel, len(gram_parts), chunk), 'solve_user...]
    ppermute x10 -> x12, starting transfers between devices: 18.6 us -> 19.1 us  [swap(): return lax.ppermute(array, ('grp', 'dev'), order)]
  transfers between devices with their start and end apart: 10 -> 12, of which waited for: 4 -> 4; matrix products, arithmetic and copies ran while one was open for 1% -> 0% of each run, Pallas kernels for 9% -> 13%
where the time goes in v2:
time: 41.7 us; the launch traced here: 41.5 us
  starting transfers between devices  19.1 us (46%)
  Pallas kernels  15.6 us (37%)
  waiting for transfers between devices  5.78 us (14%)
  local copies, waits for them, and re-layouts  0.93 us (2%)
    ppermute x12, starting transfers between devices, swap(): return lax.ppermute(array, ('grp', 'dev'), order)  19.1 us
    pallas_call x1, Pallas kernels, solve_users(): call(functools.partial(solve_kernel, len(gram_parts), chunk), 'solve_user...  9.4 us
    ppermute x12, waiting for transfers between devices, swap(): return lax.ppermute(array, ('grp', 'dev'), order)  5.78 us
    pallas_call x1, Pallas kernels, build_weights(): pl.pallas_call(functools.partial(build_kernel, mixed), grid_spec=pltpu.Pr...  3.2 us
    pallas_call x1, Pallas kernels, start_solve(): call(functools.partial(right_kernel, len(panels), chunk), 'right_side', [...  1.85 us
    unnamed x10, local copies, waits for them, and re-layouts  0.93 us
  transfers between devices with their start and end apart: 12, of which 4 were waited for; matrix products, arithmetic and copies ran while one was open for 0% of the time, Pallas kernels for 13%

profile of v2, /device:TPU:1, one launch (start us, length us, event | category | flops | bytes accessed | tf_op | source)
XLA Modules:
  0.0 41.5 jit_solution(351487873132784558)
XLA Ops:
  0.0 0.0 copy-start.3
  0.0 0.0 copy-start.2
  0.0 0.0 copy-start.1
  0.0 0.6 %copy-done.3 = s32[1,8,1]{1,2,0:T(1,128)S(1)} copy-done((s32[1,8,1]{1,2,0:T(1,128)S(1)}, s32[1,8,1]{1,2,0:T(1,128)}, u32[]{:S(2)}) %copy-start.3) | copy-done | bytes 56
  0.7 0.0 copy-done.2
  0.7 0.3 copy-done.1
  0.9 0.8 %first.1 = (bf16[384,256]{1,0:T(8,128)(2,1)S(1)}, bf16[128,256]{1,0:T(8,128)(2,1)S(1)}, bf16[128,256]{1,0:T(8,128)(2,1)S(1)}, f32[128,256]{1,0:T(8,128)S(1)}, s32[8,128]{1,0:T(8,128)S(1)}) custom-call(s32[1,4]{1,0:T(1,128)S(1)} %bitcast.2, s32[1,8]{1,0:T(1,128)S(1)} %bitcast.3, bf16[256,256]{1,0:T(8,128)(2,1)S(1)} %copy-done.1, f32[8,128]{1,0:T(8,128)S(1)} %after.4._), custom_call_target="tpu_custom_call" | custom-call | tf_op jit(solution)/shard_map/first/pallas_call | solution.py:268
  1.7 0.1 collective-permute-start
  1.8 1.4 %collective-permute-done.from_core = bf16[384,256]{1,0:T(8,128)(2,1)S(1)} collective-permute-done((bf16[384,256]{1,0:T(8,128)(2,1)S(1)}, bf16[384,256]{1,0:T(8,128)(2,1)S(1)}, u32[]{:S(2)}, u32[]{:S(2)}) %collective-permute-start) | collective-permute-done | bytes 196640 | tf_op jit(solution)/shard_map/ppermute | solution.py:261
  3.2 2.4 %collective-permute-start.1 = (bf16[256,256]{1,0:T(8,128)(2,1)S(1)}, bf16[256,256]{1,0:T(8,128)(2,1)S(1)}, u32[]{:S(2)}, u32[]{:S(2)}) collective-permute-start(bf16[256,256]{1,0:T(8,128)(2,1)S(1)} %get-tuple-element.41), channel_id=1, source_target_pairs={{0,16},{1,17},{2,18},{3,19},{4,20},{5,21},{6,22},{7,23},{8,24},{9,... | collective-permute-start | bytes 393224 | tf_op jit(solution)/shard_map/ppermute | solution.py:261
  5.7 2.3 %collective-permute-start.3 = (bf16[128,256]{1,0:T(8,128)(2,1)S(1)}, bf16[128,256]{1,0:T(8,128)(2,1)S(1)}, u32[]{:S(2)}, u32[]{:S(2)}) collective-permute-start(bf16[128,256]{1,0:T(8,128)(2,1)S(1)} %get-tuple-element.44), channel_id=1, source_target_pairs={{0,4},{1,5},{2,6},{3,7},{4,0},{5,1},{6,2},{7,3},{8,12},{9,13},{10,... | collective-permute-start | bytes 196616 | tf_op jit(solution)/shard_map/ppermute | solution.py:261
  8.0 1.3 %collective-permute-done.1.from_y = bf16[256,256]{1,0:T(8,128)(2,1)S(1)} collective-permute-done((bf16[256,256]{1,0:T(8,128)(2,1)S(1)}, bf16[256,256]{1,0:T(8,128)(2,1)S(1)}, u32[]{:S(2)}, u32[]{:S(2)}) %collective-permute-start.1) | collective-permute-done | bytes 131104 | tf_op jit(solution)/shard_map/ppermute | solution.py:261
  9.2 0.2 pack_dev.1
  9.5 3.2 %collective-permute-start.5 = (bf16[128,256]{1,0:T(8,128)(2,1)S(1)}, bf16[128,256]{1,0:T(8,128)(2,1)S(1)}, u32[]{:S(2)}, u32[]{:S(2)}) collective-permute-start(bf16[128,256]{1,0:T(8,128)(2,1)S(1)} %get-tuple-element.50), channel_id=1, source_target_pairs={{0,5},{1,4},{2,7},{3,6},{4,1},{5,0},{6,3},{7,2},{8,13},{9,12},{10,... | collective-permute-start | bytes 196616 | tf_op jit(solution)/shard_map/ppermute | solution.py:261
  12.7 0.0 collective-permute-done.3.arrived
  12.7 1.3 %collective-permute-start.4 = (bf16[128,256]{1,0:T(8,128)(2,1)S(1)}, bf16[128,256]{1,0:T(8,128)(2,1)S(1)}, u32[]{:S(2)}, u32[]{:S(2)}) collective-permute-start(bf16[128,256]{1,0:T(8,128)(2,1)S(1)} %get-tuple-element.46), channel_id=1, source_target_pairs={{0,16},{1,17},{2,18},{3,19},{4,20},{5,21},{6,22},{7,23},{8,24},{9,... | collective-permute-start | bytes 196616 | tf_op jit(solution)/shard_map/ppermute | solution.py:261
  14.0 2.1 %collective-permute-start.2 = (bf16[128,256]{1,0:T(8,128)(2,1)S(1)}, bf16[128,256]{1,0:T(8,128)(2,1)S(1)}, u32[]{:S(2)}, u32[]{:S(2)}) collective-permute-start(bf16[128,256]{1,0:T(8,128)(2,1)S(1)} %get-tuple-element.42), channel_id=1, source_target_pairs={{0,7},{1,6},{2,5},{3,4},{4,3},{5,2},{6,1},{7,0},{8,15},{9,14},{10,... | collective-permute-start | bytes 196616 | tf_op jit(solution)/shard_map/ppermute | solution.py:261
  16.1 0.0 copy-start
  16.1 0.0 copy-start.4
  16.1 1.1 %collective-permute-start.10 = (bf16[128,256]{1,0:T(8,128)(2,1)S(1)}, bf16[128,256]{1,0:T(8,128)(2,1)S(1)}, u32[]{:S(2)}, u32[]{:S(2)}) collective-permute-start(bf16[128,256]{1,0:T(8,128)(2,1)S(1)} %get-tuple-element.60), channel_id=1, source_target_pairs={{0,6},{1,7},{2,4},{3,5},{4,2},{5,3},{6,0},{7,1},{8,14},{9,15},{10,... | collective-permute-start | bytes 196616 | tf_op jit(solution)/shard_map/ppermute | solution.py:261
  17.3 0.0 collective-permute-done.5.refs_0_.refs_5_
  17.3 0.0 collective-permute-done.4.arrived
  17.3 1.3 %collective-permute-start.6 = (bf16[256,256]{1,0:T(8,128)(2,1)S(1)}, bf16[256,256]{1,0:T(8,128)(2,1)S(1)}, u32[]{:S(2)}, u32[]{:S(2)}) collective-permute-start(bf16[256,256]{1,0:T(8,128)(2,1)S(1)} %get-tuple-element.56), channel_id=1, source_target_pairs={{0,1},{1,0},{2,3},{3,2},{4,5},{5,4},{6,7},{7,6},{8,9},{9,8},{10,11... | collective-permute-start | bytes 393224 | tf_op jit(solution)/shard_map/ppermute | solution.py:261
  18.6 0.0 collective-permute-start.7
  18.6 1.4 %collective-permute-start.8 = (bf16[256,256]{1,0:T(8,128)(2,1)S(1)}, bf16[256,256]{1,0:T(8,128)(2,1)S(1)}, u32[]{:S(2)}, u32[]{:S(2)}) collective-permute-start(bf16[256,256]{1,0:T(8,128)(2,1)S(1)} %get-tuple-element.58), channel_id=1, source_target_pairs={{0,3},{1,2},{2,1},{3,0},{4,7},{5,6},{6,5},{7,4},{8,11},{9,10},{10,... | collective-permute-start | bytes 393224 | tf_op jit(solution)/shard_map/ppermute | solution.py:261
  20.0 0.0 collective-permute-done.2.refs_0_.refs_7_
  20.0 0.9 %collective-permute-start.9 = (bf16[128,256]{1,0:T(8,128)(2,1)S(1)}, bf16[128,256]{1,0:T(8,128)(2,1)S(1)}, u32[]{:S(2)}, u32[]{:S(2)}) collective-permute-start(bf16[128,256]{1,0:T(8,128)(2,1)S(1)} %get-tuple-element.59), channel_id=1, source_target_pairs={{0,4},{1,5},{2,6},{3,7},{4,0},{5,1},{6,2},{7,3},{8,12},{9,13},{10,... | collective-permute-start | bytes 196616 | tf_op jit(solution)/shard_map/ppermute | solution.py:261
  21.0 0.0 copy-done
  21.0 0.0 copy-done.4
  21.0 3.2 %build_weights.1 = (f32[512,1024]{1,0:T(8,128)S(1)}, bf16[512,1024]{1,0:T(8,128)(2,1)S(1)}, bf16[512,1024]{1,0:T(8,128)(2,1)S(1)}) custom-call(s32[1,64]{1,0:T(1,128)S(1)} %copy-done.4, bf16[64,128,128]{2,1,0:T(8,128)(2,1)S(1)} %copy-done, f32[8,128]{1,0:T(8,128)S(1)} %after.6._), custom_call_target="tpu_custom_call" | custom-call | tf_op jit(solution)/shard_map/build_weights/pallas_call | solution.py:152
  24.2 0.0 collective-permute-done.10.refs_1_.refs_6_
  24.2 0.0 collective-permute-done.6.refs_2_.refs_1_
  24.2 1.0 %collective-permute-done.7.refs_1_.refs_2_ = bf16[256,256]{1,0:T(8,128)(2,1)S(1)} collective-permute-done((bf16[256,256]{1,0:T(8,128)(2,1)S(1)}, bf16[256,256]{1,0:T(8,128)(2,1)S(1)}, u32[]{:S(2)}, u32[]{:S(2)}) %collective-permute-start.7) | collective-permute-done | bytes 131104 | tf_op jit(solution)/shard_map/ppermute | solution.py:261
  25.3 2.1 %collective-permute-done.8.refs_0_.refs_3_ = bf16[256,256]{1,0:T(8,128)(2,1)S(1)} collective-permute-done((bf16[256,256]{1,0:T(8,128)(2,1)S(1)}, bf16[256,256]{1,0:T(8,128)(2,1)S(1)}, u32[]{:S(2)}, u32[]{:S(2)}) %collective-permute-start.8) | collective-permute-done | bytes 131104 | tf_op jit(solution)/shard_map/ppermute | solution.py:261
  27.4 2.9 %collective-permute-start.11 = (bf16[128,256]{1,0:T(8,128)(2,1)S(1)}, bf16[128,256]{1,0:T(8,128)(2,1)S(1)}, u32[]{:S(2)}, u32[]{:S(2)}) collective-permute-start(bf16[128,256]{1,0:T(8,128)(2,1)S(1)} %get-tuple-element.66), channel_id=1, source_target_pairs={{0,8},{1,9},{2,10},{3,11},{4,12},{5,13},{6,14},{7,15},{8,0},{9,1},... | collective-permute-start | bytes 196616 | tf_op jit(solution)/shard_map/ppermute | solution.py:261
  30.3 0.0 collective-permute-done.9.refs_4_
  30.3 1.9 %right_side.1 = (bf16[1024,256]{1,0:T(8,128)(2,1)S(1)}, bf16[256,1024]{1,0:T(8,128)(2,1)S(1)}, f32[512,256]{1,0:T(8,128)S(1)}, f32[512,256]{1,0:T(8,128)S(1)}) custom-call(f32[512,1024]{1,0:T(8,128)S(1)} %get-tuple-element.52.weights, bf16[512,1024]{1,0:T(8,128)(2,1)S(1)} %get-tuple-element.53.refs_4_.high, bf16[512,1024]{1,0:T(8,128)(2,1)S(1)} %get-tuple-element.54.low, ...), custom_call_target="tpu_custom_call" | custom-call | tf_op jit(solution)/shard_map/right_side/pallas_call | solution.py:241
  32.1 0.0 collective-permute-done.11.refs_1_
  32.1 9.4 %solve_users.1 = f32[512,256]{1,0:T(8,128)} custom-call(f32[512,1024]{1,0:T(8,128)S(1)} %get-tuple-element.52.weights, bf16[1024,256]{1,0:T(8,128)(2,1)S(1)} %get-tuple-element.62.items, bf16[256,1024]{1,0:T(8,128)(2,1)S(1)} %get-tuple-element.63.items_t, f32[512,256]{1,0:T(8,128)S(1)} %get-tuple-element.64.right_side, ...), custom_call_target="tpu_custom_call" | custom-call | tf_op jit(solution)/shard_map/solve_users/pallas_call | solution.py:250
  (8 shorter events, 0.1 us)
Async XLA Ops:
  0.0 0.7 %copy-start.3 = (s32[1,8,1]{1,2,0:T(1,128)S(1)}, s32[1,8,1]{1,2,0:T(1,128)}, u32[]{:S(2)}) copy-start(s32[1,8,1]{1,2,0:T(1,128)} %param.7) | copy-start | bytes 100
  0.0 0.7 %copy-start.2 = (s32[1,4,1]{1,2,0:T(1,128)S(1)}, s32[1,4,1]{1,2,0:T(1,128)}, u32[]{:S(2)}) copy-start(s32[1,4,1]{1,2,0:T(1,128)} %param.6) | copy-start | bytes 52
  0.0 0.9 %copy-start.1 = (bf16[256,256]{1,0:T(8,128)(2,1)S(1)}, bf16[256,256]{1,0:T(8,128)(2,1)}, u32[]{:S(2)}) copy-start(bf16[256,256]{1,0:T(8,128)(2,1)} %items_hbm.1) | copy-start | bytes 393220
  1.7 1.5 %collective-permute-start = (bf16[384,256]{1,0:T(8,128)(2,1)S(1)}, bf16[384,256]{1,0:T(8,128)(2,1)S(1)}, u32[]{:S(2)}, u32[]{:S(2)}) collective-permute-start(bf16[384,256]{1,0:T(8,128)(2,1)S(1)} %get-tuple-element.38), channel_id=1, source_target_pairs={{0,8},{1,9},{2,10},{3,11},{4,12},{5,13},{6,14},{7,15},{8,0},{9,1},... | collective-permute-start | bytes 589832 | tf_op jit(solution)/shard_map/ppermute | solution.py:261
  3.2 6.0 %collective-permute-start.1 = (bf16[256,256]{1,0:T(8,128)(2,1)S(1)}, bf16[256,256]{1,0:T(8,128)(2,1)S(1)}, u32[]{:S(2)}, u32[]{:S(2)}) collective-permute-start(bf16[256,256]{1,0:T(8,128)(2,1)S(1)} %get-tuple-element.41), channel_id=1, source_target_pairs={{0,16},{1,17},{2,18},{3,19},{4,20},{5,21},{6,22},{7,23},{8,24},{9,... | collective-permute-start | bytes 393224 | tf_op jit(solution)/shard_map/ppermute | solution.py:261
  5.7 7.0 %collective-permute-start.3 = (bf16[128,256]{1,0:T(8,128)(2,1)S(1)}, bf16[128,256]{1,0:T(8,128)(2,1)S(1)}, u32[]{:S(2)}, u32[]{:S(2)}) collective-permute-start(bf16[128,256]{1,0:T(8,128)(2,1)S(1)} %get-tuple-element.44), channel_id=1, source_target_pairs={{0,4},{1,5},{2,6},{3,7},{4,0},{5,1},{6,2},{7,3},{8,12},{9,13},{10,... | collective-permute-start | bytes 196616 | tf_op jit(solution)/shard_map/ppermute | solution.py:261
  9.5 7.8 %collective-permute-start.5 = (bf16[128,256]{1,0:T(8,128)(2,1)S(1)}, bf16[128,256]{1,0:T(8,128)(2,1)S(1)}, u32[]{:S(2)}, u32[]{:S(2)}) collective-permute-start(bf16[128,256]{1,0:T(8,128)(2,1)S(1)} %get-tuple-element.50), channel_id=1, source_target_pairs={{0,5},{1,4},{2,7},{3,6},{4,1},{5,0},{6,3},{7,2},{8,13},{9,12},{10,... | collective-permute-start | bytes 196616 | tf_op jit(solution)/shard_map/ppermute | solution.py:261
  12.7 4.6 %collective-permute-start.4 = (bf16[128,256]{1,0:T(8,128)(2,1)S(1)}, bf16[128,256]{1,0:T(8,128)(2,1)S(1)}, u32[]{:S(2)}, u32[]{:S(2)}) collective-permute-start(bf16[128,256]{1,0:T(8,128)(2,1)S(1)} %get-tuple-element.46), channel_id=1, source_target_pairs={{0,16},{1,17},{2,18},{3,19},{4,20},{5,21},{6,22},{7,23},{8,24},{9,... | collective-permute-start | bytes 196616 | tf_op jit(solution)/shard_map/ppermute | solution.py:261
  14.0 6.0 %collective-permute-start.2 = (bf16[128,256]{1,0:T(8,128)(2,1)S(1)}, bf16[128,256]{1,0:T(8,128)(2,1)S(1)}, u32[]{:S(2)}, u32[]{:S(2)}) collective-permute-start(bf16[128,256]{1,0:T(8,128)(2,1)S(1)} %get-tuple-element.42), channel_id=1, source_target_pairs={{0,7},{1,6},{2,5},{3,4},{4,3},{5,2},{6,1},{7,0},{8,15},{9,14},{10,... | collective-permute-start | bytes 196616 | tf_op jit(solution)/shard_map/ppermute | solution.py:261
  16.1 4.9 %copy-start = (bf16[64,128,128]{2,1,0:T(8,128)(2,1)S(1)}, bf16[64,128,128]{2,1,0:T(8,128)(2,1)}, u32[]{:S(2)}) copy-start(bf16[64,128,128]{2,1,0:T(8,128)(2,1)} %tiles.1) | copy-start | bytes 6291460
  16.1 4.9 %copy-start.4 = (s32[1,64]{1,0:T(1,128)S(1)}, s32[1,64]{1,0:T(1,128)}, u32[]{:S(2)}) copy-start(s32[1,64]{1,0:T(1,128)} %slots.1) | copy-start | bytes 772
  16.1 8.1 %collective-permute-start.10 = (bf16[128,256]{1,0:T(8,128)(2,1)S(1)}, bf16[128,256]{1,0:T(8,128)(2,1)S(1)}, u32[]{:S(2)}, u32[]{:S(2)}) collective-permute-start(bf16[128,256]{1,0:T(8,128)(2,1)S(1)} %get-tuple-element.60), channel_id=1, source_target_pairs={{0,6},{1,7},{2,4},{3,5},{4,2},{5,3},{6,0},{7,1},{8,14},{9,15},{10,... | collective-permute-start | bytes 196616 | tf_op jit(solution)/shard_map/ppermute | solution.py:261
  17.3 6.9 %collective-permute-start.6 = (bf16[256,256]{1,0:T(8,128)(2,1)S(1)}, bf16[256,256]{1,0:T(8,128)(2,1)S(1)}, u32[]{:S(2)}, u32[]{:S(2)}) collective-permute-start(bf16[256,256]{1,0:T(8,128)(2,1)S(1)} %get-tuple-element.56), channel_id=1, source_target_pairs={{0,1},{1,0},{2,3},{3,2},{4,5},{5,4},{6,7},{7,6},{8,9},{9,8},{10,11... | collective-permute-start | bytes 393224 | tf_op jit(solution)/shard_map/ppermute | solution.py:261
  18.6 6.7 %collective-permute-start.7 = (bf16[256,256]{1,0:T(8,128)(2,1)S(1)}, bf16[256,256]{1,0:T(8,128)(2,1)S(1)}, u32[]{:S(2)}, u32[]{:S(2)}) collective-permute-start(bf16[256,256]{1,0:T(8,128)(2,1)S(1)} %get-tuple-element.57), channel_id=1, source_target_pairs={{0,2},{1,3},{2,0},{3,1},{4,6},{5,7},{6,4},{7,5},{8,10},{9,11},{10,... | collective-permute-start | bytes 393224 | tf_op jit(solution)/shard_map/ppermute | solution.py:261
  18.6 8.7 %collective-permute-start.8 = (bf16[256,256]{1,0:T(8,128)(2,1)S(1)}, bf16[256,256]{1,0:T(8,128)(2,1)S(1)}, u32[]{:S(2)}, u32[]{:S(2)}) collective-permute-start(bf16[256,256]{1,0:T(8,128)(2,1)S(1)} %get-tuple-element.58), channel_id=1, source_target_pairs={{0,3},{1,2},{2,1},{3,0},{4,7},{5,6},{6,5},{7,4},{8,11},{9,10},{10,... | collective-permute-start | bytes 393224 | tf_op jit(solution)/shard_map/ppermute | solution.py:261
  20.0 10.2 %collective-permute-start.9 = (bf16[128,256]{1,0:T(8,128)(2,1)S(1)}, bf16[128,256]{1,0:T(8,128)(2,1)S(1)}, u32[]{:S(2)}, u32[]{:S(2)}) collective-permute-start(bf16[128,256]{1,0:T(8,128)(2,1)S(1)} %get-tuple-element.59), channel_id=1, source_target_pairs={{0,4},{1,5},{2,6},{3,7},{4,0},{5,1},{6,2},{7,3},{8,12},{9,13},{10,... | collective-permute-start | bytes 196616 | tf_op jit(solution)/shard_map/ppermute | solution.py:261
  27.4 4.7 %collective-permute-start.11 = (bf16[128,256]{1,0:T(8,128)(2,1)S(1)}, bf16[128,256]{1,0:T(8,128)(2,1)S(1)}, u32[]{:S(2)}, u32[]{:S(2)}) collective-permute-start(bf16[128,256]{1,0:T(8,128)(2,1)S(1)} %get-tuple-element.66), channel_id=1, source_target_pairs={{0,8},{1,9},{2,10},{3,11},{4,12},{5,13},{6,14},{7,15},{8,0},{9,1},... | collective-permute-start | bytes 196616 | tf_op jit(solution)/shard_map/ppermute | solution.py:261

commit v3 on v2

v3 whole, which is shorter than its diff:
```python
import functools

import jax
import jax.numpy as jnp
from jax import lax
from jax.experimental import pallas as pl
from jax.experimental.pallas import tpu as pltpu
from jax.sharding import PartitionSpec as P

RANK = 256
BLOCK = 128
PANELS_DEV = 2
USER_BLOCKS = 4
TILES_PER = 16
ITERS = 8
BF16 = jnp.bfloat16
F32 = jnp.float32

ridge = 0.1
COST = 1000000000
LEAD = 3000000000

VM = pl.BlockSpec(memory_space=pltpu.VMEM)
ANY = pl.BlockSpec(memory_space=pl.ANY)
SM = pl.BlockSpec(memory_space=pltpu.SMEM)


def params():
    return pltpu.CompilerParams(vmem_limit_bytes=40 * 2**20)


def shape(rows, dtype=BF16):
    return jax.ShapeDtypeStruct((rows, RANK), dtype)


def call(body, name, in_specs, out_specs, out_shape, scratch=(), cost=0):
    return pl.pallas_call(
        body,
        in_specs=in_specs,
        out_specs=out_specs,
        out_shape=out_shape,
        scratch_shapes=list(scratch),
        compiler_params=params(),
        cost_estimate=None if cost is None else pl.CostEstimate(flops=cost, transcendentals=0, bytes_accessed=0),
        name=name,
    )


def own_panel(items, index):
    return items[pl.ds(pl.multiple_of(index * BLOCK, BLOCK), BLOCK), :]


def entry(row, index):
    place = lax.broadcasted_iota(jnp.int32, row.shape, 1)
    return jnp.max(jnp.where(place == index, row, 0))


def first_kernel(send, route, items, _, out, panel_y, panel_own, gram_own, picks, gram):
    group = lax.axis_index("grp")
    member = lax.axis_index("dev")
    core = lax.rem(group, 2)
    panels, routes = send[...], route[...]
    out[0:BLOCK, :] = own_panel(items, entry(panels, group ^ 1))
    out[BLOCK : 2 * BLOCK, :] = own_panel(items, entry(panels, group ^ 3))
    panel_y[...] = own_panel(items, entry(panels, group ^ 2))
    panel_own[...] = own_panel(items, entry(panels, group))
    rows = items[...]
    gram[...] = lax.dot_general(rows, rows, (((0,), (0,)), ((), ())), preferred_element_type=F32)
    out[2 * BLOCK : 3 * BLOCK, :] = own_panel(gram, 1 - core).astype(BF16)
    gram_own[...] = own_panel(gram, core)
    for step in range(8):
        picks[step : step + 1, :] = jnp.full((1, BLOCK), entry(routes, member ^ step) ^ group, jnp.int32)


def pack_y(panel_y, gram_own, from_core, out, gram_out, gram_sum):
    out[0:BLOCK, :] = panel_y[...]
    out[BLOCK : 2 * BLOCK, :] = from_core[BLOCK : 2 * BLOCK, :]
    total = gram_own[...] + from_core[2 * BLOCK : 3 * BLOCK, :].astype(F32)
    gram_out[...] = total.astype(BF16)
    gram_sum[...] = total


def pack_dev(picks, panel_own, from_core, from_y, *refs):
    outs, pool = refs[:8], refs[8]
    pool[0] = panel_own[...]
    pool[1] = from_core[0:BLOCK, :]
    pool[2] = from_y[0:BLOCK, :]
    pool[3] = from_y[BLOCK : 2 * BLOCK, :]
    for step in range(8):
        outs[step][...] = pool[jnp.max(picks[step : step + 1, :])]


def add_gram(gram_own, arrived, out, gram_sum):
    total = gram_own[...] + arrived[...].astype(F32)
    out[...] = total.astype(BF16)
    gram_sum[...] = total


def pack_near(gram_own, arrived, *refs):
    panels, outs, gram_sum = refs[:3], refs[4:7], refs[7]
    total = gram_own[...] + arrived[...].astype(F32)
    gram_sum[...] = total
    for panel, out in zip(panels, outs):
        out[0:BLOCK, :] = panel[...]
        out[BLOCK : 2 * BLOCK, :] = total.astype(BF16)


def last_gram(gram_own, *refs):
    out, gram_sum = refs[-2:]
    total = gram_own[...]
    for part in refs[:3]:
        total += part[BLOCK : 2 * BLOCK, :].astype(F32)
    out[...] = total.astype(BF16)
    gram_sum[...] = total


def touch(*refs):
    refs[-1][...] = jnp.zeros_like(refs[-1])


def after(cost, *arrays):
    return call(
        touch, "after", [ANY] * len(arrays), VM, jax.ShapeDtypeStruct((8, BLOCK), F32), cost=cost
    )(*arrays)


def build_kernel(mixed, slots, tiles, _, *refs):
    weights, high, low, target_sum = (refs[i : i + USER_BLOCKS] for i in range(0, 4 * USER_BLOCKS, USER_BLOCKS))
    turn = lax.axis_index("dev") if mixed else 0
    for ref in weights + target_sum:
        ref[...] = jnp.zeros_like(ref)
    for tile in range(TILES_PER):
        for block in range(USER_BLOCKS):
            index = block * TILES_PER + tile
            first = (slots[0, index] ^ turn) * BLOCK
            columns = pl.ds(pl.multiple_of(first, BLOCK), BLOCK)
            confidence = tiles[index].astype(F32)
            target = jnp.where(confidence > 0, 1.0 + confidence, 0.0).astype(BF16)
            weights[block][:, columns] += confidence
            target_sum[block][:, columns] += target.astype(F32)
    for block in range(USER_BLOCKS):
        total = target_sum[block][...]
        top = total.astype(BF16)
        high[block][...] = top
        low[block][...] = (total - top.astype(F32)).astype(BF16)


def build_weights(slots, confidence, after, width, mixed):
    wide = jax.ShapeDtypeStruct((BLOCK, width), F32)
    narrow = jax.ShapeDtypeStruct((BLOCK, width), BF16)
    return call(
        functools.partial(build_kernel, mixed), "build_weights", [SM, VM, ANY],
        [VM] * 3 * USER_BLOCKS, [wide] * USER_BLOCKS + [narrow] * 2 * USER_BLOCKS,
        [pltpu.VMEM((BLOCK, width), F32)] * USER_BLOCKS, cost=None,
    )(slots, confidence, after)


def right_kernel(count, *refs):
    weights, high, low = (refs[i : i + USER_BLOCKS] for i in range(0, 3 * USER_BLOCKS, USER_BLOCKS))
    panels = refs[3 * USER_BLOCKS : 3 * USER_BLOCKS + count]
    items, items_t, right_side, image = refs[-4:]
    dot = functools.partial(jnp.dot, preferred_element_type=F32)
    for i in range(count):
        rows = slice(i * BLOCK, (i + 1) * BLOCK)
        panel = panels[i][0:BLOCK, :]
        items[rows, :] = panel
        items_t[:, rows] = panel.T
    for block in range(USER_BLOCKS):
        users = slice(block * BLOCK, (block + 1) * BLOCK)
        target = dot(high[block][...], items[...]) + dot(low[block][...], items[...])
        right_side[users, :] = target
        scores = dot(target.astype(BF16), items_t[...])
        image[users, :] = dot((weights[block][...] * scores).astype(BF16), items[...])


def start_solve(built, panels, after):
    width = built[0].shape[1]
    users = USER_BLOCKS * BLOCK
    return call(
        functools.partial(right_kernel, len(panels)), "right_side",
        [VM] * (len(built) + len(panels)) + [ANY], [VM] * 4,
        [shape(width), jax.ShapeDtypeStruct((RANK, width), BF16), shape(users, F32), shape(users, F32)],
        cost=None,
    )(*built, *panels, after)


def solve_kernel(halves, unroll, *refs):
    weights, refs = refs[:USER_BLOCKS], refs[USER_BLOCKS:]
    items, items_t, right_side, first_image = refs[:4]
    gram_parts, result, gram, sems = refs[4 : 4 + halves], refs[4 + halves], refs[5 + halves], refs[6 + halves]
    state = refs[7 + halves :]
    residuals, directions, solved = (state[i : i + USER_BLOCKS] for i in range(0, 3 * USER_BLOCKS, USER_BLOCKS))
    dot = functools.partial(jnp.dot, preferred_element_type=F32)
    if halves == 1:
        gram[...] = gram_parts[0][...].astype(BF16)
    else:
        core = lax.rem(lax.axis_index("grp"), 2)
        for place, part in zip((core, 1 - core), gram_parts):
            gram[pl.ds(pl.multiple_of(place * BLOCK, BLOCK), BLOCK), :] = part[...].astype(BF16)

    def rows(block):
        return slice(block * BLOCK, (block + 1) * BLOCK)

    def image_of(block, direction, scores):
        weighted = (weights[block][...] * scores).astype(BF16)
        return dot(weighted, items[...]) + dot(direction.astype(BF16), gram[...])

    def advance(block, norm_now, direction, residual, image, last=False):
        image = image + ridge * direction
        alpha = norm_now / jnp.sum(direction * image, axis=1, keepdims=True)
        solved[block][...] += alpha * direction
        if last:
            return norm_now
        residual = residual - alpha * image
        residuals[block][...] = residual
        norm_next = jnp.sum(residual * residual, axis=1, keepdims=True)
        directions[block][...] = residual + (norm_next / norm_now) * direction
        return norm_next

    norms = []
    for block in range(USER_BLOCKS):
        start = right_side[rows(block), :]
        solved[block][...] = jnp.zeros_like(start)
        norm = jnp.sum(start * start, axis=1, keepdims=True)
        image = first_image[rows(block), :] + dot(start.astype(BF16), gram[...])
        norms.append(advance(block, norm, start, start, image))

    copies = [
        pltpu.make_async_copy(solved[block], result.at[pl.ds(block * BLOCK, BLOCK), :], sems.at[block])
        for block in range(USER_BLOCKS)
    ]

    def step(_, norms, last=False):
        after = []
        for first in range(0, USER_BLOCKS, 2):
            pair = (first, first + 1)
            now = [directions[block][...] for block in pair]
            scores = [dot(direction.astype(BF16), items_t[...]) for direction in now]
            images = [image_of(*each) for each in zip(pair, now, scores)]
            for block, direction, image in zip(pair, now, images):
                after.append(advance(block, norms[block], direction, residuals[block][...], image, last))
                if last:
                    copies[block].start()
        return tuple(after)

    norms = lax.fori_loop(1, ITERS - 1, step, tuple(norms), unroll=unroll)
    step(None, norms, True)
    for copy in copies:
        copy.wait()


def solve_users(weights, started, gram_parts, unroll=True):
    users = USER_BLOCKS * BLOCK
    return call(
        functools.partial(solve_kernel, len(gram_parts), unroll), "solve_users",
        [VM] * (USER_BLOCKS + 4 + len(gram_parts)), ANY, shape(users, F32),
        [pltpu.VMEM((RANK, RANK), BF16), pltpu.SemaphoreType.DMA((USER_BLOCKS,))]
        + [pltpu.VMEM((BLOCK, RANK), F32)] * 3 * USER_BLOCKS,
        cost=None,
    )(*weights, *started, *gram_parts)


def swap(array, group_bits, member_bits):
    order = [
        (g * 8 + d, (g ^ group_bits) * 8 + (d ^ member_bits)) for g in range(4) for d in range(8)
    ]
    return lax.ppermute(array, ("grp", "dev"), order)


def shards_4x8(item_factors, send_list, route_list, tile_slot, confidence):
    send_list, route_list = send_list.reshape(1, -1), route_list.reshape(1, -1)
    half, both = shape(BLOCK), shape(2 * BLOCK)
    total = shape(BLOCK, F32)
    out, panel_y, panel_own, gram, picks = call(
        first_kernel, "first", [VM] * 3 + [ANY], [VM] * 5,
        [shape(3 * BLOCK), half, half, total, jax.ShapeDtypeStruct((8, BLOCK), jnp.int32)],
        [pltpu.VMEM((RANK, RANK), F32)],
    )(send_list, route_list, item_factors, after(LEAD))
    from_core = swap(out, 1, 0)
    out, gram_out, gram = call(pack_y, "pack_y", [VM] * 3, [VM] * 3, [both, half, total])(
        panel_y, gram, from_core
    )
    from_y = swap(out, 2, 0)
    gram_in = swap(gram_out, 0, 4)
    outs = call(
        pack_dev, "pack_dev", [VM] * 4, [VM] * 8, [half] * 8, [pltpu.VMEM((4, BLOCK, RANK), BF16)]
    )(picks, panel_own, from_core, from_y)
    panels = [outs[0]] + [None] * 7
    for k in (4, 6, 5, 7):
        panels[k] = swap(outs[k], 0, k)
    gram_out, gram = call(add_gram, "add_gram", [VM] * 2, [VM] * 2, [half, total])(gram, gram_in)
    gram_in = swap(gram_out, 2, 0)
    token = after(COST, panels[4])
    *near, gram = call(pack_near, "pack_near", [VM] * 5 + [ANY], [VM] * 4, [both] * 3 + [total])(
        gram, gram_in, outs[1], outs[2], outs[3], token
    )
    for k in (3, 2, 1):
        panels[k] = swap(near[k - 1], 0, k)
    built = build_weights(tile_slot, confidence, after(0, panels[6], gram), 8 * BLOCK, True)
    token = after(COST, panels[5], panels[7])
    out, gram = call(last_gram, "last_gram", [VM] * 4 + [ANY] * 2, [VM] * 2, [half, total])(
        gram, panels[3], panels[2], panels[1], token, built[-1]
    )
    other = swap(out, 1, 0)
    started = start_solve(built, panels, gram)
    return solve_users(built[:USER_BLOCKS], started, [gram, other])


def shards(item_factors, send_list, route_list, tile_slot, confidence):
    partial_gram = lax.dot_general(
        item_factors, item_factors, (((0,), (0,)), ((), ())), preferred_element_type=F32
    )
    gram = lax.psum(partial_gram, ("grp", "dev"))
    own_panels = item_factors.reshape(PANELS_DEV, BLOCK, RANK)
    outgoing = own_panels[send_list[0].reshape(-1)]
    group_pool = lax.all_to_all(outgoing, "grp", split_axis=0, concat_axis=0, tiled=True)
    picked = group_pool[route_list[0].reshape(-1)]
    arrived = lax.all_to_all(picked, "dev", split_axis=0, concat_axis=0, tiled=True)
    count = arrived.shape[0]
    built = build_weights(tile_slot, confidence, gram, count * BLOCK, False)
    started = start_solve(built, [arrived[i] for i in range(count)], gram)
    return solve_users(built[:USER_BLOCKS], started, [gram], 1)


def solution(mesh):
    placed = (
        P(("grp", "dev"), None),
        P(("grp", "dev"), None, None),
        P(("grp", "dev"), None, None),
        P(("grp", "dev"), None),
        P(("grp", "dev"), None, None),
    )
    body = shards_4x8 if (mesh.shape["grp"], mesh.shape["dev"]) == (4, 8) else shards
    return jax.shard_map(
        body, mesh=mesh, in_specs=placed, out_specs=P(("grp", "dev"), None), check_vma=False
    )
```

time: 41.7 us -> 37.8 us (0.906)
  Pallas kernels: 15.6 us -> 12 us
  starting transfers between devices: 19.1 us -> 17.8 us
  waiting for transfers between devices: 5.78 us -> 6.86 us
    pallas_call x4, Pallas kernels: 15.2 us -> 11.7 us  [the longest x1 6.46 us: solve_users(): call(functools.partial(solve_kernel, len(gram_parts), unroll), 'solve_use...]
    ppermute x12, starting transfers between devices: 19.1 us -> 17.8 us  [swap(): return lax.ppermute(array, ('grp', 'dev'), order)]
    ppermute x12, waiting for transfers between devices: 5.78 us -> 6.86 us  [swap(): return lax.ppermute(array, ('grp', 'dev'), order)]
  transfers between devices with their start and end apart: 12 -> 12, of which waited for: 4 -> 4; matrix products, arithmetic and copies ran while one was open for 0% -> 0% of each run, Pallas kernels for 13% -> 14%
where the time goes in v3:
time: 37.8 us; the launch traced here: 37.7 us
  starting transfers between devices  17.8 us (47%)
  Pallas kernels  12 us (32%)
  waiting for transfers between devices  6.86 us (18%)
  local copies, waits for them, and re-layouts  0.93 us (2%)
    ppermute x12, starting transfers between devices, swap(): return lax.ppermute(array, ('grp', 'dev'), order)  17.8 us
    ppermute x12, waiting for transfers between devices, swap(): return lax.ppermute(array, ('grp', 'dev'), order)  6.86 us
    pallas_call x1, Pallas kernels, solve_users(): call(functools.partial(solve_kernel, len(gram_parts), unroll), 'solve_use...  6.46 us
    pallas_call x1, Pallas kernels, build_weights(): call(functools.partial(build_kernel, mixed), 'build_weights', [SM, VM, AN...  3.25 us
    pallas_call x1, Pallas kernels, start_solve(): call(functools.partial(right_kernel, len(panels)), 'right_side', [VM] * (...  1.63 us
    unnamed x10, local copies, waits for them, and re-layouts  0.93 us
  transfers between devices with their start and end apart: 12, of which 4 were waited for; matrix products, arithmetic and copies ran while one was open for 0% of the time, Pallas kernels for 14%

profile of v3, /device:TPU:1, one launch (start us, length us, event | category | flops | bytes accessed | tf_op | source)
XLA Modules:
  0.0 37.7 jit_solution(12287442486513545677)
XLA Ops:
  0.0 0.0 copy-start.3
  0.0 0.0 copy-start.2
  0.0 0.0 copy-start.1
  0.0 0.6 %copy-done.3 = s32[1,8,1]{1,2,0:T(1,128)S(1)} copy-done((s32[1,8,1]{1,2,0:T(1,128)S(1)}, s32[1,8,1]{1,2,0:T(1,128)}, u32[]{:S(2)}) %copy-start.3) | copy-done | bytes 56
  0.7 0.0 copy-done.2
  0.7 0.3 copy-done.1
  0.9 0.3 first.1
  1.3 0.1 collective-permute-start
  1.4 1.4 %collective-permute-done.from_core = bf16[384,256]{1,0:T(8,128)(2,1)S(1)} collective-permute-done((bf16[384,256]{1,0:T(8,128)(2,1)S(1)}, bf16[384,256]{1,0:T(8,128)(2,1)S(1)}, u32[]{:S(2)}, u32[]{:S(2)}) %collective-permute-start) | collective-permute-done | bytes 196640 | tf_op jit(solution)/shard_map/ppermute | solution.py:267
  2.8 2.4 %collective-permute-start.1 = (bf16[256,256]{1,0:T(8,128)(2,1)S(1)}, bf16[256,256]{1,0:T(8,128)(2,1)S(1)}, u32[]{:S(2)}, u32[]{:S(2)}) collective-permute-start(bf16[256,256]{1,0:T(8,128)(2,1)S(1)} %get-tuple-element.50), channel_id=1, source_target_pairs={{0,16},{1,17},{2,18},{3,19},{4,20},{5,21},{6,22},{7,23},{8,24},{9,... | collective-permute-start | bytes 393224 | tf_op jit(solution)/shard_map/ppermute | solution.py:267
  5.3 2.3 %collective-permute-start.3 = (bf16[128,256]{1,0:T(8,128)(2,1)S(1)}, bf16[128,256]{1,0:T(8,128)(2,1)S(1)}, u32[]{:S(2)}, u32[]{:S(2)}) collective-permute-start(bf16[128,256]{1,0:T(8,128)(2,1)S(1)} %get-tuple-element.53), channel_id=1, source_target_pairs={{0,4},{1,5},{2,6},{3,7},{4,0},{5,1},{6,2},{7,3},{8,12},{9,13},{10,... | collective-permute-start | bytes 196616 | tf_op jit(solution)/shard_map/ppermute | solution.py:267
  7.6 1.3 %collective-permute-done.1.from_y = bf16[256,256]{1,0:T(8,128)(2,1)S(1)} collective-permute-done((bf16[256,256]{1,0:T(8,128)(2,1)S(1)}, bf16[256,256]{1,0:T(8,128)(2,1)S(1)}, u32[]{:S(2)}, u32[]{:S(2)}) %collective-permute-start.1) | collective-permute-done | bytes 131104 | tf_op jit(solution)/shard_map/ppermute | solution.py:267
  8.8 0.2 pack_dev.1
  9.1 2.3 %collective-permute-start.5 = (bf16[128,256]{1,0:T(8,128)(2,1)S(1)}, bf16[128,256]{1,0:T(8,128)(2,1)S(1)}, u32[]{:S(2)}, u32[]{:S(2)}) collective-permute-start(bf16[128,256]{1,0:T(8,128)(2,1)S(1)} %get-tuple-element.59), channel_id=1, source_target_pairs={{0,4},{1,5},{2,6},{3,7},{4,0},{5,1},{6,2},{7,3},{8,12},{9,13},{10,... | collective-permute-start | bytes 196616 | tf_op jit(solution)/shard_map/ppermute | solution.py:267
  11.3 0.0 collective-permute-done.3.arrived
  11.4 1.3 %collective-permute-start.4 = (bf16[128,256]{1,0:T(8,128)(2,1)S(1)}, bf16[128,256]{1,0:T(8,128)(2,1)S(1)}, u32[]{:S(2)}, u32[]{:S(2)}) collective-permute-start(bf16[128,256]{1,0:T(8,128)(2,1)S(1)} %get-tuple-element.55), channel_id=1, source_target_pairs={{0,16},{1,17},{2,18},{3,19},{4,20},{5,21},{6,22},{7,23},{8,24},{9,... | collective-permute-start | bytes 196616 | tf_op jit(solution)/shard_map/ppermute | solution.py:267
  12.7 2.1 %collective-permute-start.2 = (bf16[128,256]{1,0:T(8,128)(2,1)S(1)}, bf16[128,256]{1,0:T(8,128)(2,1)S(1)}, u32[]{:S(2)}, u32[]{:S(2)}) collective-permute-start(bf16[128,256]{1,0:T(8,128)(2,1)S(1)} %get-tuple-element.51), channel_id=1, source_target_pairs={{0,6},{1,7},{2,4},{3,5},{4,2},{5,3},{6,0},{7,1},{8,14},{9,15},{10,... | collective-permute-start | bytes 196616 | tf_op jit(solution)/shard_map/ppermute | solution.py:267
  14.8 1.3 %collective-permute-start.9 = (bf16[128,256]{1,0:T(8,128)(2,1)S(1)}, bf16[128,256]{1,0:T(8,128)(2,1)S(1)}, u32[]{:S(2)}, u32[]{:S(2)}) collective-permute-start(bf16[128,256]{1,0:T(8,128)(2,1)S(1)} %get-tuple-element.77), channel_id=1, source_target_pairs={{0,5},{1,4},{2,7},{3,6},{4,1},{5,0},{6,3},{7,2},{8,13},{9,12},{10,... | collective-permute-start | bytes 196616 | tf_op jit(solution)/shard_map/ppermute | solution.py:267
  16.1 0.0 copy-start
  16.1 0.0 copy-start.4
  16.1 0.9 %collective-permute-start.10 = (bf16[128,256]{1,0:T(8,128)(2,1)S(1)}, bf16[128,256]{1,0:T(8,128)(2,1)S(1)}, u32[]{:S(2)}, u32[]{:S(2)}) collective-permute-start(bf16[128,256]{1,0:T(8,128)(2,1)S(1)} %get-tuple-element.78), channel_id=1, source_target_pairs={{0,7},{1,6},{2,5},{3,4},{4,3},{5,2},{6,1},{7,0},{8,15},{9,14},{10,... | collective-permute-start | bytes 196616 | tf_op jit(solution)/shard_map/ppermute | solution.py:267
  17.0 0.0 collective-permute-done.5.refs_0_.refs_16_
  17.0 0.0 collective-permute-done.4.arrived
  17.0 1.3 %collective-permute-start.6 = (bf16[256,256]{1,0:T(8,128)(2,1)S(1)}, bf16[256,256]{1,0:T(8,128)(2,1)S(1)}, u32[]{:S(2)}, u32[]{:S(2)}) collective-permute-start(bf16[256,256]{1,0:T(8,128)(2,1)S(1)} %get-tuple-element.74), channel_id=1, source_target_pairs={{0,1},{1,0},{2,3},{3,2},{4,5},{5,4},{6,7},{7,6},{8,9},{9,8},{10,11... | collective-permute-start | bytes 393224 | tf_op jit(solution)/shard_map/ppermute | solution.py:267
  18.3 1.4 %collective-permute-start.7 = (bf16[256,256]{1,0:T(8,128)(2,1)S(1)}, bf16[256,256]{1,0:T(8,128)(2,1)S(1)}, u32[]{:S(2)}, u32[]{:S(2)}) collective-permute-start(bf16[256,256]{1,0:T(8,128)(2,1)S(1)} %get-tuple-element.75), channel_id=1, source_target_pairs={{0,2},{1,3},{2,0},{3,1},{4,6},{5,7},{6,4},{7,5},{8,10},{9,11},{10,... | collective-permute-start | bytes 393224 | tf_op jit(solution)/shard_map/ppermute | solution.py:267
  19.7 0.0 collective-permute-done.2.refs_0_.refs_18_
  19.7 0.1 collective-permute-start.8
  19.7 0.0 copy-done
  19.7 0.0 copy-done.4
  19.7 3.3 %build_weights.1 = (f32[128,1024]{1,0:T(8,128)S(1)}, f32[128,1024]{1,0:T(8,128)S(1)}, f32[128,1024]{1,0:T(8,128)S(1)}, f32[128,1024]{1,0:T(8,128)S(1)}, bf16[128...) custom-call(s32[1,64]{1,0:T(1,128)S(1)} %copy-done.4, ...), custom_call_target="tpu_custom_call" | custom-call | tf_op jit(solution)/shard_map/build_weights/pallas_call | solution.py:151
  23.0 0.0 collective-permute-done.9.refs_0_.refs_17_
  23.0 0.0 collective-permute-done.10.refs_1_.refs_19_
  23.0 0.0 collective-permute-done.6.refs_2_.refs_13_
  23.0 2.0 %collective-permute-done.7.refs_1_.refs_14_ = bf16[256,256]{1,0:T(8,128)(2,1)S(1)} collective-permute-done((bf16[256,256]{1,0:T(8,128)(2,1)S(1)}, bf16[256,256]{1,0:T(8,128)(2,1)S(1)}, u32[]{:S(2)}, u32[]{:S(2)}) %collective-permute-start.7) | collective-permute-done | bytes 131104 | tf_op jit(solution)/shard_map/ppermute | solution.py:267
  25.0 2.2 %collective-permute-done.8.refs_0_.refs_15_ = bf16[256,256]{1,0:T(8,128)(2,1)S(1)} collective-permute-done((bf16[256,256]{1,0:T(8,128)(2,1)S(1)}, bf16[256,256]{1,0:T(8,128)(2,1)S(1)}, u32[]{:S(2)}, u32[]{:S(2)}) %collective-permute-start.8) | collective-permute-done | bytes 131104 | tf_op jit(solution)/shard_map/ppermute | solution.py:267
  27.3 2.3 %collective-permute-start.11 = (bf16[128,256]{1,0:T(8,128)(2,1)S(1)}, bf16[128,256]{1,0:T(8,128)(2,1)S(1)}, u32[]{:S(2)}, u32[]{:S(2)}) collective-permute-start(bf16[128,256]{1,0:T(8,128)(2,1)S(1)} %get-tuple-element.84), channel_id=1, source_target_pairs={{0,8},{1,9},{2,10},{3,11},{4,12},{5,13},{6,14},{7,15},{8,0},{9,1},... | collective-permute-start | bytes 196616 | tf_op jit(solution)/shard_map/ppermute | solution.py:267
  29.6 1.6 %right_side.1 = (bf16[1024,256]{1,0:T(8,128)(2,1)S(1)}, bf16[256,1024]{1,0:T(8,128)(2,1)S(1)}, f32[512,256]{1,0:T(8,128)S(1)}, f32[512,256]{1,0:T(8,128)S(1)}) custom-call(f32[128,1024]{1,0:T(8,128)S(1)} %get-tuple-element.61.refs_0_, f32[128,1024]{1,0:T(8,128)S(1)} %get-tuple-element.62.refs_1_, f32[128,1024]{1,0:T(8,128)S(1)} %get-tuple-element.63.refs_2_, ...), custom_call_target="tpu_custom_call" | custom-call | tf_op jit(solution)/shard_map/right_side/pallas_call | solution.py:179
  31.2 0.0 collective-permute-done.11.refs_9_
  31.2 6.5 %solve_users.1 = f32[512,256]{1,0:T(8,128)} custom-call(f32[128,1024]{1,0:T(8,128)S(1)} %get-tuple-element.61.refs_0_, f32[128,1024]{1,0:T(8,128)S(1)} %get-tuple-element.62.refs_1_, f32[128,1024]{1,0:T(8,128)S(1)} %get-tuple-element.63.refs_2_, f32[128,1024]{1,0:T(8,128)S(1)} %get-tuple-element.64.refs_3_, bf16[1024,256]{1,0:T(8,128)(2,1)S(1)} %get-tuple-element.80.refs_4_, ...), custom_call_target="tpu_custom_call" | custom-call | tf_op jit(solution)/shard_map/solve_users/pallas_call | solution.py:254
  (8 shorter events, 0.1 us)
Async XLA Ops:
  0.0 0.7 %copy-start.3 = (s32[1,8,1]{1,2,0:T(1,128)S(1)}, s32[1,8,1]{1,2,0:T(1,128)}, u32[]{:S(2)}) copy-start(s32[1,8,1]{1,2,0:T(1,128)} %param.7) | copy-start | bytes 100
  0.0 0.7 %copy-start.2 = (s32[1,4,1]{1,2,0:T(1,128)S(1)}, s32[1,4,1]{1,2,0:T(1,128)}, u32[]{:S(2)}) copy-start(s32[1,4,1]{1,2,0:T(1,128)} %param.6) | copy-start | bytes 52
  0.0 0.9 %copy-start.1 = (bf16[256,256]{1,0:T(8,128)(2,1)S(1)}, bf16[256,256]{1,0:T(8,128)(2,1)}, u32[]{:S(2)}) copy-start(bf16[256,256]{1,0:T(8,128)(2,1)} %items.1) | copy-start | bytes 393220
  1.3 1.5 %collective-permute-start = (bf16[384,256]{1,0:T(8,128)(2,1)S(1)}, bf16[384,256]{1,0:T(8,128)(2,1)S(1)}, u32[]{:S(2)}, u32[]{:S(2)}) collective-permute-start(bf16[384,256]{1,0:T(8,128)(2,1)S(1)} %get-tuple-element.47), channel_id=1, source_target_pairs={{0,8},{1,9},{2,10},{3,11},{4,12},{5,13},{6,14},{7,15},{8,0},{9,1},... | collective-permute-start | bytes 589832 | tf_op jit(solution)/shard_map/ppermute | solution.py:267
  2.8 6.0 %collective-permute-start.1 = (bf16[256,256]{1,0:T(8,128)(2,1)S(1)}, bf16[256,256]{1,0:T(8,128)(2,1)S(1)}, u32[]{:S(2)}, u32[]{:S(2)}) collective-permute-start(bf16[256,256]{1,0:T(8,128)(2,1)S(1)} %get-tuple-element.50), channel_id=1, source_target_pairs={{0,16},{1,17},{2,18},{3,19},{4,20},{5,21},{6,22},{7,23},{8,24},{9,... | collective-permute-start | bytes 393224 | tf_op jit(solution)/shard_map/ppermute | solution.py:267
  5.3 6.1 %collective-permute-start.3 = (bf16[128,256]{1,0:T(8,128)(2,1)S(1)}, bf16[128,256]{1,0:T(8,128)(2,1)S(1)}, u32[]{:S(2)}, u32[]{:S(2)}) collective-permute-start(bf16[128,256]{1,0:T(8,128)(2,1)S(1)} %get-tuple-element.53), channel_id=1, source_target_pairs={{0,4},{1,5},{2,6},{3,7},{4,0},{5,1},{6,2},{7,3},{8,12},{9,13},{10,... | collective-permute-start | bytes 196616 | tf_op jit(solution)/shard_map/ppermute | solution.py:267
  9.1 7.9 %collective-permute-start.5 = (bf16[128,256]{1,0:T(8,128)(2,1)S(1)}, bf16[128,256]{1,0:T(8,128)(2,1)S(1)}, u32[]{:S(2)}, u32[]{:S(2)}) collective-permute-start(bf16[128,256]{1,0:T(8,128)(2,1)S(1)} %get-tuple-element.59), channel_id=1, source_target_pairs={{0,4},{1,5},{2,6},{3,7},{4,0},{5,1},{6,2},{7,3},{8,12},{9,13},{10,... | collective-permute-start | bytes 196616 | tf_op jit(solution)/shard_map/ppermute | solution.py:267
  11.4 5.6 %collective-permute-start.4 = (bf16[128,256]{1,0:T(8,128)(2,1)S(1)}, bf16[128,256]{1,0:T(8,128)(2,1)S(1)}, u32[]{:S(2)}, u32[]{:S(2)}) collective-permute-start(bf16[128,256]{1,0:T(8,128)(2,1)S(1)} %get-tuple-element.55), channel_id=1, source_target_pairs={{0,16},{1,17},{2,18},{3,19},{4,20},{5,21},{6,22},{7,23},{8,24},{9,... | collective-permute-start | bytes 196616 | tf_op jit(solution)/shard_map/ppermute | solution.py:267
  12.7 7.0 %collective-permute-start.2 = (bf16[128,256]{1,0:T(8,128)(2,1)S(1)}, bf16[128,256]{1,0:T(8,128)(2,1)S(1)}, u32[]{:S(2)}, u32[]{:S(2)}) collective-permute-start(bf16[128,256]{1,0:T(8,128)(2,1)S(1)} %get-tuple-element.51), channel_id=1, source_target_pairs={{0,6},{1,7},{2,4},{3,5},{4,2},{5,3},{6,0},{7,1},{8,14},{9,15},{10,... | collective-permute-start | bytes 196616 | tf_op jit(solution)/shard_map/ppermute | solution.py:267
  14.8 8.2 %collective-permute-start.9 = (bf16[128,256]{1,0:T(8,128)(2,1)S(1)}, bf16[128,256]{1,0:T(8,128)(2,1)S(1)}, u32[]{:S(2)}, u32[]{:S(2)}) collective-permute-start(bf16[128,256]{1,0:T(8,128)(2,1)S(1)} %get-tuple-element.77), channel_id=1, source_target_pairs={{0,5},{1,4},{2,7},{3,6},{4,1},{5,0},{6,3},{7,2},{8,13},{9,12},{10,... | collective-permute-start | bytes 196616 | tf_op jit(solution)/shard_map/ppermute | solution.py:267
  16.1 3.7 %copy-start = (bf16[64,128,128]{2,1,0:T(8,128)(2,1)S(1)}, bf16[64,128,128]{2,1,0:T(8,128)(2,1)}, u32[]{:S(2)}) copy-start(bf16[64,128,128]{2,1,0:T(8,128)(2,1)} %tiles.1) | copy-start | bytes 6291460
  16.1 3.7 %copy-start.4 = (s32[1,64]{1,0:T(1,128)S(1)}, s32[1,64]{1,0:T(1,128)}, u32[]{:S(2)}) copy-start(s32[1,64]{1,0:T(1,128)} %slots.1) | copy-start | bytes 772
  16.1 6.9 %collective-permute-start.10 = (bf16[128,256]{1,0:T(8,128)(2,1)S(1)}, bf16[128,256]{1,0:T(8,128)(2,1)S(1)}, u32[]{:S(2)}, u32[]{:S(2)}) collective-permute-start(bf16[128,256]{1,0:T(8,128)(2,1)S(1)} %get-tuple-element.78), channel_id=1, source_target_pairs={{0,7},{1,6},{2,5},{3,4},{4,3},{5,2},{6,1},{7,0},{8,15},{9,14},{10,... | collective-permute-start | bytes 196616 | tf_op jit(solution)/shard_map/ppermute | solution.py:267
  17.0 6.0 %collective-permute-start.6 = (bf16[256,256]{1,0:T(8,128)(2,1)S(1)}, bf16[256,256]{1,0:T(8,128)(2,1)S(1)}, u32[]{:S(2)}, u32[]{:S(2)}) collective-permute-start(bf16[256,256]{1,0:T(8,128)(2,1)S(1)} %get-tuple-element.74), channel_id=1, source_target_pairs={{0,1},{1,0},{2,3},{3,2},{4,5},{5,4},{6,7},{7,6},{8,9},{9,8},{10,11... | collective-permute-start | bytes 393224 | tf_op jit(solution)/shard_map/ppermute | solution.py:267
  18.3 6.7 %collective-permute-start.7 = (bf16[256,256]{1,0:T(8,128)(2,1)S(1)}, bf16[256,256]{1,0:T(8,128)(2,1)S(1)}, u32[]{:S(2)}, u32[]{:S(2)}) collective-permute-start(bf16[256,256]{1,0:T(8,128)(2,1)S(1)} %get-tuple-element.75), channel_id=1, source_target_pairs={{0,2},{1,3},{2,0},{3,1},{4,6},{5,7},{6,4},{7,5},{8,10},{9,11},{10,... | collective-permute-start | bytes 393224 | tf_op jit(solution)/shard_map/ppermute | solution.py:267
  19.7 7.6 %collective-permute-start.8 = (bf16[256,256]{1,0:T(8,128)(2,1)S(1)}, bf16[256,256]{1,0:T(8,128)(2,1)S(1)}, u32[]{:S(2)}, u32[]{:S(2)}) collective-permute-start(bf16[256,256]{1,0:T(8,128)(2,1)S(1)} %get-tuple-element.76), channel_id=1, source_target_pairs={{0,3},{1,2},{2,1},{3,0},{4,7},{5,6},{6,5},{7,4},{8,11},{9,10},{10,... | collective-permute-start | bytes 393224 | tf_op jit(solution)/shard_map/ppermute | solution.py:267
  27.3 3.9 %collective-permute-start.11 = (bf16[128,256]{1,0:T(8,128)(2,1)S(1)}, bf16[128,256]{1,0:T(8,128)(2,1)S(1)}, u32[]{:S(2)}, u32[]{:S(2)}) collective-permute-start(bf16[128,256]{1,0:T(8,128)(2,1)S(1)} %get-tuple-element.84), channel_id=1, source_target_pairs={{0,8},{1,9},{2,10},{3,11},{4,12},{5,13},{6,14},{7,15},{8,0},{9,1},... | collective-permute-start | bytes 196616 | tf_op jit(solution)/shard_map/ppermute | solution.py:267

commit v4 on v3

--- a/solution.py
+++ b/solution.py
@@ -15,6 +15,9 @@
 ITERS = 8
 BF16 = jnp.bfloat16
 F32 = jnp.float32
+
+HALF = BLOCK // 2
+PART = 3 * HALF // 2
 
 ridge = 0.1
 COST = 1000000000
@@ -55,7 +58,29 @@
     return jnp.max(jnp.where(place == index, row, 0))
 
 
-def first_kernel(send, route, items, _, out, panel_y, panel_own, gram_own, picks, gram):
+def pack_gram(gram, parts):
+    for core in range(2):
+        rows = slice(core * BLOCK, (core + 1) * BLOCK)
+        square = gram[rows, rows]
+        side = gram[core * HALF : (core + 1) * HALF, BLOCK:]
+        parts[core, 0:HALF, 0:BLOCK] = square[0:HALF, :]
+        parts[core, 0:HALF, BLOCK:] = square[HALF:, :]
+        parts[core, HALF:, 0:BLOCK] = side[0 : HALF // 2, :]
+        parts[core, HALF:, BLOCK:] = side[HALF // 2 :, :]
+
+
+def unpack_gram(parts, gram):
+    for core in range(2):
+        rows = slice(core * BLOCK, (core + 1) * BLOCK)
+        half = slice(core * HALF, (core + 1) * HALF)
+        part = parts[core]
+        gram[rows, rows] = jnp.concatenate([part[0:HALF, 0:BLOCK], part[0:HALF, BLOCK:]], axis=0).astype(BF16)
+        side = jnp.concatenate([part[HALF:, 0:BLOCK], part[HALF:, BLOCK:]], axis=0)
+        gram[half, BLOCK:] = side.astype(BF16)
+    gram[BLOCK:, 0:BLOCK] = gram[0:BLOCK, BLOCK:].T
+
+
+def first_kernel(send, route, items, _, out, panel_y, panel_own, gram_own, picks, gram, parts):
     group = lax.axis_index("grp")
     member = lax.axis_index("dev")
     core = lax.rem(group, 2)
@@ -66,8 +91,9 @@
     panel_own[...] = own_panel(items, entry(panels, group))
     rows = items[...]
     gram[...] = lax.dot_general(rows, rows, (((0,), (0,)), ((), ())), preferred_element_type=F32)
-    out[2 * BLOCK : 3 * BLOCK, :] = own_panel(gram, 1 - core).astype(BF16)
-    gram_own[...] = own_panel(gram, core)
+    pack_gram(gram, parts)
+    out[2 * BLOCK :, :] = parts[1 - core].astype(BF16)
+    gram_own[...] = parts[core]
     for step in range(8):
         picks[step : step + 1, :] = jnp.full((1, BLOCK), entry(routes, member ^ step) ^ group, jnp.int32)
 
@@ -75,7 +101,7 @@
 def pack_y(panel_y, gram_own, from_core, out, gram_out, gram_sum):
     out[0:BLOCK, :] = panel_y[...]
     out[BLOCK : 2 * BLOCK, :] = from_core[BLOCK : 2 * BLOCK, :]
-    total = gram_own[...] + from_core[2 * BLOCK : 3 * BLOCK, :].astype(F32)
+    total = gram_own[...] + from_core[2 * BLOCK :, :].astype(F32)
     gram_out[...] = total.astype(BF16)
     gram_sum[...] = total
 
@@ -90,7 +116,7 @@
         outs[step][...] = pool[jnp.max(picks[step : step + 1, :])]
 
 
-def add_gram(gram_own, arrived, out, gram_sum):
+def add_gram(gram_own, arrived, _, out, gram_sum):
     total = gram_own[...] + arrived[...].astype(F32)
     out[...] = total.astype(BF16)
     gram_sum[...] = total
@@ -102,14 +128,14 @@
     gram_sum[...] = total
     for panel, out in zip(panels, outs):
         out[0:BLOCK, :] = panel[...]
-        out[BLOCK : 2 * BLOCK, :] = total.astype(BF16)
+        out[BLOCK:, :] = total.astype(BF16)
 
 
 def last_gram(gram_own, *refs):
     out, gram_sum = refs[-2:]
     total = gram_own[...]
     for part in refs[:3]:
-        total += part[BLOCK : 2 * BLOCK, :].astype(F32)
+        total += part[BLOCK:, :].astype(F32)
     out[...] = total.astype(BF16)
     gram_sum[...] = total
 
@@ -188,7 +214,7 @@
     weights, refs = refs[:USER_BLOCKS], refs[USER_BLOCKS:]
     items, items_t, right_side, first_image = refs[:4]
     gram_parts, result, gram, sems = refs[4 : 4 + halves], refs[4 + halves], refs[5 + halves], refs[6 + halves]
-    state = refs[7 + halves :]
+    halves_ref, state = refs[7 + halves], refs[8 + halves :]
     residuals, directions, solved = (state[i : i + USER_BLOCKS] for i in range(0, 3 * USER_BLOCKS, USER_BLOCKS))
     dot = functools.partial(jnp.dot, preferred_element_type=F32)
     if halves == 1:
@@ -196,7 +222,8 @@
     else:
         core = lax.rem(lax.axis_index("grp"), 2)
         for place, part in zip((core, 1 - core), gram_parts):
-            gram[pl.ds(pl.multiple_of(place * BLOCK, BLOCK), BLOCK), :] = part[...].astype(BF16)
+            halves_ref[place] = part[...].astype(F32)
+        unpack_gram(halves_ref, gram)
 
     def rows(block):
         return slice(block * BLOCK, (block + 1) * BLOCK)
@@ -254,7 +281,7 @@
     return call(
         functools.partial(solve_kernel, len(gram_parts), unroll), "solve_users",
         [VM] * (USER_BLOCKS + 4 + len(gram_parts)), ANY, shape(users, F32),
-        [pltpu.VMEM((RANK, RANK), BF16), pltpu.SemaphoreType.DMA((USER_BLOCKS,))]
+        [pltpu.VMEM((RANK, RANK), BF16), pltpu.SemaphoreType.DMA((USER_BLOCKS,)), pltpu.VMEM((2, PART, RANK), F32)]
         + [pltpu.VMEM((BLOCK, RANK), F32)] * 3 * USER_BLOCKS,
         cost=None,
     )(*weights, *started, *gram_parts)
@@ -270,14 +297,14 @@
 def shards_4x8(item_factors, send_list, route_list, tile_slot, confidence):
     send_list, route_list = send_list.reshape(1, -1), route_list.reshape(1, -1)
     half, both = shape(BLOCK), shape(2 * BLOCK)
-    total = shape(BLOCK, F32)
+    part, total, near_shape = shape(PART), shape(PART, F32), shape(BLOCK + PART)
     out, panel_y, panel_own, gram, picks = call(
         first_kernel, "first", [VM] * 3 + [ANY], [VM] * 5,
-        [shape(3 * BLOCK), half, half, total, jax.ShapeDtypeStruct((8, BLOCK), jnp.int32)],
-        [pltpu.VMEM((RANK, RANK), F32)],
+        [shape(2 * BLOCK + PART), half, half, total, jax.ShapeDtypeStruct((8, BLOCK), jnp.int32)],
+        [pltpu.VMEM((RANK, RANK), F32), pltpu.VMEM((2, PART, RANK), F32)],
     )(send_list, route_list, item_factors, after(LEAD))
     from_core = swap(out, 1, 0)
-    out, gram_out, gram = call(pack_y, "pack_y", [VM] * 3, [VM] * 3, [both, half, total])(
+    out, gram_out, gram = call(pack_y, "pack_y", [VM] * 3, [VM] * 3, [both, part, total])(
         panel_y, gram, from_core
     )
     from_y = swap(out, 2, 0)
@@ -288,17 +315,19 @@
     panels = [outs[0]] + [None] * 7
     for k in (4, 6, 5, 7):
         panels[k] = swap(outs[k], 0, k)
-    gram_out, gram = call(add_gram, "add_gram", [VM] * 2, [VM] * 2, [half, total])(gram, gram_in)
+    gram_out, gram = call(add_gram, "add_gram", [VM] * 2 + [ANY], [VM] * 2, [part, total])(
+        gram, gram_in, after(COST // 4, gram_in)
+    )
     gram_in = swap(gram_out, 2, 0)
     token = after(COST, panels[4])
-    *near, gram = call(pack_near, "pack_near", [VM] * 5 + [ANY], [VM] * 4, [both] * 3 + [total])(
+    *near, gram = call(pack_near, "pack_near", [VM] * 5 + [ANY], [VM] * 4, [near_shape] * 3 + [total])(
         gram, gram_in, outs[1], outs[2], outs[3], token
     )
     for k in (3, 2, 1):
         panels[k] = swap(near[k - 1], 0, k)
     built = build_weights(tile_slot, confidence, after(0, panels[6], gram), 8 * BLOCK, True)
     token = after(COST, panels[5], panels[7])
-    out, gram = call(last_gram, "last_gram", [VM] * 4 + [ANY] * 2, [VM] * 2, [half, total])(
+    out, gram = call(last_gram, "last_gram", [VM] * 4 + [ANY] * 2, [VM] * 2, [part, total])(
         gram, panels[3], panels[2], panels[1], token, built[-1]
     )
     other = swap(out, 1, 0)

time: 37.8 us -> 37.1 us (0.981)
  Pallas kernels: 12 us -> 11.6 us
    pallas_call x1, Pallas kernels: 3.25 us -> 2.82 us  [build_weights(): call(functools.partial(build_kernel, mixed), 'build_weights', [SM, VM, AN...]
  transfers between devices with their start and end apart: 12 -> 12, of which waited for: 4 -> 5; matrix products, arithmetic and copies ran while one was open for 0% -> 0% of each run, Pallas kernels for 14% -> 13%
where the time goes in v4:
time: 37.1 us; the launch traced here: 37 us
  starting transfers between devices  17.8 us (48%)
  Pallas kernels  11.6 us (31%)
  waiting for transfers between devices  6.5 us (18%)
  local copies, waits for them, and re-layouts  0.93 us (3%)
    ppermute x12, starting transfers between devices, swap(): return lax.ppermute(array, ('grp', 'dev'), order)  17.8 us
    pallas_call x1, Pallas kernels, solve_users(): call(functools.partial(solve_kernel, len(gram_parts), unroll), 'solve_use...  6.52 us
    ppermute x12, waiting for transfers between devices, swap(): return lax.ppermute(array, ('grp', 'dev'), order)  6.5 us
    pallas_call x1, Pallas kernels, build_weights(): call(functools.partial(build_kernel, mixed), 'build_weights', [SM, VM, AN...  2.82 us
    pallas_call x1, Pallas kernels, start_solve(): call(functools.partial(right_kernel, len(panels)), 'right_side', [VM] * (...  1.63 us
    unnamed x10, local copies, waits for them, and re-layouts  0.93 us
  transfers between devices with their start and end apart: 12, of which 5 were waited for; matrix products, arithmetic and copies ran while one was open for 0% of the time, Pallas kernels for 13%

profile of v4, /device:TPU:1, one launch (start us, length us, event | category | flops | bytes accessed | tf_op | source)
XLA Modules:
  0.0 37.0 jit_solution(12385498678714979582)
XLA Ops:
  0.0 0.0 copy-start.3
  0.0 0.0 copy-start.2
  0.0 0.0 copy-start.1
  0.0 0.6 %copy-done.3 = s32[1,8,1]{1,2,0:T(1,128)S(1)} copy-done((s32[1,8,1]{1,2,0:T(1,128)S(1)}, s32[1,8,1]{1,2,0:T(1,128)}, u32[]{:S(2)}) %copy-start.3) | copy-done | bytes 56
  0.7 0.0 copy-done.2
  0.7 0.3 copy-done.1
  0.9 0.3 first.1
  1.3 0.1 collective-permute-start
  1.4 1.4 %collective-permute-done.from_core = bf16[352,256]{1,0:T(8,128)(2,1)S(1)} collective-permute-done((bf16[352,256]{1,0:T(8,128)(2,1)S(1)}, bf16[352,256]{1,0:T(8,128)(2,1)S(1)}, u32[]{:S(2)}, u32[]{:S(2)}) %collective-permute-start) | collective-permute-done | bytes 180256 | tf_op jit(solution)/shard_map/ppermute | solution.py:294
  2.8 2.4 %collective-permute-start.1 = (bf16[256,256]{1,0:T(8,128)(2,1)S(1)}, bf16[256,256]{1,0:T(8,128)(2,1)S(1)}, u32[]{:S(2)}, u32[]{:S(2)}) collective-permute-start(bf16[256,256]{1,0:T(8,128)(2,1)S(1)} %get-tuple-element.50), channel_id=1, source_target_pairs={{0,16},{1,17},{2,18},{3,19},{4,20},{5,21},{6,22},{7,23},{8,24},{9,... | collective-permute-start | bytes 393224 | tf_op jit(solution)/shard_map/ppermute | solution.py:294
  5.2 2.3 %collective-permute-start.3 = (bf16[96,256]{1,0:T(8,128)(2,1)S(1)}, bf16[96,256]{1,0:T(8,128)(2,1)S(1)}, u32[]{:S(2)}, u32[]{:S(2)}) collective-permute-start(bf16[96,256]{1,0:T(8,128)(2,1)S(1)} %get-tuple-element.53), channel_id=1, source_target_pairs={{0,4},{1,5},{2,6},{3,7},{4,0},{5,1},{6,2},{7,3},{8,12},{9,13},{10,... | collective-permute-start | bytes 147464 | tf_op jit(solution)/shard_map/ppermute | solution.py:294
  7.5 1.3 %collective-permute-done.1.from_y = bf16[256,256]{1,0:T(8,128)(2,1)S(1)} collective-permute-done((bf16[256,256]{1,0:T(8,128)(2,1)S(1)}, bf16[256,256]{1,0:T(8,128)(2,1)S(1)}, u32[]{:S(2)}, u32[]{:S(2)}) %collective-permute-start.1) | collective-permute-done | bytes 131104 | tf_op jit(solution)/shard_map/ppermute | solution.py:294
  8.8 0.2 pack_dev.1
  9.0 2.3 %collective-permute-start.5 = (bf16[128,256]{1,0:T(8,128)(2,1)S(1)}, bf16[128,256]{1,0:T(8,128)(2,1)S(1)}, u32[]{:S(2)}, u32[]{:S(2)}) collective-permute-start(bf16[128,256]{1,0:T(8,128)(2,1)S(1)} %get-tuple-element.59), channel_id=1, source_target_pairs={{0,4},{1,5},{2,6},{3,7},{4,0},{5,1},{6,2},{7,3},{8,12},{9,13},{10,... | collective-permute-start | bytes 196616 | tf_op jit(solution)/shard_map/ppermute | solution.py:294
  11.3 0.0 collective-permute-done.3.refs_0_.arrived
  11.3 1.3 %collective-permute-start.4 = (bf16[96,256]{1,0:T(8,128)(2,1)S(1)}, bf16[96,256]{1,0:T(8,128)(2,1)S(1)}, u32[]{:S(2)}, u32[]{:S(2)}) collective-permute-start(bf16[96,256]{1,0:T(8,128)(2,1)S(1)} %get-tuple-element.55), channel_id=1, source_target_pairs={{0,16},{1,17},{2,18},{3,19},{4,20},{5,21},{6,22},{7,23},{8,24},{9,... | collective-permute-start | bytes 147464 | tf_op jit(solution)/shard_map/ppermute | solution.py:294
  12.6 1.1 %collective-permute-start.2 = (bf16[128,256]{1,0:T(8,128)(2,1)S(1)}, bf16[128,256]{1,0:T(8,128)(2,1)S(1)}, u32[]{:S(2)}, u32[]{:S(2)}) collective-permute-start(bf16[128,256]{1,0:T(8,128)(2,1)S(1)} %get-tuple-element.51), channel_id=1, source_target_pairs={{0,6},{1,7},{2,4},{3,5},{4,2},{5,3},{6,0},{7,1},{8,14},{9,15},{10,... | collective-permute-start | bytes 196616 | tf_op jit(solution)/shard_map/ppermute | solution.py:294
  13.7 2.3 %collective-permute-start.9 = (bf16[128,256]{1,0:T(8,128)(2,1)S(1)}, bf16[128,256]{1,0:T(8,128)(2,1)S(1)}, u32[]{:S(2)}, u32[]{:S(2)}) collective-permute-start(bf16[128,256]{1,0:T(8,128)(2,1)S(1)} %get-tuple-element.77), channel_id=1, source_target_pairs={{0,5},{1,4},{2,7},{3,6},{4,1},{5,0},{6,3},{7,2},{8,13},{9,12},{10,... | collective-permute-start | bytes 196616 | tf_op jit(solution)/shard_map/ppermute | solution.py:294
  16.0 0.0 copy-start
  16.0 0.0 copy-start.4
  16.0 0.9 %collective-permute-start.10 = (bf16[128,256]{1,0:T(8,128)(2,1)S(1)}, bf16[128,256]{1,0:T(8,128)(2,1)S(1)}, u32[]{:S(2)}, u32[]{:S(2)}) collective-permute-start(bf16[128,256]{1,0:T(8,128)(2,1)S(1)} %get-tuple-element.78), channel_id=1, source_target_pairs={{0,7},{1,6},{2,5},{3,4},{4,3},{5,2},{6,1},{7,0},{8,15},{9,14},{10,... | collective-permute-start | bytes 196616 | tf_op jit(solution)/shard_map/ppermute | solution.py:294
  16.9 0.0 collective-permute-done.5.refs_0_.refs_16_
  16.9 0.0 collective-permute-done.4.arrived
  17.0 1.3 %collective-permute-start.6 = (bf16[224,256]{1,0:T(8,128)(2,1)S(1)}, bf16[224,256]{1,0:T(8,128)(2,1)S(1)}, u32[]{:S(2)}, u32[]{:S(2)}) collective-permute-start(bf16[224,256]{1,0:T(8,128)(2,1)S(1)} %get-tuple-element.74), channel_id=1, source_target_pairs={{0,1},{1,0},{2,3},{3,2},{4,5},{5,4},{6,7},{7,6},{8,9},{9,8},{10,11... | collective-permute-start | bytes 344072 | tf_op jit(solution)/shard_map/ppermute | solution.py:294
  18.2 0.3 collective-permute-start.7
  18.6 0.0 collective-permute-done.2.refs_0_.refs_18_
  18.6 1.1 %collective-permute-start.8 = (bf16[224,256]{1,0:T(8,128)(2,1)S(1)}, bf16[224,256]{1,0:T(8,128)(2,1)S(1)}, u32[]{:S(2)}, u32[]{:S(2)}) collective-permute-start(bf16[224,256]{1,0:T(8,128)(2,1)S(1)} %get-tuple-element.76), channel_id=1, source_target_pairs={{0,3},{1,2},{2,1},{3,0},{4,7},{5,6},{6,5},{7,4},{8,11},{9,10},{10,... | collective-permute-start | bytes 344072 | tf_op jit(solution)/shard_map/ppermute | solution.py:294
  19.7 0.0 copy-done
  19.7 0.0 copy-done.4
  19.7 2.8 %build_weights.1 = (f32[128,1024]{1,0:T(8,128)S(1)}, f32[128,1024]{1,0:T(8,128)S(1)}, f32[128,1024]{1,0:T(8,128)S(1)}, f32[128,1024]{1,0:T(8,128)S(1)}, bf16[128...) custom-call(s32[1,64]{1,0:T(1,128)S(1)} %copy-done.4, ...), custom_call_target="tpu_custom_call" | custom-call | tf_op jit(solution)/shard_map/build_weights/pallas_call | solution.py:177
  22.5 0.1 collective-permute-done.9.refs_0_.refs_17_
  22.6 0.0 collective-permute-done.10.refs_1_.refs_19_
  22.6 0.0 collective-permute-done.6.refs_2_.refs_13_
  22.6 1.0 %collective-permute-done.7.refs_1_.refs_14_ = bf16[224,256]{1,0:T(8,128)(2,1)S(1)} collective-permute-done((bf16[224,256]{1,0:T(8,128)(2,1)S(1)}, bf16[224,256]{1,0:T(8,128)(2,1)S(1)}, u32[]{:S(2)}, u32[]{:S(2)}) %collective-permute-start.7) | collective-permute-done | bytes 114720 | tf_op jit(solution)/shard_map/ppermute | solution.py:294
  23.6 2.8 %collective-permute-done.8.refs_0_.refs_15_ = bf16[224,256]{1,0:T(8,128)(2,1)S(1)} collective-permute-done((bf16[224,256]{1,0:T(8,128)(2,1)S(1)}, bf16[224,256]{1,0:T(8,128)(2,1)S(1)}, u32[]{:S(2)}, u32[]{:S(2)}) %collective-permute-start.8) | collective-permute-done | bytes 114720 | tf_op jit(solution)/shard_map/ppermute | solution.py:294
  26.4 2.4 %collective-permute-start.11 = (bf16[96,256]{1,0:T(8,128)(2,1)S(1)}, bf16[96,256]{1,0:T(8,128)(2,1)S(1)}, u32[]{:S(2)}, u32[]{:S(2)}) collective-permute-start(bf16[96,256]{1,0:T(8,128)(2,1)S(1)} %get-tuple-element.84), channel_id=1, source_target_pairs={{0,8},{1,9},{2,10},{3,11},{4,12},{5,13},{6,14},{7,15},{8,0},{9,1},... | collective-permute-start | bytes 147464 | tf_op jit(solution)/shard_map/ppermute | solution.py:294
  28.8 1.6 %right_side.1 = (bf16[1024,256]{1,0:T(8,128)(2,1)S(1)}, bf16[256,1024]{1,0:T(8,128)(2,1)S(1)}, f32[512,256]{1,0:T(8,128)S(1)}, f32[512,256]{1,0:T(8,128)S(1)}) custom-call(f32[128,1024]{1,0:T(8,128)S(1)} %get-tuple-element.61.refs_0_, f32[128,1024]{1,0:T(8,128)S(1)} %get-tuple-element.62.refs_1_, f32[128,1024]{1,0:T(8,128)S(1)} %get-tuple-element.63.refs_2_, ...), custom_call_target="tpu_custom_call" | custom-call | tf_op jit(solution)/shard_map/right_side/pallas_call | solution.py:205
  30.4 0.0 collective-permute-done.11.refs_9_
  30.4 6.5 %solve_users.1 = f32[512,256]{1,0:T(8,128)} custom-call(f32[128,1024]{1,0:T(8,128)S(1)} %get-tuple-element.61.refs_0_, f32[128,1024]{1,0:T(8,128)S(1)} %get-tuple-element.62.refs_1_, f32[128,1024]{1,0:T(8,128)S(1)} %get-tuple-element.63.refs_2_, f32[128,1024]{1,0:T(8,128)S(1)} %get-tuple-element.64.refs_3_, bf16[1024,256]{1,0:T(8,128)(2,1)S(1)} %get-tuple-element.80.refs_4_, ...), custom_call_target="tpu_custom_call" | custom-call | tf_op jit(solution)/shard_map/solve_users/pallas_call | solution.py:281
  (9 shorter events, 0.1 us)
Async XLA Ops:
  0.0 0.7 %copy-start.3 = (s32[1,8,1]{1,2,0:T(1,128)S(1)}, s32[1,8,1]{1,2,0:T(1,128)}, u32[]{:S(2)}) copy-start(s32[1,8,1]{1,2,0:T(1,128)} %param.7) | copy-start | bytes 100
  0.0 0.7 %copy-start.2 = (s32[1,4,1]{1,2,0:T(1,128)S(1)}, s32[1,4,1]{1,2,0:T(1,128)}, u32[]{:S(2)}) copy-start(s32[1,4,1]{1,2,0:T(1,128)} %param.6) | copy-start | bytes 52
  0.0 0.9 %copy-start.1 = (bf16[256,256]{1,0:T(8,128)(2,1)S(1)}, bf16[256,256]{1,0:T(8,128)(2,1)}, u32[]{:S(2)}) copy-start(bf16[256,256]{1,0:T(8,128)(2,1)} %items.1) | copy-start | bytes 393220
  1.3 1.5 %collective-permute-start = (bf16[352,256]{1,0:T(8,128)(2,1)S(1)}, bf16[352,256]{1,0:T(8,128)(2,1)S(1)}, u32[]{:S(2)}, u32[]{:S(2)}) collective-permute-start(bf16[352,256]{1,0:T(8,128)(2,1)S(1)} %get-tuple-element.47), channel_id=1, source_target_pairs={{0,8},{1,9},{2,10},{3,11},{4,12},{5,13},{6,14},{7,15},{8,0},{9,1},... | collective-permute-start | bytes 540680 | tf_op jit(solution)/shard_map/ppermute | solution.py:294
  2.8 6.0 %collective-permute-start.1 = (bf16[256,256]{1,0:T(8,128)(2,1)S(1)}, bf16[256,256]{1,0:T(8,128)(2,1)S(1)}, u32[]{:S(2)}, u32[]{:S(2)}) collective-permute-start(bf16[256,256]{1,0:T(8,128)(2,1)S(1)} %get-tuple-element.50), channel_id=1, source_target_pairs={{0,16},{1,17},{2,18},{3,19},{4,20},{5,21},{6,22},{7,23},{8,24},{9,... | collective-permute-start | bytes 393224 | tf_op jit(solution)/shard_map/ppermute | solution.py:294
  5.2 6.1 %collective-permute-start.3 = (bf16[96,256]{1,0:T(8,128)(2,1)S(1)}, bf16[96,256]{1,0:T(8,128)(2,1)S(1)}, u32[]{:S(2)}, u32[]{:S(2)}) collective-permute-start(bf16[96,256]{1,0:T(8,128)(2,1)S(1)} %get-tuple-element.53), channel_id=1, source_target_pairs={{0,4},{1,5},{2,6},{3,7},{4,0},{5,1},{6,2},{7,3},{8,12},{9,13},{10,... | collective-permute-start | bytes 147464 | tf_op jit(solution)/shard_map/ppermute | solution.py:294
  9.0 7.9 %collective-permute-start.5 = (bf16[128,256]{1,0:T(8,128)(2,1)S(1)}, bf16[128,256]{1,0:T(8,128)(2,1)S(1)}, u32[]{:S(2)}, u32[]{:S(2)}) collective-permute-start(bf16[128,256]{1,0:T(8,128)(2,1)S(1)} %get-tuple-element.59), channel_id=1, source_target_pairs={{0,4},{1,5},{2,6},{3,7},{4,0},{5,1},{6,2},{7,3},{8,12},{9,13},{10,... | collective-permute-start | bytes 196616 | tf_op jit(solution)/shard_map/ppermute | solution.py:294
  11.3 5.6 %collective-permute-start.4 = (bf16[96,256]{1,0:T(8,128)(2,1)S(1)}, bf16[96,256]{1,0:T(8,128)(2,1)S(1)}, u32[]{:S(2)}, u32[]{:S(2)}) collective-permute-start(bf16[96,256]{1,0:T(8,128)(2,1)S(1)} %get-tuple-element.55), channel_id=1, source_target_pairs={{0,16},{1,17},{2,18},{3,19},{4,20},{5,21},{6,22},{7,23},{8,24},{9,... | collective-permute-start | bytes 147464 | tf_op jit(solution)/shard_map/ppermute | solution.py:294
  12.6 6.0 %collective-permute-start.2 = (bf16[128,256]{1,0:T(8,128)(2,1)S(1)}, bf16[128,256]{1,0:T(8,128)(2,1)S(1)}, u32[]{:S(2)}, u32[]{:S(2)}) collective-permute-start(bf16[128,256]{1,0:T(8,128)(2,1)S(1)} %get-tuple-element.51), channel_id=1, source_target_pairs={{0,6},{1,7},{2,4},{3,5},{4,2},{5,3},{6,0},{7,1},{8,14},{9,15},{10,... | collective-permute-start | bytes 196616 | tf_op jit(solution)/shard_map/ppermute | solution.py:294
  13.7 8.9 %collective-permute-start.9 = (bf16[128,256]{1,0:T(8,128)(2,1)S(1)}, bf16[128,256]{1,0:T(8,128)(2,1)S(1)}, u32[]{:S(2)}, u32[]{:S(2)}) collective-permute-start(bf16[128,256]{1,0:T(8,128)(2,1)S(1)} %get-tuple-element.77), channel_id=1, source_target_pairs={{0,5},{1,4},{2,7},{3,6},{4,1},{5,0},{6,3},{7,2},{8,13},{9,12},{10,... | collective-permute-start | bytes 196616 | tf_op jit(solution)/shard_map/ppermute | solution.py:294
  16.0 3.7 %copy-start = (bf16[64,128,128]{2,1,0:T(8,128)(2,1)S(1)}, bf16[64,128,128]{2,1,0:T(8,128)(2,1)}, u32[]{:S(2)}) copy-start(bf16[64,128,128]{2,1,0:T(8,128)(2,1)} %tiles.1) | copy-start | bytes 6291460
  16.0 3.7 %copy-start.4 = (s32[1,64]{1,0:T(1,128)S(1)}, s32[1,64]{1,0:T(1,128)}, u32[]{:S(2)}) copy-start(s32[1,64]{1,0:T(1,128)} %slots.1) | copy-start | bytes 772
  16.0 6.5 %collective-permute-start.10 = (bf16[128,256]{1,0:T(8,128)(2,1)S(1)}, bf16[128,256]{1,0:T(8,128)(2,1)S(1)}, u32[]{:S(2)}, u32[]{:S(2)}) collective-permute-start(bf16[128,256]{1,0:T(8,128)(2,1)S(1)} %get-tuple-element.78), channel_id=1, source_target_pairs={{0,7},{1,6},{2,5},{3,4},{4,3},{5,2},{6,1},{7,0},{8,15},{9,14},{10,... | collective-permute-start | bytes 196616 | tf_op jit(solution)/shard_map/ppermute | solution.py:294
  17.0 5.6 %collective-permute-start.6 = (bf16[224,256]{1,0:T(8,128)(2,1)S(1)}, bf16[224,256]{1,0:T(8,128)(2,1)S(1)}, u32[]{:S(2)}, u32[]{:S(2)}) collective-permute-start(bf16[224,256]{1,0:T(8,128)(2,1)S(1)} %get-tuple-element.74), channel_id=1, source_target_pairs={{0,1},{1,0},{2,3},{3,2},{4,5},{5,4},{6,7},{7,6},{8,9},{9,8},{10,11... | collective-permute-start | bytes 344072 | tf_op jit(solution)/shard_map/ppermute | solution.py:294
  18.2 5.4 %collective-permute-start.7 = (bf16[224,256]{1,0:T(8,128)(2,1)S(1)}, bf16[224,256]{1,0:T(8,128)(2,1)S(1)}, u32[]{:S(2)}, u32[]{:S(2)}) collective-permute-start(bf16[224,256]{1,0:T(8,128)(2,1)S(1)} %get-tuple-element.75), channel_id=1, source_target_pairs={{0,2},{1,3},{2,0},{3,1},{4,6},{5,7},{6,4},{7,5},{8,10},{9,11},{10,... | collective-permute-start | bytes 344072 | tf_op jit(solution)/shard_map/ppermute | solution.py:294
  18.6 7.8 %collective-permute-start.8 = (bf16[224,256]{1,0:T(8,128)(2,1)S(1)}, bf16[224,256]{1,0:T(8,128)(2,1)S(1)}, u32[]{:S(2)}, u32[]{:S(2)}) collective-permute-start(bf16[224,256]{1,0:T(8,128)(2,1)S(1)} %get-tuple-element.76), channel_id=1, source_target_pairs={{0,3},{1,2},{2,1},{3,0},{4,7},{5,6},{6,5},{7,4},{8,11},{9,10},{10,... | collective-permute-start | bytes 344072 | tf_op jit(solution)/shard_map/ppermute | solution.py:294
  26.4 4.0 %collective-permute-start.11 = (bf16[96,256]{1,0:T(8,128)(2,1)S(1)}, bf16[96,256]{1,0:T(8,128)(2,1)S(1)}, u32[]{:S(2)}, u32[]{:S(2)}) collective-permute-start(bf16[96,256]{1,0:T(8,128)(2,1)S(1)} %get-tuple-element.84), channel_id=1, source_target_pairs={{0,8},{1,9},{2,10},{3,11},{4,12},{5,13},{6,14},{7,15},{8,0},{9,1},... | collective-permute-start | bytes 147464 | tf_op jit(solution)/shard_map/ppermute | solution.py:294

commit v5 on v4

--- a/solution.py
+++ b/solution.py
@@ -80,7 +80,7 @@
     gram[BLOCK:, 0:BLOCK] = gram[0:BLOCK, BLOCK:].T
 
 
-def first_kernel(send, route, items, _, out, panel_y, panel_own, gram_own, picks, gram, parts):
+def first_kernel(items, send, route, _, out, panel_y, panel_own, gram_own, picks, gram, parts):
     group = lax.axis_index("grp")
     member = lax.axis_index("dev")
     core = lax.rem(group, 2)
@@ -191,12 +191,14 @@
         panel = panels[i][0:BLOCK, :]
         items[rows, :] = panel
         items_t[:, rows] = panel.T
-    for block in range(USER_BLOCKS):
-        users = slice(block * BLOCK, (block + 1) * BLOCK)
-        target = dot(high[block][...], items[...]) + dot(low[block][...], items[...])
-        right_side[users, :] = target
-        scores = dot(target.astype(BF16), items_t[...])
-        image[users, :] = dot((weights[block][...] * scores).astype(BF16), items[...])
+    targets = [dot(high[block][...], items[...]) + dot(low[block][...], items[...]) for block in range(USER_BLOCKS)]
+    for first in range(0, USER_BLOCKS, 2):
+        pair = (first, first + 1)
+        scores = [dot(targets[block].astype(BF16), items_t[...]) for block in pair]
+        for block, score in zip(pair, scores):
+            users = slice(block * BLOCK, (block + 1) * BLOCK)
+            right_side[users, :] = targets[block]
+            image[users, :] = dot((weights[block][...] * score).astype(BF16), items[...])
 
 
 def start_solve(built, panels, after):
@@ -302,7 +304,7 @@
         first_kernel, "first", [VM] * 3 + [ANY], [VM] * 5,
         [shape(2 * BLOCK + PART), half, half, total, jax.ShapeDtypeStruct((8, BLOCK), jnp.int32)],
         [pltpu.VMEM((RANK, RANK), F32), pltpu.VMEM((2, PART, RANK), F32)],
-    )(send_list, route_list, item_factors, after(LEAD))
+    )(item_factors, send_list, route_list, after(LEAD))
     from_core = swap(out, 1, 0)
     out, gram_out, gram = call(pack_y, "pack_y", [VM] * 3, [VM] * 3, [both, part, total])(
         panel_y, gram, from_core
@@ -313,7 +315,7 @@
         pack_dev, "pack_dev", [VM] * 4, [VM] * 8, [half] * 8, [pltpu.VMEM((4, BLOCK, RANK), BF16)]
     )(picks, panel_own, from_core, from_y)
     panels = [outs[0]] + [None] * 7
-    for k in (4, 6, 5, 7):
+    for k in (4, 7, 5, 6):
         panels[k] = swap(outs[k], 0, k)
     gram_out, gram = call(add_gram, "add_gram", [VM] * 2 + [ANY], [VM] * 2, [part, total])(
         gram, gram_in, after(COST // 4, gram_in)
@@ -325,8 +327,8 @@
     )
     for k in (3, 2, 1):
         panels[k] = swap(near[k - 1], 0, k)
-    built = build_weights(tile_slot, confidence, after(0, panels[6], gram), 8 * BLOCK, True)
-    token = after(COST, panels[5], panels[7])
+    built = build_weights(tile_slot, confidence, after(0, panels[7], gram), 8 * BLOCK, True)
+    token = after(COST, panels[5], panels[6])
     out, gram = call(last_gram, "last_gram", [VM] * 4 + [ANY] * 2, [VM] * 2, [part, total])(
         gram, panels[3], panels[2], panels[1], token, built[-1]
     )

time: 37.1 us -> 36.9 us (level)
  transfers between devices with their start and end apart: 12 -> 12, of which waited for: 5 -> 5; matrix products, arithmetic and copies ran while one was open for 0% -> 0% of each run, Pallas kernels for 13% -> 12%
where the time goes in v5:
time: 36.9 us; the launch traced here: 36.7 us
  starting transfers between devices  17.8 us (48%)
  Pallas kernels  11.4 us (31%)
  waiting for transfers between devices  6.51 us (18%)
  local copies, waits for them, and re-layouts  0.93 us (3%)
    ppermute x12, starting transfers between devices, swap(): return lax.ppermute(array, ('grp', 'dev'), order)  17.8 us
    pallas_call x1, Pallas kernels, solve_users(): call(functools.partial(solve_kernel, len(gram_parts), unroll), 'solve_use...  6.52 us
    ppermute x12, waiting for transfers between devices, swap(): return lax.ppermute(array, ('grp', 'dev'), order)  6.51 us
    pallas_call x1, Pallas kernels, build_weights(): call(functools.partial(build_kernel, mixed), 'build_weights', [SM, VM, AN...  2.83 us
    pallas_call x1, Pallas kernels, start_solve(): call(functools.partial(right_kernel, len(panels)), 'right_side', [VM] * (...  1.37 us
    unnamed x10, local copies, waits for them, and re-layouts  0.93 us
  transfers between devices with their start and end apart: 12, of which 5 were waited for; matrix products, arithmetic and copies ran while one was open for 0% of the time, Pallas kernels for 12%

profile of v5, /device:TPU:1, one launch (start us, length us, event | category | flops | bytes accessed | tf_op | source)
XLA Modules:
  0.0 36.7 jit_solution(7839432078326157976)
XLA Ops:
  0.0 0.0 copy-start.3
  0.0 0.0 copy-start.2
  0.0 0.0 copy-start.1
  0.0 0.6 %copy-done.3 = s32[1,8,1]{1,2,0:T(1,128)S(1)} copy-done((s32[1,8,1]{1,2,0:T(1,128)S(1)}, s32[1,8,1]{1,2,0:T(1,128)}, u32[]{:S(2)}) %copy-start.3) | copy-done | bytes 56
  0.7 0.0 copy-done.2
  0.7 0.3 copy-done.1
  0.9 0.3 first.1
  1.3 0.1 collective-permute-start
  1.4 1.4 %collective-permute-done.from_core = bf16[352,256]{1,0:T(8,128)(2,1)S(1)} collective-permute-done((bf16[352,256]{1,0:T(8,128)(2,1)S(1)}, bf16[352,256]{1,0:T(8,128)(2,1)S(1)}, u32[]{:S(2)}, u32[]{:S(2)}) %collective-permute-start) | collective-permute-done | bytes 180256 | tf_op jit(solution)/shard_map/ppermute | solution.py:296
  2.8 2.4 %collective-permute-start.1 = (bf16[256,256]{1,0:T(8,128)(2,1)S(1)}, bf16[256,256]{1,0:T(8,128)(2,1)S(1)}, u32[]{:S(2)}, u32[]{:S(2)}) collective-permute-start(bf16[256,256]{1,0:T(8,128)(2,1)S(1)} %get-tuple-element.50), channel_id=1, source_target_pairs={{0,16},{1,17},{2,18},{3,19},{4,20},{5,21},{6,22},{7,23},{8,24},{9,... | collective-permute-start | bytes 393224 | tf_op jit(solution)/shard_map/ppermute | solution.py:296
  5.2 2.3 %collective-permute-start.3 = (bf16[96,256]{1,0:T(8,128)(2,1)S(1)}, bf16[96,256]{1,0:T(8,128)(2,1)S(1)}, u32[]{:S(2)}, u32[]{:S(2)}) collective-permute-start(bf16[96,256]{1,0:T(8,128)(2,1)S(1)} %get-tuple-element.53), channel_id=1, source_target_pairs={{0,4},{1,5},{2,6},{3,7},{4,0},{5,1},{6,2},{7,3},{8,12},{9,13},{10,... | collective-permute-start | bytes 147464 | tf_op jit(solution)/shard_map/ppermute | solution.py:296
  7.5 1.3 %collective-permute-done.1.from_y = bf16[256,256]{1,0:T(8,128)(2,1)S(1)} collective-permute-done((bf16[256,256]{1,0:T(8,128)(2,1)S(1)}, bf16[256,256]{1,0:T(8,128)(2,1)S(1)}, u32[]{:S(2)}, u32[]{:S(2)}) %collective-permute-start.1) | collective-permute-done | bytes 131104 | tf_op jit(solution)/shard_map/ppermute | solution.py:296
  8.8 0.2 pack_dev.1
  9.0 2.3 %collective-permute-start.5 = (bf16[128,256]{1,0:T(8,128)(2,1)S(1)}, bf16[128,256]{1,0:T(8,128)(2,1)S(1)}, u32[]{:S(2)}, u32[]{:S(2)}) collective-permute-start(bf16[128,256]{1,0:T(8,128)(2,1)S(1)} %get-tuple-element.59), channel_id=1, source_target_pairs={{0,4},{1,5},{2,6},{3,7},{4,0},{5,1},{6,2},{7,3},{8,12},{9,13},{10,... | collective-permute-start | bytes 196616 | tf_op jit(solution)/shard_map/ppermute | solution.py:296
  11.3 0.0 collective-permute-done.3.refs_0_.arrived
  11.3 1.3 %collective-permute-start.4 = (bf16[96,256]{1,0:T(8,128)(2,1)S(1)}, bf16[96,256]{1,0:T(8,128)(2,1)S(1)}, u32[]{:S(2)}, u32[]{:S(2)}) collective-permute-start(bf16[96,256]{1,0:T(8,128)(2,1)S(1)} %get-tuple-element.55), channel_id=1, source_target_pairs={{0,16},{1,17},{2,18},{3,19},{4,20},{5,21},{6,22},{7,23},{8,24},{9,... | collective-permute-start | bytes 147464 | tf_op jit(solution)/shard_map/ppermute | solution.py:296
  12.6 2.0 %collective-permute-start.2 = (bf16[128,256]{1,0:T(8,128)(2,1)S(1)}, bf16[128,256]{1,0:T(8,128)(2,1)S(1)}, u32[]{:S(2)}, u32[]{:S(2)}) collective-permute-start(bf16[128,256]{1,0:T(8,128)(2,1)S(1)} %get-tuple-element.51), channel_id=1, source_target_pairs={{0,7},{1,6},{2,5},{3,4},{4,3},{5,2},{6,1},{7,0},{8,15},{9,14},{10,... | collective-permute-start | bytes 196616 | tf_op jit(solution)/shard_map/ppermute | solution.py:296
  14.6 1.4 %collective-permute-start.9 = (bf16[128,256]{1,0:T(8,128)(2,1)S(1)}, bf16[128,256]{1,0:T(8,128)(2,1)S(1)}, u32[]{:S(2)}, u32[]{:S(2)}) collective-permute-start(bf16[128,256]{1,0:T(8,128)(2,1)S(1)} %get-tuple-element.77), channel_id=1, source_target_pairs={{0,5},{1,4},{2,7},{3,6},{4,1},{5,0},{6,3},{7,2},{8,13},{9,12},{10,... | collective-permute-start | bytes 196616 | tf_op jit(solution)/shard_map/ppermute | solution.py:296
  16.0 0.0 copy-start
  16.0 0.0 copy-start.4
  16.0 0.9 %collective-permute-start.10 = (bf16[128,256]{1,0:T(8,128)(2,1)S(1)}, bf16[128,256]{1,0:T(8,128)(2,1)S(1)}, u32[]{:S(2)}, u32[]{:S(2)}) collective-permute-start(bf16[128,256]{1,0:T(8,128)(2,1)S(1)} %get-tuple-element.78), channel_id=1, source_target_pairs={{0,6},{1,7},{2,4},{3,5},{4,2},{5,3},{6,0},{7,1},{8,14},{9,15},{10,... | collective-permute-start | bytes 196616 | tf_op jit(solution)/shard_map/ppermute | solution.py:296
  16.9 0.0 collective-permute-done.5.refs_0_.refs_16_
  16.9 0.0 collective-permute-done.4.arrived
  17.0 0.4 collective-permute-start.6
  17.4 1.2 %collective-permute-start.7 = (bf16[224,256]{1,0:T(8,128)(2,1)S(1)}, bf16[224,256]{1,0:T(8,128)(2,1)S(1)}, u32[]{:S(2)}, u32[]{:S(2)}) collective-permute-start(bf16[224,256]{1,0:T(8,128)(2,1)S(1)} %get-tuple-element.75), channel_id=1, source_target_pairs={{0,2},{1,3},{2,0},{3,1},{4,6},{5,7},{6,4},{7,5},{8,10},{9,11},{10,... | collective-permute-start | bytes 344072 | tf_op jit(solution)/shard_map/ppermute | solution.py:296
  18.6 0.0 collective-permute-done.2.refs_0_.refs_19_
  18.6 1.1 %collective-permute-start.8 = (bf16[224,256]{1,0:T(8,128)(2,1)S(1)}, bf16[224,256]{1,0:T(8,128)(2,1)S(1)}, u32[]{:S(2)}, u32[]{:S(2)}) collective-permute-start(bf16[224,256]{1,0:T(8,128)(2,1)S(1)} %get-tuple-element.76), channel_id=1, source_target_pairs={{0,3},{1,2},{2,1},{3,0},{4,7},{5,6},{6,5},{7,4},{8,11},{9,10},{10,... | collective-permute-start | bytes 344072 | tf_op jit(solution)/shard_map/ppermute | solution.py:296
  19.7 0.0 copy-done
  19.7 0.0 copy-done.4
  19.7 2.8 %build_weights.1 = (f32[128,1024]{1,0:T(8,128)S(1)}, f32[128,1024]{1,0:T(8,128)S(1)}, f32[128,1024]{1,0:T(8,128)S(1)}, f32[128,1024]{1,0:T(8,128)S(1)}, bf16[128...) custom-call(s32[1,64]{1,0:T(1,128)S(1)} %copy-done.4, ...), custom_call_target="tpu_custom_call" | custom-call | tf_op jit(solution)/shard_map/build_weights/pallas_call | solution.py:177
  22.6 0.1 collective-permute-done.9.refs_0_.refs_17_
  22.6 0.0 collective-permute-done.10.refs_1_.refs_18_
  22.6 0.0 collective-permute-done.6.refs_2_.refs_13_
  22.6 0.4 %collective-permute-done.7.refs_1_.refs_14_ = bf16[224,256]{1,0:T(8,128)(2,1)S(1)} collective-permute-done((bf16[224,256]{1,0:T(8,128)(2,1)S(1)}, bf16[224,256]{1,0:T(8,128)(2,1)S(1)}, u32[]{:S(2)}, u32[]{:S(2)}) %collective-permute-start.7) | collective-permute-done | bytes 114720 | tf_op jit(solution)/shard_map/ppermute | solution.py:296
  23.0 3.4 %collective-permute-done.8.refs_0_.refs_15_ = bf16[224,256]{1,0:T(8,128)(2,1)S(1)} collective-permute-done((bf16[224,256]{1,0:T(8,128)(2,1)S(1)}, bf16[224,256]{1,0:T(8,128)(2,1)S(1)}, u32[]{:S(2)}, u32[]{:S(2)}) %collective-permute-start.8) | collective-permute-done | bytes 114720 | tf_op jit(solution)/shard_map/ppermute | solution.py:296
  26.5 2.3 %collective-permute-start.11 = (bf16[96,256]{1,0:T(8,128)(2,1)S(1)}, bf16[96,256]{1,0:T(8,128)(2,1)S(1)}, u32[]{:S(2)}, u32[]{:S(2)}) collective-permute-start(bf16[96,256]{1,0:T(8,128)(2,1)S(1)} %get-tuple-element.84), channel_id=1, source_target_pairs={{0,8},{1,9},{2,10},{3,11},{4,12},{5,13},{6,14},{7,15},{8,0},{9,1},... | collective-permute-start | bytes 147464 | tf_op jit(solution)/shard_map/ppermute | solution.py:296
  28.8 1.4 %right_side.1 = (bf16[1024,256]{1,0:T(8,128)(2,1)S(1)}, bf16[256,1024]{1,0:T(8,128)(2,1)S(1)}, f32[512,256]{1,0:T(8,128)S(1)}, f32[512,256]{1,0:T(8,128)S(1)}) custom-call(f32[128,1024]{1,0:T(8,128)S(1)} %get-tuple-element.61.refs_0_, f32[128,1024]{1,0:T(8,128)S(1)} %get-tuple-element.62.refs_1_, f32[128,1024]{1,0:T(8,128)S(1)} %get-tuple-element.63.refs_2_, ...), custom_call_target="tpu_custom_call" | custom-call | tf_op jit(solution)/shard_map/right_side/pallas_call | solution.py:207
  30.2 0.0 collective-permute-done.11.refs_9_
  30.2 6.5 %solve_users.1 = f32[512,256]{1,0:T(8,128)} custom-call(f32[128,1024]{1,0:T(8,128)S(1)} %get-tuple-element.61.refs_0_, f32[128,1024]{1,0:T(8,128)S(1)} %get-tuple-element.62.refs_1_, f32[128,1024]{1,0:T(8,128)S(1)} %get-tuple-element.63.refs_2_, f32[128,1024]{1,0:T(8,128)S(1)} %get-tuple-element.64.refs_3_, bf16[1024,256]{1,0:T(8,128)(2,1)S(1)} %get-tuple-element.80.refs_4_, ...), custom_call_target="tpu_custom_call" | custom-call | tf_op jit(solution)/shard_map/solve_users/pallas_call | solution.py:283
  (9 shorter events, 0.1 us)
Async XLA Ops:
  0.0 0.7 %copy-start.3 = (s32[1,8,1]{1,2,0:T(1,128)S(1)}, s32[1,8,1]{1,2,0:T(1,128)}, u32[]{:S(2)}) copy-start(s32[1,8,1]{1,2,0:T(1,128)} %param.7) | copy-start | bytes 100
  0.0 0.7 %copy-start.2 = (s32[1,4,1]{1,2,0:T(1,128)S(1)}, s32[1,4,1]{1,2,0:T(1,128)}, u32[]{:S(2)}) copy-start(s32[1,4,1]{1,2,0:T(1,128)} %param.6) | copy-start | bytes 52
  0.0 0.9 %copy-start.1 = (bf16[256,256]{1,0:T(8,128)(2,1)S(1)}, bf16[256,256]{1,0:T(8,128)(2,1)}, u32[]{:S(2)}) copy-start(bf16[256,256]{1,0:T(8,128)(2,1)} %items.1) | copy-start | bytes 393220
  1.3 1.5 %collective-permute-start = (bf16[352,256]{1,0:T(8,128)(2,1)S(1)}, bf16[352,256]{1,0:T(8,128)(2,1)S(1)}, u32[]{:S(2)}, u32[]{:S(2)}) collective-permute-start(bf16[352,256]{1,0:T(8,128)(2,1)S(1)} %get-tuple-element.47), channel_id=1, source_target_pairs={{0,8},{1,9},{2,10},{3,11},{4,12},{5,13},{6,14},{7,15},{8,0},{9,1},... | collective-permute-start | bytes 540680 | tf_op jit(solution)/shard_map/ppermute | solution.py:296
  2.8 6.0 %collective-permute-start.1 = (bf16[256,256]{1,0:T(8,128)(2,1)S(1)}, bf16[256,256]{1,0:T(8,128)(2,1)S(1)}, u32[]{:S(2)}, u32[]{:S(2)}) collective-permute-start(bf16[256,256]{1,0:T(8,128)(2,1)S(1)} %get-tuple-element.50), channel_id=1, source_target_pairs={{0,16},{1,17},{2,18},{3,19},{4,20},{5,21},{6,22},{7,23},{8,24},{9,... | collective-permute-start | bytes 393224 | tf_op jit(solution)/shard_map/ppermute | solution.py:296
  5.2 6.1 %collective-permute-start.3 = (bf16[96,256]{1,0:T(8,128)(2,1)S(1)}, bf16[96,256]{1,0:T(8,128)(2,1)S(1)}, u32[]{:S(2)}, u32[]{:S(2)}) collective-permute-start(bf16[96,256]{1,0:T(8,128)(2,1)S(1)} %get-tuple-element.53), channel_id=1, source_target_pairs={{0,4},{1,5},{2,6},{3,7},{4,0},{5,1},{6,2},{7,3},{8,12},{9,13},{10,... | collective-permute-start | bytes 147464 | tf_op jit(solution)/shard_map/ppermute | solution.py:296
  9.0 7.9 %collective-permute-start.5 = (bf16[128,256]{1,0:T(8,128)(2,1)S(1)}, bf16[128,256]{1,0:T(8,128)(2,1)S(1)}, u32[]{:S(2)}, u32[]{:S(2)}) collective-permute-start(bf16[128,256]{1,0:T(8,128)(2,1)S(1)} %get-tuple-element.59), channel_id=1, source_target_pairs={{0,4},{1,5},{2,6},{3,7},{4,0},{5,1},{6,2},{7,3},{8,12},{9,13},{10,... | collective-permute-start | bytes 196616 | tf_op jit(solution)/shard_map/ppermute | solution.py:296
  11.3 5.6 %collective-permute-start.4 = (bf16[96,256]{1,0:T(8,128)(2,1)S(1)}, bf16[96,256]{1,0:T(8,128)(2,1)S(1)}, u32[]{:S(2)}, u32[]{:S(2)}) collective-permute-start(bf16[96,256]{1,0:T(8,128)(2,1)S(1)} %get-tuple-element.55), channel_id=1, source_target_pairs={{0,16},{1,17},{2,18},{3,19},{4,20},{5,21},{6,22},{7,23},{8,24},{9,... | collective-permute-start | bytes 147464 | tf_op jit(solution)/shard_map/ppermute | solution.py:296
  12.6 6.0 %collective-permute-start.2 = (bf16[128,256]{1,0:T(8,128)(2,1)S(1)}, bf16[128,256]{1,0:T(8,128)(2,1)S(1)}, u32[]{:S(2)}, u32[]{:S(2)}) collective-permute-start(bf16[128,256]{1,0:T(8,128)(2,1)S(1)} %get-tuple-element.51), channel_id=1, source_target_pairs={{0,7},{1,6},{2,5},{3,4},{4,3},{5,2},{6,1},{7,0},{8,15},{9,14},{10,... | collective-permute-start | bytes 196616 | tf_op jit(solution)/shard_map/ppermute | solution.py:296
  14.6 8.0 %collective-permute-start.9 = (bf16[128,256]{1,0:T(8,128)(2,1)S(1)}, bf16[128,256]{1,0:T(8,128)(2,1)S(1)}, u32[]{:S(2)}, u32[]{:S(2)}) collective-permute-start(bf16[128,256]{1,0:T(8,128)(2,1)S(1)} %get-tuple-element.77), channel_id=1, source_target_pairs={{0,5},{1,4},{2,7},{3,6},{4,1},{5,0},{6,3},{7,2},{8,13},{9,12},{10,... | collective-permute-start | bytes 196616 | tf_op jit(solution)/shard_map/ppermute | solution.py:296
  16.0 3.7 %copy-start = (bf16[64,128,128]{2,1,0:T(8,128)(2,1)S(1)}, bf16[64,128,128]{2,1,0:T(8,128)(2,1)}, u32[]{:S(2)}) copy-start(bf16[64,128,128]{2,1,0:T(8,128)(2,1)} %tiles.1) | copy-start | bytes 6291460
  16.0 3.7 %copy-start.4 = (s32[1,64]{1,0:T(1,128)S(1)}, s32[1,64]{1,0:T(1,128)}, u32[]{:S(2)}) copy-start(s32[1,64]{1,0:T(1,128)} %slots.1) | copy-start | bytes 772
  16.0 6.6 %collective-permute-start.10 = (bf16[128,256]{1,0:T(8,128)(2,1)S(1)}, bf16[128,256]{1,0:T(8,128)(2,1)S(1)}, u32[]{:S(2)}, u32[]{:S(2)}) collective-permute-start(bf16[128,256]{1,0:T(8,128)(2,1)S(1)} %get-tuple-element.78), channel_id=1, source_target_pairs={{0,6},{1,7},{2,4},{3,5},{4,2},{5,3},{6,0},{7,1},{8,14},{9,15},{10,... | collective-permute-start | bytes 196616 | tf_op jit(solution)/shard_map/ppermute | solution.py:296
  17.0 5.6 %collective-permute-start.6 = (bf16[224,256]{1,0:T(8,128)(2,1)S(1)}, bf16[224,256]{1,0:T(8,128)(2,1)S(1)}, u32[]{:S(2)}, u32[]{:S(2)}) collective-permute-start(bf16[224,256]{1,0:T(8,128)(2,1)S(1)} %get-tuple-element.74), channel_id=1, source_target_pairs={{0,1},{1,0},{2,3},{3,2},{4,5},{5,4},{6,7},{7,6},{8,9},{9,8},{10,11... | collective-permute-start | bytes 344072 | tf_op jit(solution)/shard_map/ppermute | solution.py:296
  17.4 5.7 %collective-permute-start.7 = (bf16[224,256]{1,0:T(8,128)(2,1)S(1)}, bf16[224,256]{1,0:T(8,128)(2,1)S(1)}, u32[]{:S(2)}, u32[]{:S(2)}) collective-permute-start(bf16[224,256]{1,0:T(8,128)(2,1)S(1)} %get-tuple-element.75), channel_id=1, source_target_pairs={{0,2},{1,3},{2,0},{3,1},{4,6},{5,7},{6,4},{7,5},{8,10},{9,11},{10,... | collective-permute-start | bytes 344072 | tf_op jit(solution)/shard_map/ppermute | solution.py:296
  18.6 7.9 %collective-permute-start.8 = (bf16[224,256]{1,0:T(8,128)(2,1)S(1)}, bf16[224,256]{1,0:T(8,128)(2,1)S(1)}, u32[]{:S(2)}, u32[]{:S(2)}) collective-permute-start(bf16[224,256]{1,0:T(8,128)(2,1)S(1)} %get-tuple-element.76), channel_id=1, source_target_pairs={{0,3},{1,2},{2,1},{3,0},{4,7},{5,6},{6,5},{7,4},{8,11},{9,10},{10,... | collective-permute-start | bytes 344072 | tf_op jit(solution)/shard_map/ppermute | solution.py:296
  26.5 3.7 %collective-permute-start.11 = (bf16[96,256]{1,0:T(8,128)(2,1)S(1)}, bf16[96,256]{1,0:T(8,128)(2,1)S(1)}, u32[]{:S(2)}, u32[]{:S(2)}) collective-permute-start(bf16[96,256]{1,0:T(8,128)(2,1)S(1)} %get-tuple-element.84), channel_id=1, source_target_pairs={{0,8},{1,9},{2,10},{3,11},{4,12},{5,13},{6,14},{7,15},{8,0},{9,1},... | collective-permute-start | bytes 147464 | tf_op jit(solution)/shard_map/ppermute | solution.py:296

commit v6 on v5

--- a/solution.py
+++ b/solution.py
@@ -192,13 +192,11 @@
         items[rows, :] = panel
         items_t[:, rows] = panel.T
     targets = [dot(high[block][...], items[...]) + dot(low[block][...], items[...]) for block in range(USER_BLOCKS)]
-    for first in range(0, USER_BLOCKS, 2):
-        pair = (first, first + 1)
-        scores = [dot(targets[block].astype(BF16), items_t[...]) for block in pair]
-        for block, score in zip(pair, scores):
-            users = slice(block * BLOCK, (block + 1) * BLOCK)
-            right_side[users, :] = targets[block]
-            image[users, :] = dot((weights[block][...] * score).astype(BF16), items[...])
+    scores = [dot(target.astype(BF16), items_t[...]) for target in targets]
+    for block, (target, score) in enumerate(zip(targets, scores)):
+        users = slice(block * BLOCK, (block + 1) * BLOCK)
+        right_side[users, :] = target
+        image[users, :] = dot((weights[block][...] * score).astype(BF16), items[...])
 
 
 def start_solve(built, panels, after):

time: 36.9 us -> 36.8 us (level)
  transfers between devices with their start and end apart: 12 -> 12, of which waited for: 5 -> 4; matrix products, arithmetic and copies ran while one was open for 0% -> 0% of each run, Pallas kernels for 12% -> 12%
where the time goes in v6:
time: 36.8 us; the launch traced here: 36.6 us
  starting transfers between devices  17.8 us (48%)
  Pallas kernels  11.3 us (31%)
  waiting for transfers between devices  6.49 us (18%)
  local copies, waits for them, and re-layouts  0.93 us (3%)
    ppermute x12, starting transfers between devices, swap(): return lax.ppermute(array, ('grp', 'dev'), order)  17.8 us
    pallas_call x1, Pallas kernels, solve_users(): call(functools.partial(solve_kernel, len(gram_parts), unroll), 'solve_use...  6.53 us
    ppermute x12, waiting for transfers between devices, swap(): return lax.ppermute(array, ('grp', 'dev'), order)  6.49 us
    pallas_call x1, Pallas kernels, build_weights(): call(functools.partial(build_kernel, mixed), 'build_weights', [SM, VM, AN...  2.85 us
    pallas_call x1, Pallas kernels, start_solve(): call(functools.partial(right_kernel, len(panels)), 'right_side', [VM] * (...  1.3 us
    unnamed x10, local copies, waits for them, and re-layouts  0.93 us
  transfers between devices with their start and end apart: 12, of which 4 were waited for; matrix products, arithmetic and copies ran while one was open for 0% of the time, Pallas kernels for 12%

profile of v6, /device:TPU:1, one launch (start us, length us, event | category | flops | bytes accessed | tf_op | source)
XLA Modules:
  0.0 36.6 jit_solution(10829472220255370627)
XLA Ops:
  0.0 0.0 copy-start.3
  0.0 0.0 copy-start.2
  0.0 0.0 copy-start.1
  0.0 0.6 %copy-done.3 = s32[1,8,1]{1,2,0:T(1,128)S(1)} copy-done((s32[1,8,1]{1,2,0:T(1,128)S(1)}, s32[1,8,1]{1,2,0:T(1,128)}, u32[]{:S(2)}) %copy-start.3) | copy-done | bytes 56
  0.7 0.0 copy-done.2
  0.7 0.3 copy-done.1
  0.9 0.3 first.1
  1.3 0.1 collective-permute-start
  1.4 1.4 %collective-permute-done.from_core = bf16[352,256]{1,0:T(8,128)(2,1)S(1)} collective-permute-done((bf16[352,256]{1,0:T(8,128)(2,1)S(1)}, bf16[352,256]{1,0:T(8,128)(2,1)S(1)}, u32[]{:S(2)}, u32[]{:S(2)}) %collective-permute-start) | collective-permute-done | bytes 180256 | tf_op jit(solution)/shard_map/ppermute | solution.py:294
  2.8 2.4 %collective-permute-start.1 = (bf16[256,256]{1,0:T(8,128)(2,1)S(1)}, bf16[256,256]{1,0:T(8,128)(2,1)S(1)}, u32[]{:S(2)}, u32[]{:S(2)}) collective-permute-start(bf16[256,256]{1,0:T(8,128)(2,1)S(1)} %get-tuple-element.50), channel_id=1, source_target_pairs={{0,16},{1,17},{2,18},{3,19},{4,20},{5,21},{6,22},{7,23},{8,24},{9,... | collective-permute-start | bytes 393224 | tf_op jit(solution)/shard_map/ppermute | solution.py:294
  5.2 2.3 %collective-permute-start.3 = (bf16[96,256]{1,0:T(8,128)(2,1)S(1)}, bf16[96,256]{1,0:T(8,128)(2,1)S(1)}, u32[]{:S(2)}, u32[]{:S(2)}) collective-permute-start(bf16[96,256]{1,0:T(8,128)(2,1)S(1)} %get-tuple-element.53), channel_id=1, source_target_pairs={{0,4},{1,5},{2,6},{3,7},{4,0},{5,1},{6,2},{7,3},{8,12},{9,13},{10,... | collective-permute-start | bytes 147464 | tf_op jit(solution)/shard_map/ppermute | solution.py:294
  7.5 1.3 %collective-permute-done.1.from_y = bf16[256,256]{1,0:T(8,128)(2,1)S(1)} collective-permute-done((bf16[256,256]{1,0:T(8,128)(2,1)S(1)}, bf16[256,256]{1,0:T(8,128)(2,1)S(1)}, u32[]{:S(2)}, u32[]{:S(2)}) %collective-permute-start.1) | collective-permute-done | bytes 131104 | tf_op jit(solution)/shard_map/ppermute | solution.py:294
  8.8 0.2 pack_dev.1
  9.0 2.3 %collective-permute-start.5 = (bf16[128,256]{1,0:T(8,128)(2,1)S(1)}, bf16[128,256]{1,0:T(8,128)(2,1)S(1)}, u32[]{:S(2)}, u32[]{:S(2)}) collective-permute-start(bf16[128,256]{1,0:T(8,128)(2,1)S(1)} %get-tuple-element.59), channel_id=1, source_target_pairs={{0,4},{1,5},{2,6},{3,7},{4,0},{5,1},{6,2},{7,3},{8,12},{9,13},{10,... | collective-permute-start | bytes 196616 | tf_op jit(solution)/shard_map/ppermute | solution.py:294
  11.3 0.0 collective-permute-done.3.refs_0_.arrived
  11.3 1.3 %collective-permute-start.4 = (bf16[96,256]{1,0:T(8,128)(2,1)S(1)}, bf16[96,256]{1,0:T(8,128)(2,1)S(1)}, u32[]{:S(2)}, u32[]{:S(2)}) collective-permute-start(bf16[96,256]{1,0:T(8,128)(2,1)S(1)} %get-tuple-element.55), channel_id=1, source_target_pairs={{0,16},{1,17},{2,18},{3,19},{4,20},{5,21},{6,22},{7,23},{8,24},{9,... | collective-permute-start | bytes 147464 | tf_op jit(solution)/shard_map/ppermute | solution.py:294
  12.6 2.0 %collective-permute-start.2 = (bf16[128,256]{1,0:T(8,128)(2,1)S(1)}, bf16[128,256]{1,0:T(8,128)(2,1)S(1)}, u32[]{:S(2)}, u32[]{:S(2)}) collective-permute-start(bf16[128,256]{1,0:T(8,128)(2,1)S(1)} %get-tuple-element.51), channel_id=1, source_target_pairs={{0,7},{1,6},{2,5},{3,4},{4,3},{5,2},{6,1},{7,0},{8,15},{9,14},{10,... | collective-permute-start | bytes 196616 | tf_op jit(solution)/shard_map/ppermute | solution.py:294
  14.6 1.4 %collective-permute-start.9 = (bf16[128,256]{1,0:T(8,128)(2,1)S(1)}, bf16[128,256]{1,0:T(8,128)(2,1)S(1)}, u32[]{:S(2)}, u32[]{:S(2)}) collective-permute-start(bf16[128,256]{1,0:T(8,128)(2,1)S(1)} %get-tuple-element.77), channel_id=1, source_target_pairs={{0,5},{1,4},{2,7},{3,6},{4,1},{5,0},{6,3},{7,2},{8,13},{9,12},{10,... | collective-permute-start | bytes 196616 | tf_op jit(solution)/shard_map/ppermute | solution.py:294
  16.0 0.0 copy-start
  16.0 0.0 copy-start.4
  16.0 0.9 %collective-permute-start.10 = (bf16[128,256]{1,0:T(8,128)(2,1)S(1)}, bf16[128,256]{1,0:T(8,128)(2,1)S(1)}, u32[]{:S(2)}, u32[]{:S(2)}) collective-permute-start(bf16[128,256]{1,0:T(8,128)(2,1)S(1)} %get-tuple-element.78), channel_id=1, source_target_pairs={{0,6},{1,7},{2,4},{3,5},{4,2},{5,3},{6,0},{7,1},{8,14},{9,15},{10,... | collective-permute-start | bytes 196616 | tf_op jit(solution)/shard_map/ppermute | solution.py:294
  16.9 0.0 collective-permute-done.5.refs_0_.refs_16_
  16.9 0.0 collective-permute-done.4.arrived
  17.0 0.4 collective-permute-start.6
  17.4 1.2 %collective-permute-start.7 = (bf16[224,256]{1,0:T(8,128)(2,1)S(1)}, bf16[224,256]{1,0:T(8,128)(2,1)S(1)}, u32[]{:S(2)}, u32[]{:S(2)}) collective-permute-start(bf16[224,256]{1,0:T(8,128)(2,1)S(1)} %get-tuple-element.75), channel_id=1, source_target_pairs={{0,2},{1,3},{2,0},{3,1},{4,6},{5,7},{6,4},{7,5},{8,10},{9,11},{10,... | collective-permute-start | bytes 344072 | tf_op jit(solution)/shard_map/ppermute | solution.py:294
  18.6 0.0 collective-permute-done.2.refs_0_.refs_19_
  18.6 1.1 %collective-permute-start.8 = (bf16[224,256]{1,0:T(8,128)(2,1)S(1)}, bf16[224,256]{1,0:T(8,128)(2,1)S(1)}, u32[]{:S(2)}, u32[]{:S(2)}) collective-permute-start(bf16[224,256]{1,0:T(8,128)(2,1)S(1)} %get-tuple-element.76), channel_id=1, source_target_pairs={{0,3},{1,2},{2,1},{3,0},{4,7},{5,6},{6,5},{7,4},{8,11},{9,10},{10,... | collective-permute-start | bytes 344072 | tf_op jit(solution)/shard_map/ppermute | solution.py:294
  19.7 0.0 copy-done
  19.7 0.0 copy-done.4
  19.7 2.9 %build_weights.1 = (f32[128,1024]{1,0:T(8,128)S(1)}, f32[128,1024]{1,0:T(8,128)S(1)}, f32[128,1024]{1,0:T(8,128)S(1)}, f32[128,1024]{1,0:T(8,128)S(1)}, bf16[128...) custom-call(s32[1,64]{1,0:T(1,128)S(1)} %copy-done.4, ...), custom_call_target="tpu_custom_call" | custom-call | tf_op jit(solution)/shard_map/build_weights/pallas_call | solution.py:177
  22.6 0.0 collective-permute-done.9.refs_0_.refs_17_
  22.6 0.0 collective-permute-done.10.refs_1_.refs_18_
  22.6 0.0 collective-permute-done.6.refs_2_.refs_13_
  22.6 0.4 %collective-permute-done.7.refs_1_.refs_14_ = bf16[224,256]{1,0:T(8,128)(2,1)S(1)} collective-permute-done((bf16[224,256]{1,0:T(8,128)(2,1)S(1)}, bf16[224,256]{1,0:T(8,128)(2,1)S(1)}, u32[]{:S(2)}, u32[]{:S(2)}) %collective-permute-start.7) | collective-permute-done | bytes 114720 | tf_op jit(solution)/shard_map/ppermute | solution.py:294
  23.0 3.4 %collective-permute-done.8.refs_0_.refs_15_ = bf16[224,256]{1,0:T(8,128)(2,1)S(1)} collective-permute-done((bf16[224,256]{1,0:T(8,128)(2,1)S(1)}, bf16[224,256]{1,0:T(8,128)(2,1)S(1)}, u32[]{:S(2)}, u32[]{:S(2)}) %collective-permute-start.8) | collective-permute-done | bytes 114720 | tf_op jit(solution)/shard_map/ppermute | solution.py:294
  26.5 2.3 %collective-permute-start.11 = (bf16[96,256]{1,0:T(8,128)(2,1)S(1)}, bf16[96,256]{1,0:T(8,128)(2,1)S(1)}, u32[]{:S(2)}, u32[]{:S(2)}) collective-permute-start(bf16[96,256]{1,0:T(8,128)(2,1)S(1)} %get-tuple-element.84), channel_id=1, source_target_pairs={{0,8},{1,9},{2,10},{3,11},{4,12},{5,13},{6,14},{7,15},{8,0},{9,1},... | collective-permute-start | bytes 147464 | tf_op jit(solution)/shard_map/ppermute | solution.py:294
  28.8 1.3 %right_side.1 = (bf16[1024,256]{1,0:T(8,128)(2,1)S(1)}, bf16[256,1024]{1,0:T(8,128)(2,1)S(1)}, f32[512,256]{1,0:T(8,128)S(1)}, f32[512,256]{1,0:T(8,128)S(1)}) custom-call(f32[128,1024]{1,0:T(8,128)S(1)} %get-tuple-element.61.refs_0_, f32[128,1024]{1,0:T(8,128)S(1)} %get-tuple-element.62.refs_1_, f32[128,1024]{1,0:T(8,128)S(1)} %get-tuple-element.63.refs_2_, ...), custom_call_target="tpu_custom_call" | custom-call | tf_op jit(solution)/shard_map/right_side/pallas_call | solution.py:205
  30.1 0.0 collective-permute-done.11.refs_9_
  30.1 6.5 %solve_users.1 = f32[512,256]{1,0:T(8,128)} custom-call(f32[128,1024]{1,0:T(8,128)S(1)} %get-tuple-element.61.refs_0_, f32[128,1024]{1,0:T(8,128)S(1)} %get-tuple-element.62.refs_1_, f32[128,1024]{1,0:T(8,128)S(1)} %get-tuple-element.63.refs_2_, f32[128,1024]{1,0:T(8,128)S(1)} %get-tuple-element.64.refs_3_, bf16[1024,256]{1,0:T(8,128)(2,1)S(1)} %get-tuple-element.80.refs_4_, ...), custom_call_target="tpu_custom_call" | custom-call | tf_op jit(solution)/shard_map/solve_users/pallas_call | solution.py:281
  (9 shorter events, 0.1 us)
Async XLA Ops:
  0.0 0.7 %copy-start.3 = (s32[1,8,1]{1,2,0:T(1,128)S(1)}, s32[1,8,1]{1,2,0:T(1,128)}, u32[]{:S(2)}) copy-start(s32[1,8,1]{1,2,0:T(1,128)} %param.7) | copy-start | bytes 100
  0.0 0.7 %copy-start.2 = (s32[1,4,1]{1,2,0:T(1,128)S(1)}, s32[1,4,1]{1,2,0:T(1,128)}, u32[]{:S(2)}) copy-start(s32[1,4,1]{1,2,0:T(1,128)} %param.6) | copy-start | bytes 52
  0.0 0.9 %copy-start.1 = (bf16[256,256]{1,0:T(8,128)(2,1)S(1)}, bf16[256,256]{1,0:T(8,128)(2,1)}, u32[]{:S(2)}) copy-start(bf16[256,256]{1,0:T(8,128)(2,1)} %items.1) | copy-start | bytes 393220
  1.3 1.5 %collective-permute-start = (bf16[352,256]{1,0:T(8,128)(2,1)S(1)}, bf16[352,256]{1,0:T(8,128)(2,1)S(1)}, u32[]{:S(2)}, u32[]{:S(2)}) collective-permute-start(bf16[352,256]{1,0:T(8,128)(2,1)S(1)} %get-tuple-element.47), channel_id=1, source_target_pairs={{0,8},{1,9},{2,10},{3,11},{4,12},{5,13},{6,14},{7,15},{8,0},{9,1},... | collective-permute-start | bytes 540680 | tf_op jit(solution)/shard_map/ppermute | solution.py:294
  2.8 6.0 %collective-permute-start.1 = (bf16[256,256]{1,0:T(8,128)(2,1)S(1)}, bf16[256,256]{1,0:T(8,128)(2,1)S(1)}, u32[]{:S(2)}, u32[]{:S(2)}) collective-permute-start(bf16[256,256]{1,0:T(8,128)(2,1)S(1)} %get-tuple-element.50), channel_id=1, source_target_pairs={{0,16},{1,17},{2,18},{3,19},{4,20},{5,21},{6,22},{7,23},{8,24},{9,... | collective-permute-start | bytes 393224 | tf_op jit(solution)/shard_map/ppermute | solution.py:294
  5.2 6.1 %collective-permute-start.3 = (bf16[96,256]{1,0:T(8,128)(2,1)S(1)}, bf16[96,256]{1,0:T(8,128)(2,1)S(1)}, u32[]{:S(2)}, u32[]{:S(2)}) collective-permute-start(bf16[96,256]{1,0:T(8,128)(2,1)S(1)} %get-tuple-element.53), channel_id=1, source_target_pairs={{0,4},{1,5},{2,6},{3,7},{4,0},{5,1},{6,2},{7,3},{8,12},{9,13},{10,... | collective-permute-start | bytes 147464 | tf_op jit(solution)/shard_map/ppermute | solution.py:294
  9.0 7.9 %collective-permute-start.5 = (bf16[128,256]{1,0:T(8,128)(2,1)S(1)}, bf16[128,256]{1,0:T(8,128)(2,1)S(1)}, u32[]{:S(2)}, u32[]{:S(2)}) collective-permute-start(bf16[128,256]{1,0:T(8,128)(2,1)S(1)} %get-tuple-element.59), channel_id=1, source_target_pairs={{0,4},{1,5},{2,6},{3,7},{4,0},{5,1},{6,2},{7,3},{8,12},{9,13},{10,... | collective-permute-start | bytes 196616 | tf_op jit(solution)/shard_map/ppermute | solution.py:294
  11.3 5.6 %collective-permute-start.4 = (bf16[96,256]{1,0:T(8,128)(2,1)S(1)}, bf16[96,256]{1,0:T(8,128)(2,1)S(1)}, u32[]{:S(2)}, u32[]{:S(2)}) collective-permute-start(bf16[96,256]{1,0:T(8,128)(2,1)S(1)} %get-tuple-element.55), channel_id=1, source_target_pairs={{0,16},{1,17},{2,18},{3,19},{4,20},{5,21},{6,22},{7,23},{8,24},{9,... | collective-permute-start | bytes 147464 | tf_op jit(solution)/shard_map/ppermute | solution.py:294
  12.6 6.0 %collective-permute-start.2 = (bf16[128,256]{1,0:T(8,128)(2,1)S(1)}, bf16[128,256]{1,0:T(8,128)(2,1)S(1)}, u32[]{:S(2)}, u32[]{:S(2)}) collective-permute-start(bf16[128,256]{1,0:T(8,128)(2,1)S(1)} %get-tuple-element.51), channel_id=1, source_target_pairs={{0,7},{1,6},{2,5},{3,4},{4,3},{5,2},{6,1},{7,0},{8,15},{9,14},{10,... | collective-permute-start | bytes 196616 | tf_op jit(solution)/shard_map/ppermute | solution.py:294
  14.6 8.0 %collective-permute-start.9 = (bf16[128,256]{1,0:T(8,128)(2,1)S(1)}, bf16[128,256]{1,0:T(8,128)(2,1)S(1)}, u32[]{:S(2)}, u32[]{:S(2)}) collective-permute-start(bf16[128,256]{1,0:T(8,128)(2,1)S(1)} %get-tuple-element.77), channel_id=1, source_target_pairs={{0,5},{1,4},{2,7},{3,6},{4,1},{5,0},{6,3},{7,2},{8,13},{9,12},{10,... | collective-permute-start | bytes 196616 | tf_op jit(solution)/shard_map/ppermute | solution.py:294
  16.0 3.7 %copy-start = (bf16[64,128,128]{2,1,0:T(8,128)(2,1)S(1)}, bf16[64,128,128]{2,1,0:T(8,128)(2,1)}, u32[]{:S(2)}) copy-start(bf16[64,128,128]{2,1,0:T(8,128)(2,1)} %tiles.1) | copy-start | bytes 6291460
  16.0 3.7 %copy-start.4 = (s32[1,64]{1,0:T(1,128)S(1)}, s32[1,64]{1,0:T(1,128)}, u32[]{:S(2)}) copy-start(s32[1,64]{1,0:T(1,128)} %slots.1) | copy-start | bytes 772
  16.0 6.6 %collective-permute-start.10 = (bf16[128,256]{1,0:T(8,128)(2,1)S(1)}, bf16[128,256]{1,0:T(8,128)(2,1)S(1)}, u32[]{:S(2)}, u32[]{:S(2)}) collective-permute-start(bf16[128,256]{1,0:T(8,128)(2,1)S(1)} %get-tuple-element.78), channel_id=1, source_target_pairs={{0,6},{1,7},{2,4},{3,5},{4,2},{5,3},{6,0},{7,1},{8,14},{9,15},{10,... | collective-permute-start | bytes 196616 | tf_op jit(solution)/shard_map/ppermute | solution.py:294
  17.0 5.6 %collective-permute-start.6 = (bf16[224,256]{1,0:T(8,128)(2,1)S(1)}, bf16[224,256]{1,0:T(8,128)(2,1)S(1)}, u32[]{:S(2)}, u32[]{:S(2)}) collective-permute-start(bf16[224,256]{1,0:T(8,128)(2,1)S(1)} %get-tuple-element.74), channel_id=1, source_target_pairs={{0,1},{1,0},{2,3},{3,2},{4,5},{5,4},{6,7},{7,6},{8,9},{9,8},{10,11... | collective-permute-start | bytes 344072 | tf_op jit(solution)/shard_map/ppermute | solution.py:294
  17.4 5.7 %collective-permute-start.7 = (bf16[224,256]{1,0:T(8,128)(2,1)S(1)}, bf16[224,256]{1,0:T(8,128)(2,1)S(1)}, u32[]{:S(2)}, u32[]{:S(2)}) collective-permute-start(bf16[224,256]{1,0:T(8,128)(2,1)S(1)} %get-tuple-element.75), channel_id=1, source_target_pairs={{0,2},{1,3},{2,0},{3,1},{4,6},{5,7},{6,4},{7,5},{8,10},{9,11},{10,... | collective-permute-start | bytes 344072 | tf_op jit(solution)/shard_map/ppermute | solution.py:294
  18.6 7.9 %collective-permute-start.8 = (bf16[224,256]{1,0:T(8,128)(2,1)S(1)}, bf16[224,256]{1,0:T(8,128)(2,1)S(1)}, u32[]{:S(2)}, u32[]{:S(2)}) collective-permute-start(bf16[224,256]{1,0:T(8,128)(2,1)S(1)} %get-tuple-element.76), channel_id=1, source_target_pairs={{0,3},{1,2},{2,1},{3,0},{4,7},{5,6},{6,5},{7,4},{8,11},{9,10},{10,... | collective-permute-start | bytes 344072 | tf_op jit(solution)/shard_map/ppermute | solution.py:294
  26.5 3.6 %collective-permute-start.11 = (bf16[96,256]{1,0:T(8,128)(2,1)S(1)}, bf16[96,256]{1,0:T(8,128)(2,1)S(1)}, u32[]{:S(2)}, u32[]{:S(2)}) collective-permute-start(bf16[96,256]{1,0:T(8,128)(2,1)S(1)} %get-tuple-element.84), channel_id=1, source_target_pairs={{0,8},{1,9},{2,10},{3,11},{4,12},{5,13},{6,14},{7,15},{8,0},{9,1},... | collective-permute-start | bytes 147464 | tf_op jit(solution)/shard_map/ppermute | solution.py:294
